TPU v7x, 128 devices: a whole 4x4x4 slice. The times are simulated.
128 devices in a mesh: img: 16 (over z_hi, x, core), ori: 8 (over z_lo, y).
Axes of the slice: x: 4, y: 4, z: 4 (z_hi: 2, z_lo: 2; z = z_hi * 2 + z_lo), core: 2. Of those that a mesh axis runs over, the one named last changes fastest.
Arguments:
- images: bfloat16 [4096, 32768], P('img')
- classes: int32 [4096], P('img'), may hold values from 0 to 31
- contrast: float32 [32, 16384], replicated, may hold values from 0.1 to 1
- noise_weight: float32 [16384], replicated, may hold values from 0.5 to 2
- projections: bfloat16 [8, 192, 32768], P('ori', 'img')
- proj_index: int32 [4096], P('ori'), may hold values from 0 to 191, as said below
Outputs:
- log_weights: float32 [4096, 4096], P('img', 'ori')
- back_sums: bfloat16 [8, 192, 32768], P('ori', 'img')
- contrast_mass: float32 [8, 192, 16384], P('ori', 'img')
Inputs may be any that keep to these rules, and one draw needn't show every extreme that they name: proj_index[j] names a projection of orientation block j // 512; every one of a block's 192 projections is named by at least one orientation of that block.
All inputs are finite; a program needn't handle non-finite values.
Results may differ from a plain program's by a relative error of at most 0.017.
Values may be sent and summed in bfloat16 or wider, within the bound.
No kernel may reach another device: no remote copies, remote signals or barrier semaphores. Data moves between devices by JAX's collectives and lax.ppermute only.
A program may use at most 320 MiB of HBM per device.

v0:
```python
import jax
import jax.numpy as jnp
from jax import lax
from jax.sharding import PartitionSpec as P

PRECISE = lax.Precision.HIGHEST


def shards(images, classes, contrast, noise_weight, projections, proj_index):
    img_rows = images.shape[0]
    half_len = contrast.shape[1]
    class_count = contrast.shape[0]
    shard_len = projections.shape[1]
    block_width = shard_len * lax.axis_size("img")
    class_hot = (classes[:, None] == jnp.arange(class_count, dtype=jnp.int32)[None, :]).astype(
        jnp.float32
    )
    amplitude = jnp.dot(class_hot, contrast * noise_weight[None, :], precision=PRECISE)
    weighted = (
        (images.astype(jnp.float32).reshape(img_rows, 2, half_len) * amplitude[:, None, :])
        .reshape(img_rows, 2 * half_len)
        .astype(jnp.bfloat16)
    )
    half_quad = 0.5 * contrast * contrast * noise_weight[None, :]
    squared = contrast * contrast
    slab_rows = lax.all_gather(projections, "img", axis=1, tiled=True).reshape(-1, 2 * half_len)
    correl = lax.dot_general(
        weighted, slab_rows, (((1,), (1,)), ((), ())), preferred_element_type=jnp.float32
    )
    power = jnp.sum(jnp.square(slab_rows.astype(jnp.float32).reshape(-1, 2, half_len)), axis=1)
    quad_part = lax.dot_general(half_quad, power, (((1,), (1,)), ((), ())), precision=PRECISE)
    choose = (jnp.arange(block_width, dtype=jnp.int32)[:, None] == proj_index[None, :]).astype(
        jnp.float32
    )
    scores = jnp.dot(
        correl - jnp.dot(class_hot, quad_part, precision=PRECISE), choose, precision=PRECISE
    )
    local_peak = jnp.max(scores, axis=1)
    highest = lax.pmax(local_peak, "ori")
    summed = lax.psum(jnp.sum(jnp.exp(scores - highest[:, None]), axis=1), "ori")
    log_weights = scores - (highest + jnp.log(summed))[:, None]
    chances = jnp.exp(log_weights).astype(jnp.bfloat16)
    per_proj = lax.dot_general(
        chances,
        choose.astype(jnp.bfloat16),
        (((1,), (1,)), ((), ())),
        preferred_element_type=jnp.float32,
    ).astype(jnp.bfloat16)
    back_sums = lax.psum_scatter(
        lax.dot_general(
            per_proj, weighted, (((0,), (0,)), ((), ())), preferred_element_type=jnp.float32
        ).astype(jnp.bfloat16),
        "img",
        scatter_dimension=0,
        tiled=True,
    )
    class_totals = lax.dot_general(
        per_proj.astype(jnp.float32), class_hot, (((0,), (0,)), ((), ())), precision=PRECISE
    )
    own_totals = lax.psum_scatter(class_totals, "img", scatter_dimension=0, tiled=True)
    contrast_mass = jnp.dot(own_totals, squared, precision=PRECISE)
    return (
        log_weights,
        back_sums.reshape(1, shard_len, 2 * half_len),
        contrast_mass.reshape(1, shard_len, half_len),
    )


def solution(mesh):
    in_specs = (P("img", None), P("img"), P(), P(), P("ori", "img", None), P("ori"))
    out_specs = (P("img", "ori"), P("ori", "img", None), P("ori", "img", None))
    return jax.shard_map(shards, mesh=mesh, in_specs=in_specs, out_specs=out_specs, check_vma=False)
```

profile of v0, /device:TPU:72, one launch (start us, length us, event | category | flops | bytes accessed | tf_op | source)
XLA Modules:
  0.0 730.8 jit_solution(8142748993954926975)
XLA Ops:
  7.2 0.0 all-gather.2.cloned.1.call-start
  7.2 3.7 copy.12
  10.9 0.0 all-gather.2.cloned.1.call-update
  11.0 12.1 %fusion.9 = f32[256,16384]{1,0:T(8,128)} fusion(f32[32,16384]{1,0:T(8,128)} %param.8, f32[16384]{0:T(1024)} %param.9, s32[256]{0:T(256)} %param.7), kind=kOutput, calls=%fused_computation.11 | convolution fusion | flops 1611145216 | bytes 18940928 | tf_op jit(solution)/shard_map/dot_general | solution.py:18
  23.1 17.7 %mul.39 = f32[256,2,16384]{2,1,0:T(2,128)} broadcast(f32[256,16384]{1,0:T(8,128)} %fusion.9), dimensions={0,2} | broadcast | bytes 50331648 | tf_op jit(solution)/shard_map/mul | solution.py:20
  40.8 32.5 %copy.15 = f32[32,8,2,16384]{3,1,2,0:T(8,128)} copy(f32[32,8,2,16384]{3,2,1,0:T(2,128)} %bitcast.21) | data formatting | bytes 67108864
  73.3 85.6 %all-gather.2.cloned.1.call-done = bf16[1,192,32768]{2,0,1:T(2,128)(2,1)} async-done(((bf16[1,12,32768]{2,0,1:T(2,128)(2,1)}), bf16[1,192,32768]{2,0,1:T(2,128)(2,1)}) %all-gather.2.cloned.1.call-update) | async-done | bytes 12582928 | tf_op jit(solution)/shard_map/all_gather | solution.py:26
  158.9 81.1 %multiply_reduce_fusion = f32[192,32768]{1,0:T(8,128)} fusion(bf16[1,192,32768]{2,0,1:T(2,128)(2,1)} %all-gather.2.cloned.1.call-done), kind=kLoop, calls=%fused_computation.2 | loop fusion | flops 12582912 | bytes 37748736 | tf_op jit(solution)/shard_map/square | solution.py:30
  240.0 32.3 %square.11 = f32[192,2,16384]{2,1,0:T(2,128)} reshape(f32[192,32768]{1,0:T(8,128)} %multiply_reduce_fusion) | data formatting | bytes 50331648 | tf_op jit(solution)/shard_map/square | solution.py:30
  272.3 0.0 copy-start
  272.3 0.0 copy-start.2
  272.3 36.1 %reduce_sum.18 = f32[192,16384]{1,0:T(8,128)} reduce(f32[192,2,16384]{2,1,0:T(2,128)} %square.11, f32[]{:T(128)} %constant.1.clone.1), dimensions={1}, to_apply=%region_0.0 | reduce | flops 3145728 | bytes 37748740 | tf_op jit(solution)/shard_map/reduce_sum | solution.py:30
  308.4 0.0 copy-done
  308.4 0.0 copy-done.2
  308.4 14.4 %fusion.6 = f32[32,192]{1,0:T(8,128)S(1)} fusion(f32[192,16384]{1,0:T(8,128)} %reduce_sum.18, f32[32,16384]{1,0:T(8,128)S(1)} %copy-done, f32[16384]{0:T(1024)S(1)} %copy-done.2), kind=kOutput, calls=%fused_computation.9 | convolution fusion | flops 1209532416 | bytes 14770176 | tf_op jit(solution)/shard_map/dot_general | solution.py:31
  322.8 0.0 copy-start.3
  322.8 0.0 copy-start.4
  322.8 29.3 %fusion.2 = f32[256,192]{0,1:T(8,128)S(1)} fusion(bf16[1,192,32768]{2,0,1:T(2,128)(2,1)} %all-gather.2.cloned.1.call-done, f32[256,32768]{1,0:T(8,128)} %bitcast.19, bf16[256,32768]{1,0:T(8,128)(2,1)} %param.6), kind=kOutput, calls=%fused_computation.4 | convolution fusion | flops 3246391296 | bytes 63111168 | tf_op jit(solution)/shard_map/dot_general | solution.py:27
  352.2 0.0 copy-done.3
  352.2 0.3 convolution_subtract_fusion
  352.5 0.0 copy-done.4
  352.5 0.5 fusion.24
  353.0 17.5 %pmax.7 = f32[256]{0:T(256)S(1)} all-reduce(f32[256]{0:T(256)S(1)} %get-tuple-element.12), channel_id=1, replica_groups=mesh['img'=16,'ori'=8] {'ori'}, use_global_device_ids=true, to_apply=%region_2.0 | all-reduce | flops 256 | bytes 2048 | tf_op jit(solution)/shard_map/pmax | solution.py:39
  370.6 0.2 exponential_reduce_fusion
  370.8 19.2 %psum.7 = f32[256]{0:T(256)S(1)} all-reduce(f32[256]{0:T(256)S(1)} %exponential_reduce_fusion), channel_id=1, replica_groups=mesh['img'=16,'ori'=8] {'ori'}, use_global_device_ids=true, to_apply=%region_4.0 | all-reduce | flops 256 | bytes 2048 | tf_op jit(solution)/shard_map/psum | solution.py:40
  390.0 0.1 broadcast_subtract_fusion
  390.1 0.0 copy-start.1
  390.2 0.3 convolution_convert_fusion.1
  390.4 0.5 copy-done.1
  390.9 0.0 copy-start.5
  390.9 21.9 %convolution_convert_fusion = bf16[192,32768]{1,0:T(8,128)(2,1)} fusion(bf16[256,192]{0,1:T(8,128)(2,1)S(1)} %convolution_convert_fusion.1, f32[256,32768]{1,0:T(8,128)} %bitcast.20, bf16[256,32768]{1,0:T(8,128)(2,1)} %param.6), kind=kOutput, calls=%fused_computation | convolution fusion | flops 3252682752 | bytes 63012864 | tf_op jit(solution)/shard_map/dot_general | solution.py:50
  412.9 99.3 %fusion = bf16[16,32768]{1,0:T(8,128)(2,1)S(1)} fusion(bf16[192,32768]{1,0:T(8,128)(2,1)} %convolution_convert_fusion), kind=kCustom, calls=%all-reduce-scatter | all-reduce-scatter fusion | flops 8388609 | bytes 13632000
  512.2 1.9 collective-permute-start
  514.1 1.9 collective-permute-start.1
  516.1 1.9 collective-permute-start.2
  518.0 1.2 slice
  519.2 2.0 collective-permute-start.3
  521.2 0.2 fusion.17
  521.4 101.0 %fusion.1 = f32[16,32]{1,0:T(8,128)S(1)} fusion(f32[192,32]{1,0:T(8,128)S(1)} %fusion.17), kind=kCustom, calls=%all-reduce-scatter.1 | all-reduce-scatter fusion | flops 8193 | bytes 27136
  622.4 1.9 collective-permute-start.7
  624.4 7.5 %collective-permute-done.7 = f32[12,32]{1,0:T(8,128)S(1)} collective-permute-done((f32[12,32]{1,0:T(8,128)S(1)}, f32[12,32]{1,0:T(8,128)S(1)}, u32[]{:S(2)}, u32[]{:S(2)}) %collective-permute-start.7) | collective-permute-done | bytes 1568
  631.9 1.9 collective-permute-start.4
  633.8 6.7 collective-permute-done.4
  640.5 1.9 collective-permute-start.5
  642.4 7.2 collective-permute-done.5
  649.6 1.9 collective-permute-start.6
  651.5 0.0 copy-done.5
  651.5 0.6 dynamic-slice.6
  652.8 5.7 collective-permute-done.6
  658.5 0.4 concatenate.1
  658.9 1.2 convolution_bitcast_fusion
  660.1 1.7 copy.13
  661.8 0.0 collective-permute-done.3
  661.8 0.0 collective-permute-done
  661.8 0.0 collective-permute-done.1
  661.8 0.0 collective-permute-done.2
  661.8 59.5 %concatenate = bf16[76,32768]{1,0:T(8,128)(2,1)} concatenate(bf16[12,32768]{1,0:T(8,128)(2,1)} %collective-permute-done.3, bf16[16,32768]{1,0:T(8,128)(2,1)} %collective-permute-done.2, bf16[16,32768]{1,0:T(8,128)(2,1)} %collective-permute-done.1, bf16[16,32768]{1,0:T(8,128)(2,1)} %collective-permute-done, bf16[16,32768]{1,0:T(8,128)(2,1)S(1)} %fusion), dimensions={0} | concatenate | bytes 9961472
  721.3 2.6 dynamic-slice_bitcast_fusion
  (2 shorter events, 0.0 us)
Async XLA Ops:
  7.2 151.7 %all-gather.2.cloned.1.call-start = ((), (), s32[]{:S(2)}) async-start(), calls=%async_computation | async-start | bytes 26738688 | tf_op jit(solution)/shard_map/all_gather | solution.py:26
  272.3 36.1 %copy-start = (f32[32,16384]{1,0:T(8,128)S(1)}, f32[32,16384]{1,0:T(8,128)}, u32[]{:S(2)}) copy-start(f32[32,16384]{1,0:T(8,128)} %param.8) | copy-start | bytes 6291460
  272.3 36.1 %copy-start.2 = (f32[16384]{0:T(1024)S(1)}, f32[16384]{0:T(1024)}, u32[]{:S(2)}) copy-start(f32[16384]{0:T(1024)} %param.9) | copy-start | bytes 196612
  322.8 29.4 %copy-start.3 = (s32[256]{0:T(256)S(1)}, s32[256]{0:T(256)}, u32[]{:S(2)}) copy-start(s32[256]{0:T(256)} %param.7) | copy-start | bytes 3076
  322.8 29.7 %copy-start.4 = (s32[512]{0:T(512)S(1)}, s32[512]{0:T(512)}, u32[]{:S(2)}) copy-start(s32[512]{0:T(512)} %param.11) | copy-start | bytes 6148
  390.1 0.8 copy-start.1
  390.9 260.6 %copy-start.5 = (u32[128]{0:T(128)S(1)}, u32[128]{0:T(128)}, u32[]{:S(2)}) copy-start(u32[128]{0:T(128)} %constant.9) | copy-start | bytes 1540
  512.2 149.6 %collective-permute-start = (bf16[16,32768]{1,0:T(8,128)(2,1)S(1)}, bf16[16,32768]{1,0:T(8,128)(2,1)}, u32[]{:S(2)}, u32[]{:S(2)}) collective-permute-start(bf16[16,32768]{1,0:T(8,128)(2,1)S(1)} %fusion), channel_id=1, source_target_pairs={{0,8},{8,16},{16,24},{24,32},{32,40},{40,48},{48,56},{56,64},{64,7... | collective-permute-start | bytes 3145736
  514.1 147.6 %collective-permute-start.1 = (bf16[16,32768]{1,0:T(8,128)(2,1)S(1)}, bf16[16,32768]{1,0:T(8,128)(2,1)}, u32[]{:S(2)}, u32[]{:S(2)}) collective-permute-start(bf16[16,32768]{1,0:T(8,128)(2,1)S(1)} %fusion), channel_id=1, source_target_pairs={{0,16},{8,24},{16,32},{24,40},{32,48},{40,56},{48,64},{56,72},{64,... | collective-permute-start | bytes 3145736
  516.1 145.7 %collective-permute-start.2 = (bf16[16,32768]{1,0:T(8,128)(2,1)S(1)}, bf16[16,32768]{1,0:T(8,128)(2,1)}, u32[]{:S(2)}, u32[]{:S(2)}) collective-permute-start(bf16[16,32768]{1,0:T(8,128)(2,1)S(1)} %fusion), channel_id=1, source_target_pairs={{0,24},{8,32},{16,40},{24,48},{32,56},{40,64},{48,72},{56,80},{64,... | collective-permute-start | bytes 3145736
  519.2 142.6 %collective-permute-start.3 = (bf16[12,32768]{1,0:T(8,128)(2,1)}, bf16[12,32768]{1,0:T(8,128)(2,1)}, u32[]{:S(2)}, u32[]{:S(2)}) collective-permute-start(bf16[12,32768]{1,0:T(8,128)(2,1)} %slice), channel_id=1, source_target_pairs={{0,32},{8,40},{16,48},{24,56},{32,64},{40,72},{48,80},{56,88},{64,... | collective-permute-start | bytes 2359304
  622.4 9.4 %collective-permute-start.7 = (f32[12,32]{1,0:T(8,128)S(1)}, f32[12,32]{1,0:T(8,128)S(1)}, u32[]{:S(2)}, u32[]{:S(2)}) collective-permute-start(f32[12,32]{1,0:T(8,128)S(1)} %slice.1), channel_id=1, source_target_pairs={{0,32},{8,40},{16,48},{24,56},{32,64},{40,72},{48,80},{56,88},{64,... | collective-permute-start | bytes 4616
  631.9 8.6 %collective-permute-start.4 = (f32[16,32]{1,0:T(8,128)S(1)}, f32[16,32]{1,0:T(8,128)S(1)}, u32[]{:S(2)}, u32[]{:S(2)}) collective-permute-start(f32[16,32]{1,0:T(8,128)S(1)} %fusion.1), channel_id=1, source_target_pairs={{0,8},{8,16},{16,24},{24,32},{32,40},{40,48},{48,56},{56,64},{64,7... | collective-permute-start | bytes 6152
  640.5 9.1 %collective-permute-start.5 = (f32[16,32]{1,0:T(8,128)S(1)}, f32[16,32]{1,0:T(8,128)S(1)}, u32[]{:S(2)}, u32[]{:S(2)}) collective-permute-start(f32[16,32]{1,0:T(8,128)S(1)} %fusion.1), channel_id=1, source_target_pairs={{0,16},{8,24},{16,32},{24,40},{32,48},{40,56},{48,64},{56,72},{64,... | collective-permute-start | bytes 6152
  649.6 8.9 %collective-permute-start.6 = (f32[16,32]{1,0:T(8,128)S(1)}, f32[16,32]{1,0:T(8,128)S(1)}, u32[]{:S(2)}, u32[]{:S(2)}) collective-permute-start(f32[16,32]{1,0:T(8,128)S(1)} %fusion.1), channel_id=1, source_target_pairs={{0,24},{8,32},{16,40},{24,48},{32,56},{40,64},{48,72},{56,80},{64,... | collective-permute-start | bytes 6152
Sparse Core Ops, SparseCore 0:
  11.1 147.7 all-gather.1
where the time goes:
time: 736 us; the launch traced here: 731 us
  blocking collectives  237 us (32%)
  local copies, waits for them, and re-layouts  153 us (21%)
  other arithmetic  118 us (16%)
  waiting for transfers between devices  113 us (15%)
  matrix products  80.3 us (11%)
  starting transfers between devices  15.4 us (2%)
  between operations  14.9 us (2%)
    unnamed x2, blocking collectives  200 us
    unnamed x20, local copies, waits for them, and re-layouts  100 us
    all_gather x1, waiting for transfers between devices, shards(): lax.all_gather(projections, 'img', axis=1, tiled=True)  85.6 us
    square x1, other arithmetic, shards(): jnp.square(slab_rows.astype(jnp.float32).reshape(-1, 2, half_len))  81.1 us
    reduce_sum x1, other arithmetic, shards(): jnp.sum(jnp.square(slab_rows.astype(jnp.float32).reshape(-1, 2, half_len)...  36.1 us
    square x1, local copies, waits for them, and re-layouts, shards(): jnp.square(slab_rows.astype(jnp.float32).reshape(-1, 2, half_len))  32.3 us
    dot_general x1, matrix products, shards(): lax.dot_general(weighted, slab_rows, (((1,), (1,)), ((), ())), preferred_...  29.3 us
    unnamed x9, waiting for transfers between devices  27.1 us
  transfers between devices with their start and end apart: 9, of which 5 were waited for; matrix products, arithmetic and copies ran while one was open for 23% of the time, Pallas kernels for 0%

commit v1 on v0

v1 whole, which is shorter than its diff:
```python
import functools

import jax
import jax.numpy as jnp
from jax import lax
from jax.experimental import pallas as pl
from jax.experimental.pallas import tpu as pltpu
from jax.sharding import PartitionSpec as P

PRECISE = lax.Precision.HIGHEST
F32 = jnp.float32
BF16 = jnp.bfloat16
NX, NC = 4, 2
TAIL = 128
NT = (((1,), (1,)), ((), ()))
NN = (((1,), (0,)), ((), ()))
VMEM_LIMIT = 48 * 1024 * 1024


def img_perm(dz, dx, dc):
    pairs = []
    for z in range(2):
        for x in range(NX):
            for c in range(NC):
                src = (z * NX + x) * NC + c
                dst = ((z ^ dz) * NX + (x + dx) % NX) * NC + (c ^ dc)
                pairs.append((src, dst))
    return pairs


def ori_perm(dz, dy):
    return [(z * 4 + y, (z ^ dz) * 4 + (y + dy) % 4) for z in range(2) for y in range(4)]


def to_xp(v):
    return lax.ppermute(v, "img", img_perm(0, 1, 0))


def to_xm(v):
    return lax.ppermute(v, "img", img_perm(0, -1, 0))


def to_z(v):
    return lax.ppermute(v, "img", img_perm(1, 0, 0))


def to_core(v):
    return lax.ppermute(v, "img", img_perm(0, 0, 1))


def params(n=1):
    return pltpu.CompilerParams(
        dimension_semantics=("arbitrary",) * n, vmem_limit_bytes=VMEM_LIMIT
    )


def full(shape):
    return pl.BlockSpec(shape, lambda j: (0,) * len(shape))


def weigh_kernel(core, keep_img, give_img, hot3, contrast, noise, keep_out, give_out):
    amp = contrast[...] * noise[...]
    a1 = amp.astype(BF16)
    rest = amp - a1.astype(F32)
    a2 = rest.astype(BF16)
    a3 = (rest - a2.astype(F32)).astype(BF16)
    table = jnp.concatenate([a1, a2, a3], axis=0)
    amplitude = lax.dot_general(hot3[...], table, NN, preferred_element_type=F32)
    give_out[...] = (give_img[...].astype(F32) * amplitude).astype(BF16)
    keep_out[...] = (keep_img[...].astype(F32) * amplitude).astype(BF16)


def weigh(core, images, hot3, contrast, noise):
    rows, cols = images.shape
    half = cols // 2
    kb = 1024
    nb = half // kb
    classes = contrast.shape[0]
    return pl.pallas_call(
        weigh_kernel,
        grid_spec=pltpu.PrefetchScalarGridSpec(
            num_scalar_prefetch=1,
            grid=(nb,),
            in_specs=[
                pl.BlockSpec((rows, kb), lambda j, s: (0, s[0] * nb + j)),
                pl.BlockSpec((rows, kb), lambda j, s: (0, (1 - s[0]) * nb + j)),
                pl.BlockSpec(hot3.shape, lambda j, s: (0, 0)),
                pl.BlockSpec((classes, kb), lambda j, s: (0, j)),
                pl.BlockSpec((1, kb), lambda j, s: (0, j)),
            ],
            out_specs=[
                pl.BlockSpec((rows, kb), lambda j, s: (0, j)),
                pl.BlockSpec((rows, kb), lambda j, s: (0, j)),
            ],
        ),
        out_shape=[jax.ShapeDtypeStruct((rows, half), BF16)] * 2,
        compiler_params=params(),
        cost_estimate=pl.CostEstimate(
            flops=2 * rows * 96 * half, bytes_accessed=8 * rows * half, transcendentals=0
        ),
        name="weigh",
    )(core, images, images, hot3, contrast, noise)


def score_kernel(n_parts, has_acc, nb, *refs):
    parts = refs[:n_parts]
    w_own, w_sib, contrast, noise, hot = refs[n_parts : n_parts + 5]
    pos = n_parts + 5
    acc_in = refs[pos] if has_acc else None
    out, acc, qacc = refs[pos + has_acc :]
    j = pl.program_id(0)

    @pl.when(j == 0)
    def _():
        acc[...] = jnp.zeros_like(acc)
        qacc[...] = jnp.zeros_like(qacc)

    pieces = [r[...].astype(F32) for r in parts]
    used = sum(p.shape[0] for p in pieces)
    pieces.append(jnp.zeros((128 - used, pieces[0].shape[1]), F32))
    p32 = jnp.concatenate(pieces, axis=0)
    pb = p32.astype(BF16)
    rows = w_own.shape[0]
    acc[:rows, :] += lax.dot_general(w_own[...], pb, NT, preferred_element_type=F32)
    acc[rows:, :] += lax.dot_general(w_sib[...], pb, NT, preferred_element_type=F32)
    sq = p32 * p32
    hi = sq.astype(BF16)
    lo = (sq - hi.astype(F32)).astype(BF16)
    hq = 0.5 * contrast[...] * contrast[...] * noise[...]
    h1 = hq.astype(BF16)
    h2 = (hq - h1.astype(F32)).astype(BF16)
    hh = jnp.concatenate([h1, h2], axis=0)
    qacc[...] += lax.dot_general(hh, hi, NT, preferred_element_type=F32) + lax.dot_general(
        hh, lo, NT, preferred_element_type=F32
    )

    @pl.when(j == nb - 1)
    def _():
        n_cls = h1.shape[0]
        quad = qacc[:n_cls, :] + qacc[n_cls:, :]
        total = acc[...] - jnp.dot(hot[...], quad, precision=PRECISE, preferred_element_type=F32)
        turned = jnp.transpose(total)[:used, :]
        if has_acc:
            turned = turned + acc_in[...]
        out[...] = turned


def score(parts, w_own, w_sib, contrast, noise, hot, quarter, acc_in):
    part_rows, q = parts[0].shape
    rows = w_own.shape[0]
    n_cls = contrast.shape[0]
    kb = 1024
    nb = q // kb
    used = part_rows * len(parts)
    off = quarter * nb
    in_specs = [pl.BlockSpec((part_rows, kb), lambda j: (0, j)) for _ in parts]
    in_specs += [
        pl.BlockSpec((rows, kb), lambda j: (0, off + j)),
        pl.BlockSpec((rows, kb), lambda j: (0, off + j)),
        pl.BlockSpec((n_cls, kb), lambda j: (0, off + j)),
        pl.BlockSpec((1, kb), lambda j: (0, off + j)),
        full(hot.shape),
    ]
    args = [*parts, w_own, w_sib, contrast, noise, hot]
    if acc_in is not None:
        in_specs.append(full((used, 2 * rows)))
        args.append(acc_in)
    return pl.pallas_call(
        functools.partial(score_kernel, len(parts), acc_in is not None, nb),
        grid=(nb,),
        in_specs=in_specs,
        out_specs=full((used, 2 * rows)),
        out_shape=jax.ShapeDtypeStruct((used, 2 * rows), F32),
        scratch_shapes=[
            pltpu.VMEM((2 * rows, 128), F32),
            pltpu.VMEM((2 * n_cls, 128), F32),
        ],
        compiler_params=params(),
        cost_estimate=pl.CostEstimate(
            flops=2 * 2 * rows * 256 * q, bytes_accessed=4 * rows * q, transcendentals=0
        ),
        name="score",
    )(*args)


def stat_kernel(am, ar, bm, br, cnt_a, cnt_b, a_out, b_out, st_out):
    rows = am.shape[1] // 2

    def both(mine, recv):
        r = recv[...]
        return mine[...] + jnp.concatenate([r[:, rows:], r[:, :rows]], axis=1)

    a = both(am, ar)
    b = both(bm, br)
    a_out[...] = a
    b_out[...] = b
    peak = jnp.maximum(jnp.max(a, axis=0, keepdims=True), jnp.max(b, axis=0, keepdims=True))
    mass = jnp.sum(jnp.exp(a - peak) * cnt_a[...], axis=0, keepdims=True) + jnp.sum(
        jnp.exp(b - peak) * cnt_b[...], axis=0, keepdims=True
    )
    st_out[0:1, :] = peak
    st_out[1:2, :] = mass


def chance_kernel(n, *refs):
    a, b, cnt_a, cnt_b, hot = refs[:5]
    stats = refs[5 : 5 + n]
    pa, pb, la, lb, ta, tb = refs[5 + n :]
    peak = stats[0][0:1, :]
    for s in stats[1:]:
        peak = jnp.maximum(peak, s[0:1, :])
    mass = jnp.zeros_like(peak)
    for s in stats:
        mass = mass + s[1:2, :] * jnp.exp(s[0:1, :] - peak)
    shift = peak + jnp.log(mass)
    own = la.shape[1]
    for src, cnt, p_out, l_out, t_out in ((a, cnt_a, pa, la, ta), (b, cnt_b, pb, lb, tb)):
        lw = src[...] - shift
        l_out[...] = lw[:, :own]
        chance = jnp.exp(lw).astype(BF16).astype(F32)
        per = (chance * cnt[...]).astype(BF16)
        p_out[...] = per
        tot = jnp.dot(per, hot[...], preferred_element_type=F32)
        hi = tot.astype(BF16).astype(F32)
        t_out[...] = hi + pltpu.roll(tot - hi, 32, 1)


def whole(kernel, out_shape, name, *args):
    return pl.pallas_call(
        kernel,
        out_shape=out_shape,
        compiler_params=pltpu.CompilerParams(vmem_limit_bytes=VMEM_LIMIT),
        name=name,
    )(*args)


def back_kernel(n_parts, nb, kb, tail, *refs):
    pa, pb, w_own, w_sib, ta, tb = refs[:6]
    outs = refs[6:]
    j = pl.program_id(0)
    per = jnp.concatenate([pa[...], pb[...]], axis=0)
    rows = w_own.shape[0]
    res = lax.dot_general(
        per[:, :rows], w_own[...], NN, preferred_element_type=F32
    ) + lax.dot_general(per[:, rows:], w_sib[...], NN, preferred_element_type=F32)
    h = per.shape[0] // n_parts
    at = pl.ds(pl.multiple_of(j * kb, kb), kb)
    for i, o in enumerate(outs):
        o[:, at] = res[i * h : (i + 1) * h, :].astype(BF16)
    if tail:

        @pl.when(j == nb - 1)
        def _():
            tot = jnp.concatenate([ta[...], tb[...]], axis=0)
            for i, o in enumerate(outs):
                o[:, nb * kb :] = tot[i * h : (i + 1) * h, :].astype(BF16)


def back(pa, pb, w_own, w_sib, ta, tb, quarter, n_parts, tail):
    rows, half = w_own.shape
    q = half // 2
    kb = 1024
    nb = q // kb
    off = quarter * nb
    h = (pa.shape[0] + pb.shape[0]) // n_parts
    width = q + (TAIL if tail else 0)
    return pl.pallas_call(
        functools.partial(back_kernel, n_parts, nb, kb, tail),
        grid=(nb,),
        in_specs=[
            full(pa.shape),
            full(pb.shape),
            pl.BlockSpec((rows, kb), lambda j: (0, off + j)),
            pl.BlockSpec((rows, kb), lambda j: (0, off + j)),
            full(ta.shape),
            full(tb.shape),
        ],
        out_specs=[full((h, width))] * n_parts,
        out_shape=[jax.ShapeDtypeStruct((h, width), BF16)] * n_parts,
        compiler_params=params(),
        cost_estimate=pl.CostEstimate(
            flops=2 * 2 * rows * 256 * q, bytes_accessed=4 * rows * q, transcendentals=0
        ),
        name="back",
    )(pa, pb, w_own, w_sib, ta, tb)


def add_tail(tail):
    tot = tail + pltpu.roll(tail, TAIL - 32, 1)
    lane = lax.broadcasted_iota(jnp.int32, tail.shape, 1)
    tot = jnp.where(lane < 32, tot, 0.0)
    hi = tot.astype(BF16).astype(F32)
    return hi + pltpu.roll(tot - hi, 32, 1)


def add_kernel(n, tail, *refs):
    out = refs[n]
    width = out.shape[1] - (TAIL if tail else 0)
    total = refs[0][...].astype(F32)
    for r in refs[1:n]:
        total = total + r[...].astype(F32)
    if tail:
        out[:, :width] = total[:, :width].astype(BF16)
        out[:, width:] = add_tail(total[:, width:]).astype(BF16)
    else:
        out[...] = total.astype(BF16)


def add(*arrays, tail):
    return whole(
        functools.partial(add_kernel, len(arrays), tail),
        jax.ShapeDtypeStruct(arrays[0].shape, BF16),
        "add",
        *arrays,
    )


def tie(value, *others):
    return lax.optimization_barrier((value, *others))[0]


def shards(images, classes, contrast, noise_weight, projections, proj_index):
    half = contrast.shape[1]
    quart = half // 2
    n_cls = contrast.shape[0]
    own_rows = projections.shape[1]
    h = 2 * own_rows
    me = lax.axis_index("img")
    core = (me % NC).astype(jnp.int32)
    chip = (me // NC).astype(jnp.int32)
    first = core == 0
    noise = noise_weight[None, :]

    mine = projections[0]
    low, high = mine[:, :half], mine[:, half:]
    got = to_core(jnp.where(first, high, low))
    kept = jnp.where(first, low, high)
    shard = jnp.where(
        first, jnp.concatenate([kept, got], axis=0), jnp.concatenate([got, kept], axis=0)
    )
    own = [shard[:, :quart], shard[:, quart:]]

    xm_a, xp_a, zz_a = to_xp(own[0]), to_xm(own[0]), to_z(own[0])
    xm_b, xp_b, zz_b = to_xp(own[1]), to_xm(own[1]), to_z(own[1])
    x2_a, x2_b = to_xp(xm_a), to_xm(xp_b)
    zz_a2, zz_b2 = tie(zz_a, x2_a, x2_b), tie(zz_b, x2_a, x2_b)
    zm_a, zp_a, z2_a = to_xp(zz_a2), to_xm(zz_a2), to_z(x2_a)
    zm_b, zp_b, z2_b = to_xp(zz_b2), to_xm(zz_b2), to_z(x2_b)

    sib_classes = to_core(classes)
    ids = jnp.arange(n_cls, dtype=jnp.int32)[None, :]
    hot_own = (classes[:, None] == ids).astype(BF16)
    both_classes = jnp.concatenate([classes, sib_classes])
    hot = (both_classes[:, None] == ids).astype(F32)
    hot_wide = (both_classes[:, None] == jnp.arange(TAIL, dtype=jnp.int32)[None, :]).astype(BF16)
    hot3 = jnp.concatenate([hot_own] * 3, axis=1)
    w_own, w_give = weigh(core.reshape(1), images, hot3, contrast, noise)
    w_sib = to_core(w_give)

    target = proj_index // h
    dz = (target // NX) ^ (chip // NX)
    dx = (target - chip) % NX
    near = jnp.where(dx == 0, 0, jnp.where(dx == 1, 1, jnp.where(dx == 3, 2, 4)))
    far = jnp.where(dx == 0, 3, jnp.where(dx == 1, 5, jnp.where(dx == 3, 6, 7)))
    rel = jnp.where(dz == 0, near, far) * h + proj_index % h
    block_width = 8 * h
    choose = (jnp.arange(block_width, dtype=jnp.int32)[:, None] == rel[None, :]).astype(F32)
    counts = jnp.sum(choose, axis=1, keepdims=True)
    cnt_a, cnt_b = counts[: 4 * h], counts[4 * h :]

    table = (contrast, noise, hot)
    sa = score([own[0], xp_a, xm_a, zz_a], w_own, w_sib, *table, 0, None)
    sa = score([own[1], xp_b, xm_b, zz_b], w_own, w_sib, *table, 1, sa)
    sb = score([x2_a, zp_a, zm_a, z2_a], w_own, w_sib, *table, 0, None)
    sb = score([x2_b, zp_b, zm_b, z2_b], w_own, w_sib, *table, 1, sb)
    ra, rb = to_core(sa), to_core(sb)
    group = jax.ShapeDtypeStruct(sa.shape, F32)
    stat_shape = jax.ShapeDtypeStruct((2, sa.shape[1]), F32)
    ta, tb, stat = whole(
        stat_kernel, [group, group, stat_shape], "stat", sa, ra, sb, rb, cnt_a, cnt_b
    )
    stats = [stat]
    for z in range(2):
        for y in range(4):
            if z or y:
                stats.append(lax.ppermute(stat, "ori", ori_perm(z, y)))
    per_shape = jax.ShapeDtypeStruct(sa.shape, BF16)
    lw_shape = jax.ShapeDtypeStruct((sa.shape[0], sa.shape[1] // 2), F32)
    tot_shape = jax.ShapeDtypeStruct((sa.shape[0], TAIL), F32)
    pa, pb, la, lb, tot_a, tot_b = whole(
        functools.partial(chance_kernel, len(stats)),
        [per_shape, per_shape, lw_shape, lw_shape, tot_shape, tot_shape],
        "chance",
        ta,
        tb,
        cnt_a,
        cnt_b,
        hot_wide,
        *stats,
    )
    log_weights = lax.dot_general(
        jnp.concatenate([la, lb], axis=0), choose, (((0,), (0,)), ((), ())), precision=PRECISE
    )

    bo_a, bxp_a, bxm_a, bzz_a, bx2_a, bzp_a, bzm_a, bz2_a = back(
        pa, pb, w_own, w_sib, tot_a, tot_b, 0, 8, True
    )
    bo_b, bxp_b, bxm_b, bzz_b, bx2_b, bzp_b, bzm_b, bz2_b = back(
        pa, pb, w_own, w_sib, tot_a, tot_b, 1, 8, False
    )
    r_z2a, r_zma, r_zpa = to_z(bz2_a), to_xm(bzm_a), to_xp(bzp_a)
    r_z2b, r_zmb, r_zpb = to_z(bz2_b), to_xm(bzm_b), to_xp(bzp_b)
    r_x2a = to_xm(add(bx2_a, r_z2a, tail=True))
    r_x2b = to_xp(add(bx2_b, r_z2b, tail=False))
    r_zza = to_z(add(bzz_a, r_zma, r_zpa, tail=True))
    r_zzb = to_z(add(bzz_b, r_zmb, r_zpb, tail=False))
    r_xpa, r_xmb = to_xp(bxp_a), to_xm(bxm_b)
    r_xma = to_xm(add(bxm_a, r_x2a, tail=True))
    r_xpb = to_xp(add(bxp_b, r_x2b, tail=False))
    fin_a = add(bo_a, r_xpa, r_xma, r_zza, tail=True)
    fin_b = add(bo_b, r_xpb, r_xmb, r_zzb, tail=False)

    fin = jnp.concatenate([fin_a[:, :quart], fin_b], axis=1)
    got = to_core(jnp.where(first, fin[own_rows:], fin[:own_rows]))
    kept = jnp.where(first, fin[:own_rows], fin[own_rows:])
    back_sums = jnp.where(
        first, jnp.concatenate([kept, got], axis=1), jnp.concatenate([got, kept], axis=1)
    )
    ends = fin_a[:, quart:].astype(F32)
    totals = ends[:, :n_cls] + ends[:, n_cls : 2 * n_cls]
    totals = jnp.where(first, totals[:own_rows], totals[own_rows:])
    contrast_mass = jnp.dot(totals, contrast * contrast, precision=PRECISE)
    return log_weights, back_sums[None], contrast_mass[None]


def solution(mesh):
    in_specs = (P("img", None), P("img"), P(), P(), P("ori", "img", None), P("ori"))
    out_specs = (P("img", "ori"), P("ori", "img", None), P("ori", "img", None))
    return jax.shard_map(shards, mesh=mesh, in_specs=in_specs, out_specs=out_specs, check_vma=False)
```

time: 736 us -> 198 us (0.27)
  the two profiles are of different devices: /device:TPU:72 before, /device:TPU:1 now
where the time goes in v1:
time: 198 us; the launch traced here: 197 us
  Pallas kernels  69.9 us (35%)
  starting transfers between devices  64.6 us (33%)
  waiting for transfers between devices  51.2 us (26%)
  local copies, waits for them, and re-layouts  4.54 us (2%)
  other arithmetic  3.37 us (2%)
  matrix products  2.39 us (1%)
    pallas_call x4, Pallas kernels, score(): pl.pallas_call(functools.partial(score_kernel, len(parts), acc_in is not...  34.3 us
    ppermute x10, starting transfers between devices, to_xm(): return lax.ppermute(v, 'img', img_perm(0, -1, 0))  23.4 us
    pallas_call x1, Pallas kernels, weigh(): pl.pallas_call(weigh_kernel, grid_spec=pltpu.PrefetchScalarGridSpec(num_s...  19.2 us
    ppermute x8, starting transfers between devices, to_z(): return lax.ppermute(v, 'img', img_perm(1, 0, 0))  17.3 us
    ppermute x8, waiting for transfers between devices, to_z(): return lax.ppermute(v, 'img', img_perm(1, 0, 0))  16.8 us
    pallas_call x2, Pallas kernels, back(): pl.pallas_call(functools.partial(back_kernel, n_parts, nb, kb, tail), gri...  14.1 us
    ppermute x10, waiting for transfers between devices, to_xm(): return lax.ppermute(v, 'img', img_perm(0, -1, 0))  12 us
    ppermute x6, starting transfers between devices, to_core(): return lax.ppermute(v, 'img', img_perm(0, 0, 1))  11.7 us
  transfers between devices with their start and end apart: 41, of which 15 were waited for; matrix products, arithmetic and copies ran while one was open for 3% of the time, Pallas kernels for 22%

profile of v1, /device:TPU:1, one launch (start us, length us, event | category | flops | bytes accessed | tf_op | source)
XLA Modules:
  0.0 197.1 jit_solution(7489591028058800949)
XLA Ops:
  0.6 0.8 iota_compare_fusion.4
  1.6 1.6 copy-done
  3.2 0.8 copy-done.2
  4.0 19.2 %weigh.1 = (bf16[256,16384]{1,0:T(8,128)(2,1)}, bf16[256,16384]{1,0:T(8,128)(2,1)}) custom-call(s32[1]{0:T(128)} %bitcast.1.core, bf16[256,32768]{1,0:T(8,128)(2,1)} %give_img.1, bf16[256,32768]{1,0:T(8,128)(2,1)} %give_img.1, bf16[256,96]{1,0:T(8,128)(2,1)S(1)} %add_convert_fusion.hot3, f32[32,16384]{1,0:T(8,128)S(1)} %copy-done, f32[1,16384]{1,0:T(1,128)S(1)} %bitcast.12), custom_call_target="tpu_custom_call" | custom-call | flops 805306368 | bytes 33554432 | tf_op jit(solution)/shard_map/weigh/pallas_call | solution.py:79
  23.2 1.4 collective-permute-start.4
  24.9 9.1 %collective-permute-done = bf16[12,16384]{1,0:T(8,128)(2,1)S(1)} collective-permute-done((bf16[12,16384]{1,0:T(8,128)(2,1)S(1)}, bf16[12,16384]{1,0:T(8,128)(2,1)S(1)}, u32[]{:S(2)}, u32[]{:S(2)}) %collective-permute-start) | collective-permute-done | bytes 393248 | tf_op jit(solution)/shard_map/ppermute | solution.py:48
  34.0 0.4 maximum_select_fusion.1
  34.4 2.6 %collective-permute-start.1 = (bf16[24,8192]{1,0:T(8,128)(2,1)S(1)}, bf16[24,8192]{1,0:T(8,128)(2,1)S(1)}, u32[]{:S(2)}, u32[]{:S(2)}) collective-permute-start(bf16[24,8192]{1,0:T(8,128)(2,1)S(1)} %get-tuple-element.72.refs_0_), channel_id=1, source_target_pairs={{0,48},{8,56},{16,0},{24,8},{32,16},{40,24},{48,32},{56,40},{64,11... | collective-permute-start | bytes 1179656 | tf_op jit(solution)/shard_map/ppermute | solution.py:40
  37.1 3.6 %collective-permute-start.8 = (bf16[24,8192]{1,0:T(8,128)(2,1)S(1)}, bf16[24,8192]{1,0:T(8,128)(2,1)}, u32[]{:S(2)}, u32[]{:S(2)}) collective-permute-start(bf16[24,8192]{1,0:T(8,128)(2,1)S(1)} %get-tuple-element.71.refs_0_), channel_id=1, source_target_pairs={{0,64},{8,72},{16,80},{24,88},{32,96},{40,104},{48,112},{56,120},{... | collective-permute-start | bytes 1179656 | tf_op jit(solution)/shard_map/ppermute | solution.py:44
  40.7 0.7 collective-permute-start.5
  41.4 4.1 %collective-permute-done.1.refs_1_ = bf16[24,8192]{1,0:T(8,128)(2,1)S(1)} collective-permute-done((bf16[24,8192]{1,0:T(8,128)(2,1)S(1)}, bf16[24,8192]{1,0:T(8,128)(2,1)S(1)}, u32[]{:S(2)}, u32[]{:S(2)}) %collective-permute-start.1) | collective-permute-done | bytes 393248 | tf_op jit(solution)/shard_map/ppermute | solution.py:40
  45.4 3.5 %collective-permute-start.10 = (bf16[24,8192]{1,0:T(8,128)(2,1)S(1)}, bf16[24,8192]{1,0:T(8,128)(2,1)}, u32[]{:S(2)}, u32[]{:S(2)}) collective-permute-start(bf16[24,8192]{1,0:T(8,128)(2,1)S(1)} %collective-permute-done.1.refs_1_), channel_id=1, source_target_pairs={{0,48},{8,56},{16,0},{24,8},{32,16},{40,24},{48,32},{56,40},{64,11... | collective-permute-start | bytes 1179656 | tf_op jit(solution)/shard_map/ppermute | solution.py:40
  49.1 3.6 %collective-permute-start.3 = (bf16[24,8192]{1,0:T(8,128)(2,1)S(1)}, bf16[24,8192]{1,0:T(8,128)(2,1)S(1)}, u32[]{:S(2)}, u32[]{:S(2)}) collective-permute-start(bf16[24,8192]{1,0:T(8,128)(2,1)S(1)} %get-tuple-element.72.refs_0_), channel_id=1, source_target_pairs={{0,64},{8,72},{16,80},{24,88},{32,96},{40,104},{48,112},{56,120},{... | collective-permute-start | bytes 1179656 | tf_op jit(solution)/shard_map/ppermute | solution.py:44
  52.7 2.7 %collective-permute-start.6 = (bf16[24,8192]{1,0:T(8,128)(2,1)S(1)}, bf16[24,8192]{1,0:T(8,128)(2,1)S(1)}, u32[]{:S(2)}, u32[]{:S(2)}) collective-permute-start(bf16[24,8192]{1,0:T(8,128)(2,1)S(1)} %get-tuple-element.71.refs_0_), channel_id=1, source_target_pairs={{0,48},{8,56},{16,0},{24,8},{32,16},{40,24},{48,32},{56,40},{64,11... | collective-permute-start | bytes 1179656 | tf_op jit(solution)/shard_map/ppermute | solution.py:40
  55.4 1.1 collective-permute-done.10.refs_0_
  56.5 3.4 %collective-permute-done.11.refs_0_ = bf16[24,8192]{1,0:T(8,128)(2,1)} collective-permute-done((bf16[24,8192]{1,0:T(8,128)(2,1)}, bf16[24,8192]{1,0:T(8,128)(2,1)}, u32[]{:S(2)}, u32[]{:S(2)}) %collective-permute-start.11) | collective-permute-done | bytes 393248 | tf_op jit(solution)/shard_map/ppermute | solution.py:36
  60.2 0.7 collective-permute-done.3.refs_3_
  60.9 0.7 collective-permute-start.16
  61.6 3.3 %collective-permute-done.6.refs_1_ = bf16[24,8192]{1,0:T(8,128)(2,1)S(1)} collective-permute-done((bf16[24,8192]{1,0:T(8,128)(2,1)S(1)}, bf16[24,8192]{1,0:T(8,128)(2,1)S(1)}, u32[]{:S(2)}, u32[]{:S(2)}) %collective-permute-start.6) | collective-permute-done | bytes 393248 | tf_op jit(solution)/shard_map/ppermute | solution.py:40
  65.0 3.4 %collective-permute-start.12 = (bf16[24,8192]{1,0:T(8,128)(2,1)S(1)}, bf16[24,8192]{1,0:T(8,128)(2,1)S(1)}, u32[]{:S(2)}, u32[]{:S(2)}) collective-permute-start(bf16[24,8192]{1,0:T(8,128)(2,1)S(1)} %collective-permute-done.3.refs_3_), channel_id=1, source_target_pairs={{0,48},{8,56},{16,0},{24,8},{32,16},{40,24},{48,32},{56,40},{64,11... | collective-permute-start | bytes 1179656 | tf_op jit(solution)/shard_map/ppermute | solution.py:40
  68.4 3.4 %collective-permute-start.17 = (bf16[24,8192]{1,0:T(8,128)(2,1)}, bf16[24,8192]{1,0:T(8,128)(2,1)S(1)}, u32[]{:S(2)}, u32[]{:S(2)}) collective-permute-start(bf16[24,8192]{1,0:T(8,128)(2,1)} %collective-permute-done.11.refs_0_), channel_id=1, source_target_pairs={{0,64},{8,72},{16,80},{24,88},{32,96},{40,104},{48,112},{56,120},{... | collective-permute-start | bytes 1179656 | tf_op jit(solution)/shard_map/ppermute | solution.py:44
  71.8 8.7 %score.4.refs_9_ = f32[96,512]{1,0:T(8,128)S(1)} custom-call(bf16[24,8192]{1,0:T(8,128)(2,1)S(1)} %get-tuple-element.71.refs_0_, bf16[24,8192]{1,0:T(8,128)(2,1)S(1)} %collective-permute-done.6.refs_1_, bf16[24,8192]{1,0:T(8,128)(2,1)} %collective-permute-done.7.refs_2_, bf16[24,8192]{1,0:T(8,128)(2,1)} %collective-permute-done.8.refs_3_, ...), custom_call_target="tpu_custom_call" | custom-call | flops 2147483648 | bytes 8388608 | tf_op jit(solution)/shard_map/score/pallas_call | solution.py:168
  80.6 8.6 %score.5.am = f32[96,512]{1,0:T(8,128)S(1)} custom-call(bf16[24,8192]{1,0:T(8,128)(2,1)S(1)} %get-tuple-element.72.refs_0_, bf16[24,8192]{1,0:T(8,128)(2,1)S(1)} %collective-permute-done.1.refs_1_, bf16[24,8192]{1,0:T(8,128)(2,1)S(1)} %collective-permute-done.2.refs_2_, bf16[24,8192]{1,0:T(8,128)(2,1)S(1)} %collective-permute-done.3.refs_3_, ...), custom_call_target="tpu_custom_call" | custom-call | flops 2147483648 | bytes 8388608 | tf_op jit(solution)/shard_map/score/pallas_call | solution.py:168
  89.3 4.0 %collective-permute-start.9 = (f32[96,512]{1,0:T(8,128)S(1)}, f32[96,512]{1,0:T(8,128)S(1)}, u32[]{:S(2)}, u32[]{:S(2)}) collective-permute-start(f32[96,512]{1,0:T(8,128)S(1)} %score.5.am), channel_id=1, source_target_pairs={{0,8},{8,0},{16,24},{24,16},{32,40},{40,32},{48,56},{56,48},{64,72... | collective-permute-start | bytes 589832 | tf_op jit(solution)/shard_map/ppermute | solution.py:48
  93.2 8.5 %score.6.refs_9_ = f32[96,512]{1,0:T(8,128)S(1)} custom-call(bf16[24,8192]{1,0:T(8,128)(2,1)} %collective-permute-done.11.refs_0_, bf16[24,8192]{1,0:T(8,128)(2,1)S(1)} %collective-permute-done.15.refs_1_, bf16[24,8192]{1,0:T(8,128)(2,1)S(1)} %collective-permute-done.16.refs_2_, bf16[24,8192]{1,0:T(8,128)(2,1)S(1)} %collective-permute-done.17.refs_3_, ...), custom_call_target="tpu_custom_call" | custom-call | flops 2147483648 | bytes 8388608 | tf_op jit(solution)/shard_map/score/pallas_call | solution.py:168
  101.8 8.6 %score.7.bm = f32[96,512]{1,0:T(8,128)S(1)} custom-call(bf16[24,8192]{1,0:T(8,128)(2,1)} %collective-permute-done.10.refs_0_, bf16[24,8192]{1,0:T(8,128)(2,1)S(1)} %collective-permute-done.12.refs_1_, bf16[24,8192]{1,0:T(8,128)(2,1)S(1)} %collective-permute-done.13.refs_2_, bf16[24,8192]{1,0:T(8,128)(2,1)S(1)} %collective-permute-done.14.refs_3_, ...), custom_call_target="tpu_custom_call" | custom-call | flops 2147483648 | bytes 8388608 | tf_op jit(solution)/shard_map/score/pallas_call | solution.py:168
  110.8 1.1 collective-permute-done.18.br
  112.0 1.4 collective-permute-start.19
  113.4 2.6 %collective-permute-start.20 = (f32[2,512]{1,0:T(2,128)S(1)}, f32[2,512]{1,0:T(2,128)S(1)}, u32[]{:S(2)}, u32[]{:S(2)}) collective-permute-start(f32[2,512]{1,0:T(2,128)S(1)} %get-tuple-element.38.refs_5_), channel_id=1, source_target_pairs={{0,2},{1,3},{2,0},{3,1},{4,6},{5,7},{6,4},{7,5},{8,10},{9,11},{10,... | collective-permute-start | bytes 12296 | tf_op jit(solution)/shard_map/ppermute | solution.py:386
  116.0 1.1 collective-permute-start.21
  117.1 1.2 collective-permute-start.22
  118.3 0.3 collective-permute-start.23
  118.7 1.7 collective-permute-start.24
  120.4 1.6 collective-permute-start.25
  122.2 0.7 collective-permute-done.23.refs_10_
  122.9 0.6 collective-permute-done.24.refs_11_
  123.5 0.2 collective-permute-done.25.refs_12_
  123.8 0.4 chance.1
  124.1 7.0 %back.2 = (bf16[24,8320]{1,0:T(8,128)(2,1)S(1)}, bf16[24,8320]{1,0:T(8,128)(2,1)S(1)}, bf16[24,8320]{1,0:T(8,128)(2,1)S(1)}, bf16[24,8320]{1,0:T(8,128)(2,1)S(1)...) custom-call(bf16[96,512]{1,0:T(8,128)(2,1)S(1)} %get-tuple-element.4, ...), custom_call_target="tpu_custom_call" | custom-call | flops 2147483648 | bytes 8388608 | tf_op jit(solution)/shard_map/back/pallas_call | solution.py:267
  131.2 3.3 %collective-permute-start.27 = (bf16[24,8320]{1,0:T(8,128)(2,1)S(1)}, bf16[24,8320]{1,0:T(8,128)(2,1)S(1)}, u32[]{:S(2)}, u32[]{:S(2)}) collective-permute-start(bf16[24,8320]{1,0:T(8,128)(2,1)S(1)} %get-tuple-element.49), channel_id=1, source_target_pairs={{0,64},{8,72},{16,80},{24,88},{32,96},{40,104},{48,112},{56,120},{... | collective-permute-start | bytes 1198088 | tf_op jit(solution)/shard_map/ppermute | solution.py:44
  134.5 2.9 %collective-permute-start.30 = (bf16[24,8320]{1,0:T(8,128)(2,1)S(1)}, bf16[24,8320]{1,0:T(8,128)(2,1)S(1)}, u32[]{:S(2)}, u32[]{:S(2)}) collective-permute-start(bf16[24,8320]{1,0:T(8,128)(2,1)S(1)} %get-tuple-element.51), channel_id=1, source_target_pairs={{0,48},{8,56},{16,0},{24,8},{32,16},{40,24},{48,32},{56,40},{64,11... | collective-permute-start | bytes 1198088 | tf_op jit(solution)/shard_map/ppermute | solution.py:40
  137.4 7.0 %back.3 = (bf16[24,8192]{1,0:T(8,128)(2,1)S(1)}, bf16[24,8192]{1,0:T(8,128)(2,1)S(1)}, bf16[24,8192]{1,0:T(8,128)(2,1)S(1)}, bf16[24,8192]{1,0:T(8,128)(2,1)S(1)...) custom-call(bf16[96,512]{1,0:T(8,128)(2,1)S(1)} %get-tuple-element.4, ...), custom_call_target="tpu_custom_call" | custom-call | flops 2147483648 | bytes 8388608 | tf_op jit(solution)/shard_map/back/pallas_call | solution.py:267
  144.6 0.2 add.49
  144.8 2.7 %collective-permute-start.28 = (bf16[24,8320]{1,0:T(8,128)(2,1)S(1)}, bf16[24,8320]{1,0:T(8,128)(2,1)S(1)}, u32[]{:S(2)}, u32[]{:S(2)}) collective-permute-start(bf16[24,8320]{1,0:T(8,128)(2,1)S(1)} %add.49), channel_id=1, source_target_pairs={{0,48},{8,56},{16,0},{24,8},{32,16},{40,24},{48,32},{56,40},{64,11... | collective-permute-start | bytes 1198088 | tf_op jit(solution)/shard_map/ppermute | solution.py:40
  147.7 5.8 %collective-permute-done.33.refs_1_ = bf16[24,8192]{1,0:T(8,128)(2,1)S(1)} collective-permute-done((bf16[24,8192]{1,0:T(8,128)(2,1)S(1)}, bf16[24,8192]{1,0:T(8,128)(2,1)S(1)}, u32[]{:S(2)}, u32[]{:S(2)}) %collective-permute-start.33) | collective-permute-done | bytes 393248 | tf_op jit(solution)/shard_map/ppermute | solution.py:44
  153.5 0.9 collective-permute-start.34
  154.4 2.0 collective-permute-start.36
  156.4 0.3 add.51
  156.7 0.5 collective-permute-start.26
  157.2 0.2 add.50
  157.5 3.5 %collective-permute-done.37.refs_1_ = bf16[24,8192]{1,0:T(8,128)(2,1)S(1)} collective-permute-done((bf16[24,8192]{1,0:T(8,128)(2,1)S(1)}, bf16[24,8192]{1,0:T(8,128)(2,1)S(1)}, u32[]{:S(2)}, u32[]{:S(2)}) %collective-permute-start.37) | collective-permute-done | bytes 393248 | tf_op jit(solution)/shard_map/ppermute | solution.py:40
  161.0 2.6 %collective-permute-start.32 = (bf16[24,8320]{1,0:T(8,128)(2,1)S(1)}, bf16[24,8320]{1,0:T(8,128)(2,1)S(1)}, u32[]{:S(2)}, u32[]{:S(2)}) collective-permute-start(bf16[24,8320]{1,0:T(8,128)(2,1)S(1)} %add.51), channel_id=1, source_target_pairs={{0,64},{8,72},{16,80},{24,88},{32,96},{40,104},{48,112},{56,120},{... | collective-permute-start | bytes 1198088 | tf_op jit(solution)/shard_map/ppermute | solution.py:44
  163.6 3.4 %collective-permute-start.29 = (bf16[24,8320]{1,0:T(8,128)(2,1)S(1)}, bf16[24,8320]{1,0:T(8,128)(2,1)S(1)}, u32[]{:S(2)}, u32[]{:S(2)}) collective-permute-start(bf16[24,8320]{1,0:T(8,128)(2,1)S(1)} %add.50), channel_id=1, source_target_pairs={{0,48},{8,56},{16,0},{24,8},{32,16},{40,24},{48,32},{56,40},{64,11... | collective-permute-start | bytes 1198088 | tf_op jit(solution)/shard_map/ppermute | solution.py:40
  167.2 2.3 %collective-permute-done.34.refs_1_ = bf16[24,8192]{1,0:T(8,128)(2,1)S(1)} collective-permute-done((bf16[24,8192]{1,0:T(8,128)(2,1)S(1)}, bf16[24,8192]{1,0:T(8,128)(2,1)S(1)}, u32[]{:S(2)}, u32[]{:S(2)}) %collective-permute-start.34) | collective-permute-done | bytes 393248 | tf_op jit(solution)/shard_map/ppermute | solution.py:36
  169.5 0.5 collective-permute-start.39
  170.2 1.2 fusion.2
  171.4 10.3 %collective-permute-done.39.refs_3_ = bf16[24,8192]{1,0:T(8,128)(2,1)S(1)} collective-permute-done((bf16[24,8192]{1,0:T(8,128)(2,1)S(1)}, bf16[24,8192]{1,0:T(8,128)(2,1)S(1)}, u32[]{:S(2)}, u32[]{:S(2)}) %collective-permute-start.39) | collective-permute-done | bytes 393248 | tf_op jit(solution)/shard_map/ppermute | solution.py:44
  181.7 4.8 %collective-permute-done.35.refs_1_ = bf16[24,8192]{1,0:T(8,128)(2,1)S(1)} collective-permute-done((bf16[24,8192]{1,0:T(8,128)(2,1)S(1)}, bf16[24,8192]{1,0:T(8,128)(2,1)S(1)}, u32[]{:S(2)}, u32[]{:S(2)}) %collective-permute-start.35) | collective-permute-done | bytes 393248 | tf_op jit(solution)/shard_map/ppermute | solution.py:36
  186.7 0.4 add.52
  187.2 0.2 select_bitcast_fusion
  187.4 5.4 %collective-permute-start.40 = (bf16[12,16384]{1,0:T(8,128)(2,1)S(1)}, bf16[12,16384]{1,0:T(8,128)(2,1)S(1)}, u32[]{:S(2)}, u32[]{:S(2)}) collective-permute-start(bf16[12,16384]{1,0:T(8,128)(2,1)S(1)} %get-tuple-element.70), channel_id=1, source_target_pairs={{0,8},{8,0},{16,24},{24,16},{32,40},{40,32},{48,56},{56,48},{64,72... | collective-permute-start | bytes 1179656 | tf_op jit(solution)/shard_map/ppermute | solution.py:48
  192.9 1.2 convolution_bitcast_fusion
  194.1 1.7 copy.18
  195.8 1.3 maximum_select_fusion
  (72 shorter events, 2.7 us)
Async XLA Ops:
  1.6 1.6 copy-start
  3.2 0.8 copy-start.2
  4.0 20.7 %copy-start.4 = (bf16[1,12,32768]{2,1,0:T(8,128)(2,1)S(1)}, bf16[1,12,32768]{2,1,0:T(8,128)(2,1)}, u32[]{:S(2)}) copy-start(bf16[1,12,32768]{2,1,0:T(8,128)(2,1)} %param.10) | copy-start | bytes 2359300
  23.2 45.1 %collective-permute-start.4 = (bf16[256,16384]{1,0:T(8,128)(2,1)}, bf16[256,16384]{1,0:T(8,128)(2,1)}, u32[]{:S(2)}, u32[]{:S(2)}) collective-permute-start(bf16[256,16384]{1,0:T(8,128)(2,1)} %get-tuple-element.33), channel_id=1, source_target_pairs={{0,8},{8,0},{16,24},{24,16},{32,40},{40,32},{48,56},{56,48},{64,72... | collective-permute-start | bytes 25165832 | tf_op jit(solution)/shard_map/ppermute | solution.py:48
  24.8 15.9 %copy-start.5 = (s32[256]{0:T(256)S(1)}, s32[256]{0:T(256)}, u32[]{:S(2)}) copy-start(s32[256]{0:T(256)} %param.7) | copy-start | bytes 3076
  24.8 24.2 %copy-start.6 = (s32[512]{0:T(512)S(1)}, s32[512]{0:T(512)}, u32[]{:S(2)}) copy-start(s32[512]{0:T(512)} %param.11) | copy-start | bytes 6148
  24.8 47.0 %copy-start.1 = (f32[32,16384]{1,0:T(8,128)S(1)}, f32[32,16384]{1,0:T(8,128)}, u32[]{:S(2)}) copy-start(f32[32,16384]{1,0:T(8,128)} %refs_6_.7) | copy-start | bytes 6291460
  24.8 47.0 %copy-start.3 = (f32[16384]{0:T(1024)S(1)}, f32[16384]{0:T(1024)}, u32[]{:S(2)}) copy-start(f32[16384]{0:T(1024)} %param.9) | copy-start | bytes 196612
  24.8 9.2 %collective-permute-start = (bf16[12,16384]{1,0:T(8,128)(2,1)S(1)}, bf16[12,16384]{1,0:T(8,128)(2,1)S(1)}, u32[]{:S(2)}, u32[]{:S(2)}) collective-permute-start(bf16[12,16384]{1,0:T(8,128)(2,1)S(1)} %get-tuple-element.68), channel_id=1, source_target_pairs={{0,8},{8,0},{16,24},{24,16},{32,40},{40,32},{48,56},{56,48},{64,72... | collective-permute-start | bytes 1179656 | tf_op jit(solution)/shard_map/ppermute | solution.py:48
  34.4 11.0 %collective-permute-start.1 = (bf16[24,8192]{1,0:T(8,128)(2,1)S(1)}, bf16[24,8192]{1,0:T(8,128)(2,1)S(1)}, u32[]{:S(2)}, u32[]{:S(2)}) collective-permute-start(bf16[24,8192]{1,0:T(8,128)(2,1)S(1)} %get-tuple-element.72.refs_0_), channel_id=1, source_target_pairs={{0,48},{8,56},{16,0},{24,8},{32,16},{40,24},{48,32},{56,40},{64,11... | collective-permute-start | bytes 1179656 | tf_op jit(solution)/shard_map/ppermute | solution.py:40
  37.0 11.9 %collective-permute-start.7 = (bf16[24,8192]{1,0:T(8,128)(2,1)S(1)}, bf16[24,8192]{1,0:T(8,128)(2,1)}, u32[]{:S(2)}, u32[]{:S(2)}) collective-permute-start(bf16[24,8192]{1,0:T(8,128)(2,1)S(1)} %get-tuple-element.71.refs_0_), channel_id=1, source_target_pairs={{0,16},{8,24},{16,32},{24,40},{32,48},{40,56},{48,0},{56,8},{64,80... | collective-permute-start | bytes 1179656 | tf_op jit(solution)/shard_map/ppermute | solution.py:36
  37.1 15.7 %collective-permute-start.8 = (bf16[24,8192]{1,0:T(8,128)(2,1)S(1)}, bf16[24,8192]{1,0:T(8,128)(2,1)}, u32[]{:S(2)}, u32[]{:S(2)}) collective-permute-start(bf16[24,8192]{1,0:T(8,128)(2,1)S(1)} %get-tuple-element.71.refs_0_), channel_id=1, source_target_pairs={{0,64},{8,72},{16,80},{24,88},{32,96},{40,104},{48,112},{56,120},{... | collective-permute-start | bytes 1179656 | tf_op jit(solution)/shard_map/ppermute | solution.py:44
  40.7 8.5 %collective-permute-start.5 = (s32[256]{0:T(256)S(1)}, s32[256]{0:T(256)S(1)}, u32[]{:S(2)}, u32[]{:S(2)}) collective-permute-start(s32[256]{0:T(256)S(1)} %copy-done.5), channel_id=1, source_target_pairs={{0,8},{8,0},{16,24},{24,16},{32,40},{40,32},{48,56},{56,48},{64,72... | collective-permute-start | bytes 3080 | tf_op jit(solution)/shard_map/ppermute | solution.py:48
  45.4 11.1 %collective-permute-start.10 = (bf16[24,8192]{1,0:T(8,128)(2,1)S(1)}, bf16[24,8192]{1,0:T(8,128)(2,1)}, u32[]{:S(2)}, u32[]{:S(2)}) collective-permute-start(bf16[24,8192]{1,0:T(8,128)(2,1)S(1)} %collective-permute-done.1.refs_1_), channel_id=1, source_target_pairs={{0,48},{8,56},{16,0},{24,8},{32,16},{40,24},{48,32},{56,40},{64,11... | collective-permute-start | bytes 1179656 | tf_op jit(solution)/shard_map/ppermute | solution.py:40
  48.9 11.0 %collective-permute-start.11 = (bf16[24,8192]{1,0:T(8,128)(2,1)}, bf16[24,8192]{1,0:T(8,128)(2,1)}, u32[]{:S(2)}, u32[]{:S(2)}) collective-permute-start(bf16[24,8192]{1,0:T(8,128)(2,1)} %collective-permute-done.7.refs_2_), channel_id=1, source_target_pairs={{0,16},{8,24},{16,32},{24,40},{32,48},{40,56},{48,0},{56,8},{64,80... | collective-permute-start | bytes 1179656 | tf_op jit(solution)/shard_map/ppermute | solution.py:36
  49.1 11.8 %collective-permute-start.3 = (bf16[24,8192]{1,0:T(8,128)(2,1)S(1)}, bf16[24,8192]{1,0:T(8,128)(2,1)S(1)}, u32[]{:S(2)}, u32[]{:S(2)}) collective-permute-start(bf16[24,8192]{1,0:T(8,128)(2,1)S(1)} %get-tuple-element.72.refs_0_), channel_id=1, source_target_pairs={{0,64},{8,72},{16,80},{24,88},{32,96},{40,104},{48,112},{56,120},{... | collective-permute-start | bytes 1179656 | tf_op jit(solution)/shard_map/ppermute | solution.py:44
  52.7 12.2 %collective-permute-start.6 = (bf16[24,8192]{1,0:T(8,128)(2,1)S(1)}, bf16[24,8192]{1,0:T(8,128)(2,1)S(1)}, u32[]{:S(2)}, u32[]{:S(2)}) collective-permute-start(bf16[24,8192]{1,0:T(8,128)(2,1)S(1)} %get-tuple-element.71.refs_0_), channel_id=1, source_target_pairs={{0,48},{8,56},{16,0},{24,8},{32,16},{40,24},{48,32},{56,40},{64,11... | collective-permute-start | bytes 1179656 | tf_op jit(solution)/shard_map/ppermute | solution.py:40
  56.5 23.9 %collective-permute-start.2 = (bf16[24,8192]{1,0:T(8,128)(2,1)S(1)}, bf16[24,8192]{1,0:T(8,128)(2,1)S(1)}, u32[]{:S(2)}, u32[]{:S(2)}) collective-permute-start(bf16[24,8192]{1,0:T(8,128)(2,1)S(1)} %get-tuple-element.72.refs_0_), channel_id=1, source_target_pairs={{0,16},{8,24},{16,32},{24,40},{32,48},{40,56},{48,0},{56,8},{64,80... | collective-permute-start | bytes 1179656 | tf_op jit(solution)/shard_map/ppermute | solution.py:36
  59.9 20.6 %collective-permute-start.15 = (bf16[24,8192]{1,0:T(8,128)(2,1)}, bf16[24,8192]{1,0:T(8,128)(2,1)S(1)}, u32[]{:S(2)}, u32[]{:S(2)}) collective-permute-start(bf16[24,8192]{1,0:T(8,128)(2,1)} %collective-permute-done.8.refs_3_), channel_id=1, source_target_pairs={{0,48},{8,56},{16,0},{24,8},{32,16},{40,24},{48,32},{56,40},{64,11... | collective-permute-start | bytes 1179656 | tf_op jit(solution)/shard_map/ppermute | solution.py:40
  60.9 28.3 %collective-permute-start.16 = (bf16[24,8192]{1,0:T(8,128)(2,1)}, bf16[24,8192]{1,0:T(8,128)(2,1)S(1)}, u32[]{:S(2)}, u32[]{:S(2)}) collective-permute-start(bf16[24,8192]{1,0:T(8,128)(2,1)} %collective-permute-done.8.refs_3_), channel_id=1, source_target_pairs={{0,16},{8,24},{16,32},{24,40},{32,48},{40,56},{48,0},{56,8},{64,80... | collective-permute-start | bytes 1179656 | tf_op jit(solution)/shard_map/ppermute | solution.py:36
  65.0 36.8 %collective-permute-start.12 = (bf16[24,8192]{1,0:T(8,128)(2,1)S(1)}, bf16[24,8192]{1,0:T(8,128)(2,1)S(1)}, u32[]{:S(2)}, u32[]{:S(2)}) collective-permute-start(bf16[24,8192]{1,0:T(8,128)(2,1)S(1)} %collective-permute-done.3.refs_3_), channel_id=1, source_target_pairs={{0,48},{8,56},{16,0},{24,8},{32,16},{40,24},{48,32},{56,40},{64,11... | collective-permute-start | bytes 1179656 | tf_op jit(solution)/shard_map/ppermute | solution.py:40
  68.4 24.9 %collective-permute-start.17 = (bf16[24,8192]{1,0:T(8,128)(2,1)}, bf16[24,8192]{1,0:T(8,128)(2,1)S(1)}, u32[]{:S(2)}, u32[]{:S(2)}) collective-permute-start(bf16[24,8192]{1,0:T(8,128)(2,1)} %collective-permute-done.11.refs_0_), channel_id=1, source_target_pairs={{0,64},{8,72},{16,80},{24,88},{32,96},{40,104},{48,112},{56,120},{... | collective-permute-start | bytes 1179656 | tf_op jit(solution)/shard_map/ppermute | solution.py:44
  80.4 21.3 %collective-permute-start.13 = (bf16[24,8192]{1,0:T(8,128)(2,1)S(1)}, bf16[24,8192]{1,0:T(8,128)(2,1)S(1)}, u32[]{:S(2)}, u32[]{:S(2)}) collective-permute-start(bf16[24,8192]{1,0:T(8,128)(2,1)S(1)} %collective-permute-done.3.refs_3_), channel_id=1, source_target_pairs={{0,16},{8,24},{16,32},{24,40},{32,48},{40,56},{48,0},{56,8},{64,80... | collective-permute-start | bytes 1179656 | tf_op jit(solution)/shard_map/ppermute | solution.py:36
  80.5 21.2 %collective-permute-start.14 = (bf16[24,8192]{1,0:T(8,128)(2,1)}, bf16[24,8192]{1,0:T(8,128)(2,1)S(1)}, u32[]{:S(2)}, u32[]{:S(2)}) collective-permute-start(bf16[24,8192]{1,0:T(8,128)(2,1)} %collective-permute-done.10.refs_0_), channel_id=1, source_target_pairs={{0,64},{8,72},{16,80},{24,88},{32,96},{40,104},{48,112},{56,120},{... | collective-permute-start | bytes 1179656 | tf_op jit(solution)/shard_map/ppermute | solution.py:44
  89.3 21.5 %collective-permute-start.9 = (f32[96,512]{1,0:T(8,128)S(1)}, f32[96,512]{1,0:T(8,128)S(1)}, u32[]{:S(2)}, u32[]{:S(2)}) collective-permute-start(f32[96,512]{1,0:T(8,128)S(1)} %score.5.am), channel_id=1, source_target_pairs={{0,8},{8,0},{16,24},{24,16},{32,40},{40,32},{48,56},{56,48},{64,72... | collective-permute-start | bytes 589832 | tf_op jit(solution)/shard_map/ppermute | solution.py:48
  110.4 1.5 collective-permute-start.18
  112.0 6.7 %collective-permute-start.19 = (f32[2,512]{1,0:T(2,128)S(1)}, f32[2,512]{1,0:T(2,128)S(1)}, u32[]{:S(2)}, u32[]{:S(2)}) collective-permute-start(f32[2,512]{1,0:T(2,128)S(1)} %get-tuple-element.38.refs_5_), channel_id=1, source_target_pairs={{0,1},{1,2},{2,3},{3,0},{4,5},{5,6},{6,7},{7,4},{8,9},{9,10},{10,1... | collective-permute-start | bytes 12296 | tf_op jit(solution)/shard_map/ppermute | solution.py:386
  113.4 7.0 %collective-permute-start.20 = (f32[2,512]{1,0:T(2,128)S(1)}, f32[2,512]{1,0:T(2,128)S(1)}, u32[]{:S(2)}, u32[]{:S(2)}) collective-permute-start(f32[2,512]{1,0:T(2,128)S(1)} %get-tuple-element.38.refs_5_), channel_id=1, source_target_pairs={{0,2},{1,3},{2,0},{3,1},{4,6},{5,7},{6,4},{7,5},{8,10},{9,11},{10,... | collective-permute-start | bytes 12296 | tf_op jit(solution)/shard_map/ppermute | solution.py:386
  116.0 6.2 %collective-permute-start.21 = (f32[2,512]{1,0:T(2,128)S(1)}, f32[2,512]{1,0:T(2,128)S(1)}, u32[]{:S(2)}, u32[]{:S(2)}) collective-permute-start(f32[2,512]{1,0:T(2,128)S(1)} %get-tuple-element.38.refs_5_), channel_id=1, source_target_pairs={{0,3},{1,0},{2,1},{3,2},{4,7},{5,4},{6,5},{7,6},{8,11},{9,8},{10,9... | collective-permute-start | bytes 12296 | tf_op jit(solution)/shard_map/ppermute | solution.py:386
  117.1 5.1 %collective-permute-start.22 = (f32[2,512]{1,0:T(2,128)S(1)}, f32[2,512]{1,0:T(2,128)S(1)}, u32[]{:S(2)}, u32[]{:S(2)}) collective-permute-start(f32[2,512]{1,0:T(2,128)S(1)} %get-tuple-element.38.refs_5_), channel_id=1, source_target_pairs={{0,4},{1,5},{2,6},{3,7},{4,0},{5,1},{6,2},{7,3},{8,12},{9,13},{10,... | collective-permute-start | bytes 12296 | tf_op jit(solution)/shard_map/ppermute | solution.py:386
  118.3 4.6 %collective-permute-start.23 = (f32[2,512]{1,0:T(2,128)S(1)}, f32[2,512]{1,0:T(2,128)S(1)}, u32[]{:S(2)}, u32[]{:S(2)}) collective-permute-start(f32[2,512]{1,0:T(2,128)S(1)} %get-tuple-element.38.refs_5_), channel_id=1, source_target_pairs={{0,5},{1,6},{2,7},{3,4},{4,1},{5,2},{6,3},{7,0},{8,13},{9,14},{10,... | collective-permute-start | bytes 12296 | tf_op jit(solution)/shard_map/ppermute | solution.py:386
  118.7 4.9 %collective-permute-start.24 = (f32[2,512]{1,0:T(2,128)S(1)}, f32[2,512]{1,0:T(2,128)S(1)}, u32[]{:S(2)}, u32[]{:S(2)}) collective-permute-start(f32[2,512]{1,0:T(2,128)S(1)} %get-tuple-element.38.refs_5_), channel_id=1, source_target_pairs={{0,6},{1,7},{2,4},{3,5},{4,2},{5,3},{6,0},{7,1},{8,14},{9,15},{10,... | collective-permute-start | bytes 12296 | tf_op jit(solution)/shard_map/ppermute | solution.py:386
  120.4 3.4 %collective-permute-start.25 = (f32[2,512]{1,0:T(2,128)S(1)}, f32[2,512]{1,0:T(2,128)S(1)}, u32[]{:S(2)}, u32[]{:S(2)}) collective-permute-start(f32[2,512]{1,0:T(2,128)S(1)} %get-tuple-element.38.refs_5_), channel_id=1, source_target_pairs={{0,7},{1,4},{2,5},{3,6},{4,3},{5,0},{6,1},{7,2},{8,15},{9,12},{10,... | collective-permute-start | bytes 12296 | tf_op jit(solution)/shard_map/ppermute | solution.py:386
  131.2 13.4 %collective-permute-start.27 = (bf16[24,8320]{1,0:T(8,128)(2,1)S(1)}, bf16[24,8320]{1,0:T(8,128)(2,1)S(1)}, u32[]{:S(2)}, u32[]{:S(2)}) collective-permute-start(bf16[24,8320]{1,0:T(8,128)(2,1)S(1)} %get-tuple-element.49), channel_id=1, source_target_pairs={{0,64},{8,72},{16,80},{24,88},{32,96},{40,104},{48,112},{56,120},{... | collective-permute-start | bytes 1198088 | tf_op jit(solution)/shard_map/ppermute | solution.py:44
  134.5 19.0 %collective-permute-start.30 = (bf16[24,8320]{1,0:T(8,128)(2,1)S(1)}, bf16[24,8320]{1,0:T(8,128)(2,1)S(1)}, u32[]{:S(2)}, u32[]{:S(2)}) collective-permute-start(bf16[24,8320]{1,0:T(8,128)(2,1)S(1)} %get-tuple-element.51), channel_id=1, source_target_pairs={{0,48},{8,56},{16,0},{24,8},{32,16},{40,24},{48,32},{56,40},{64,11... | collective-permute-start | bytes 1198088 | tf_op jit(solution)/shard_map/ppermute | solution.py:40
  137.4 17.0 %collective-permute-start.31 = (bf16[24,8320]{1,0:T(8,128)(2,1)S(1)}, bf16[24,8320]{1,0:T(8,128)(2,1)S(1)}, u32[]{:S(2)}, u32[]{:S(2)}) collective-permute-start(bf16[24,8320]{1,0:T(8,128)(2,1)S(1)} %get-tuple-element.52), channel_id=1, source_target_pairs={{0,16},{8,24},{16,32},{24,40},{32,48},{40,56},{48,0},{56,8},{64,80... | collective-permute-start | bytes 1198088 | tf_op jit(solution)/shard_map/ppermute | solution.py:36
  144.5 9.0 %collective-permute-start.33 = (bf16[24,8192]{1,0:T(8,128)(2,1)S(1)}, bf16[24,8192]{1,0:T(8,128)(2,1)S(1)}, u32[]{:S(2)}, u32[]{:S(2)}) collective-permute-start(bf16[24,8192]{1,0:T(8,128)(2,1)S(1)} %get-tuple-element.56), channel_id=1, source_target_pairs={{0,64},{8,72},{16,80},{24,88},{32,96},{40,104},{48,112},{56,120},{... | collective-permute-start | bytes 1179656 | tf_op jit(solution)/shard_map/ppermute | solution.py:44
  144.8 11.9 %collective-permute-start.28 = (bf16[24,8320]{1,0:T(8,128)(2,1)S(1)}, bf16[24,8320]{1,0:T(8,128)(2,1)S(1)}, u32[]{:S(2)}, u32[]{:S(2)}) collective-permute-start(bf16[24,8320]{1,0:T(8,128)(2,1)S(1)} %add.49), channel_id=1, source_target_pairs={{0,48},{8,56},{16,0},{24,8},{32,16},{40,24},{48,32},{56,40},{64,11... | collective-permute-start | bytes 1198088 | tf_op jit(solution)/shard_map/ppermute | solution.py:40
  147.6 13.4 %collective-permute-start.37 = (bf16[24,8192]{1,0:T(8,128)(2,1)S(1)}, bf16[24,8192]{1,0:T(8,128)(2,1)S(1)}, u32[]{:S(2)}, u32[]{:S(2)}) collective-permute-start(bf16[24,8192]{1,0:T(8,128)(2,1)S(1)} %get-tuple-element.59), channel_id=1, source_target_pairs={{0,48},{8,56},{16,0},{24,8},{32,16},{40,24},{48,32},{56,40},{64,11... | collective-permute-start | bytes 1179656 | tf_op jit(solution)/shard_map/ppermute | solution.py:40
  153.4 10.2 %collective-permute-start.38 = (bf16[24,8192]{1,0:T(8,128)(2,1)S(1)}, bf16[24,8192]{1,0:T(8,128)(2,1)S(1)}, u32[]{:S(2)}, u32[]{:S(2)}) collective-permute-start(bf16[24,8192]{1,0:T(8,128)(2,1)S(1)} %get-tuple-element.60), channel_id=1, source_target_pairs={{0,16},{8,24},{16,32},{24,40},{32,48},{40,56},{48,0},{56,8},{64,80... | collective-permute-start | bytes 1179656 | tf_op jit(solution)/shard_map/ppermute | solution.py:36
  153.5 16.0 %collective-permute-start.34 = (bf16[24,8192]{1,0:T(8,128)(2,1)S(1)}, bf16[24,8192]{1,0:T(8,128)(2,1)S(1)}, u32[]{:S(2)}, u32[]{:S(2)}) collective-permute-start(bf16[24,8192]{1,0:T(8,128)(2,1)S(1)} %add.53), channel_id=1, source_target_pairs={{0,16},{8,24},{16,32},{24,40},{32,48},{40,56},{48,0},{56,8},{64,80... | collective-permute-start | bytes 1179656 | tf_op jit(solution)/shard_map/ppermute | solution.py:36
  154.4 15.7 %collective-permute-start.36 = (bf16[24,8192]{1,0:T(8,128)(2,1)S(1)}, bf16[24,8192]{1,0:T(8,128)(2,1)S(1)}, u32[]{:S(2)}, u32[]{:S(2)}) collective-permute-start(bf16[24,8192]{1,0:T(8,128)(2,1)S(1)} %get-tuple-element.57), channel_id=1, source_target_pairs={{0,48},{8,56},{16,0},{24,8},{32,16},{40,24},{48,32},{56,40},{64,11... | collective-permute-start | bytes 1179656 | tf_op jit(solution)/shard_map/ppermute | solution.py:40
  156.7 30.0 %collective-permute-start.26 = (bf16[24,8320]{1,0:T(8,128)(2,1)S(1)}, bf16[24,8320]{1,0:T(8,128)(2,1)S(1)}, u32[]{:S(2)}, u32[]{:S(2)}) collective-permute-start(bf16[24,8320]{1,0:T(8,128)(2,1)S(1)} %get-tuple-element.46), channel_id=1, source_target_pairs={{0,16},{8,24},{16,32},{24,40},{32,48},{40,56},{48,0},{56,8},{64,80... | collective-permute-start | bytes 1198088 | tf_op jit(solution)/shard_map/ppermute | solution.py:36
  161.0 25.7 %collective-permute-start.32 = (bf16[24,8320]{1,0:T(8,128)(2,1)S(1)}, bf16[24,8320]{1,0:T(8,128)(2,1)S(1)}, u32[]{:S(2)}, u32[]{:S(2)}) collective-permute-start(bf16[24,8320]{1,0:T(8,128)(2,1)S(1)} %add.51), channel_id=1, source_target_pairs={{0,64},{8,72},{16,80},{24,88},{32,96},{40,104},{48,112},{56,120},{... | collective-permute-start | bytes 1198088 | tf_op jit(solution)/shard_map/ppermute | solution.py:44
  163.6 23.1 %collective-permute-start.29 = (bf16[24,8320]{1,0:T(8,128)(2,1)S(1)}, bf16[24,8320]{1,0:T(8,128)(2,1)S(1)}, u32[]{:S(2)}, u32[]{:S(2)}) collective-permute-start(bf16[24,8320]{1,0:T(8,128)(2,1)S(1)} %add.50), channel_id=1, source_target_pairs={{0,48},{8,56},{16,0},{24,8},{32,16},{40,24},{48,32},{56,40},{64,11... | collective-permute-start | bytes 1198088 | tf_op jit(solution)/shard_map/ppermute | solution.py:40
  169.5 12.2 %collective-permute-start.39 = (bf16[24,8192]{1,0:T(8,128)(2,1)S(1)}, bf16[24,8192]{1,0:T(8,128)(2,1)S(1)}, u32[]{:S(2)}, u32[]{:S(2)}) collective-permute-start(bf16[24,8192]{1,0:T(8,128)(2,1)S(1)} %add.55), channel_id=1, source_target_pairs={{0,64},{8,72},{16,80},{24,88},{32,96},{40,104},{48,112},{56,120},{... | collective-permute-start | bytes 1179656 | tf_op jit(solution)/shard_map/ppermute | solution.py:44
  170.1 16.4 %collective-permute-start.35 = (bf16[24,8192]{1,0:T(8,128)(2,1)S(1)}, bf16[24,8192]{1,0:T(8,128)(2,1)S(1)}, u32[]{:S(2)}, u32[]{:S(2)}) collective-permute-start(bf16[24,8192]{1,0:T(8,128)(2,1)S(1)} %add.54), channel_id=1, source_target_pairs={{0,16},{8,24},{16,32},{24,40},{32,48},{40,56},{48,0},{56,8},{64,80... | collective-permute-start | bytes 1179656 | tf_op jit(solution)/shard_map/ppermute | solution.py:36
  187.4 8.3 %collective-permute-start.40 = (bf16[12,16384]{1,0:T(8,128)(2,1)S(1)}, bf16[12,16384]{1,0:T(8,128)(2,1)S(1)}, u32[]{:S(2)}, u32[]{:S(2)}) collective-permute-start(bf16[12,16384]{1,0:T(8,128)(2,1)S(1)} %get-tuple-element.70), channel_id=1, source_target_pairs={{0,8},{8,0},{16,24},{24,16},{32,40},{40,32},{48,56},{56,48},{64,72... | collective-permute-start | bytes 1179656 | tf_op jit(solution)/shard_map/ppermute | solution.py:48

commit v2 on v1

v2 whole, which is shorter than its diff:
```python
import functools

import jax
import jax.numpy as jnp
from jax import lax
from jax.experimental import pallas as pl
from jax.experimental.pallas import tpu as pltpu
from jax.sharding import PartitionSpec as P

PRECISE = lax.Precision.HIGHEST
F32 = jnp.float32
BF16 = jnp.bfloat16
NX, NC = 4, 2
TAIL = 128
LANES = 256
KB = 1024
CHEAP = pl.CostEstimate(flops=1024, bytes_accessed=1024, transcendentals=0)
NT = (((1,), (1,)), ((), ()))
NN = (((1,), (0,)), ((), ()))
VMEM_LIMIT = 48 * 1024 * 1024


def img_perm(dz, dx, dc):
    pairs = []
    for z in range(2):
        for x in range(NX):
            for c in range(NC):
                src = (z * NX + x) * NC + c
                dst = ((z ^ dz) * NX + (x + dx) % NX) * NC + (c ^ dc)
                pairs.append((src, dst))
    return pairs


def ori_perm(dz, dy):
    return [(z * 4 + y, (z ^ dz) * 4 + (y + dy) % 4) for z in range(2) for y in range(4)]


def to_xp(v):
    return lax.ppermute(v, "img", img_perm(0, 1, 0))


def to_xm(v):
    return lax.ppermute(v, "img", img_perm(0, -1, 0))


def to_z(v):
    return lax.ppermute(v, "img", img_perm(1, 0, 0))


def to_core(v):
    return lax.ppermute(v, "img", img_perm(0, 0, 1))


def params(mib=48):
    return pltpu.CompilerParams(
        dimension_semantics=("arbitrary",), vmem_limit_bytes=mib * 1024 * 1024
    )


def full(shape):
    return pl.BlockSpec(shape, lambda j: (0,) * len(shape))


def weigh_kernel(core, keep, give, hot3, contrast, noise, keep_out, give_out):
    amp = contrast[...] * noise[...]
    a1 = amp.astype(BF16)
    rest = amp - a1.astype(F32)
    a2 = rest.astype(BF16)
    a3 = (rest - a2.astype(F32)).astype(BF16)
    table = jnp.concatenate([a1, a2, a3], axis=0)
    amplitude = lax.dot_general(hot3[...], table, NN, preferred_element_type=F32)
    for img, out in ((give, give_out), (keep, keep_out)):
        value = (img[...].astype(F32) * amplitude).astype(BF16)
        for i in range(out.shape[0]):
            out[i] = value[:, i * KB : (i + 1) * KB]


def weigh(core, images, hot3, contrast, noise, quarter):
    rows, cols = images.shape
    half = cols // 2
    wide = 4
    kb = wide * KB
    nb = half // kb
    n_cls = contrast.shape[0]
    off = quarter * nb // 2
    return pl.pallas_call(
        weigh_kernel,
        grid_spec=pltpu.PrefetchScalarGridSpec(
            num_scalar_prefetch=1,
            grid=(nb // 2,),
            in_specs=[
                pl.BlockSpec((rows, kb), lambda j, s: (0, s[0] * nb + off + j)),
                pl.BlockSpec((rows, kb), lambda j, s: (0, (1 - s[0]) * nb + off + j)),
                pl.BlockSpec(hot3.shape, lambda j, s: (0, 0)),
                pl.BlockSpec((n_cls, kb), lambda j, s: (0, off + j)),
                pl.BlockSpec((1, kb), lambda j, s: (0, off + j)),
            ],
            out_specs=[pl.BlockSpec((wide, rows, KB), lambda j, s: (j, 0, 0))] * 2,
        ),
        out_shape=[jax.ShapeDtypeStruct((half // KB // 2, rows, KB), BF16)] * 2,
        compiler_params=params(),
        cost_estimate=CHEAP,
        name="weigh",
    )(core, images, images, hot3, contrast, noise)


def table_kernel(contrast, noise, out):
    hq = 0.5 * contrast[...] * contrast[...] * noise[...]
    h1 = hq.astype(BF16)
    h2 = (hq - h1.astype(F32)).astype(BF16)
    out[...] = jnp.concatenate([h1, h2], axis=0)


def quad_table(contrast, noise):
    n_cls, half = contrast.shape
    kb = 4 * KB
    return pl.pallas_call(
        table_kernel,
        grid=(half // kb,),
        in_specs=[
            pl.BlockSpec((n_cls, kb), lambda j: (0, j)),
            pl.BlockSpec((1, kb), lambda j: (0, j)),
        ],
        out_specs=pl.BlockSpec((2 * n_cls, kb), lambda j: (0, j)),
        out_shape=jax.ShapeDtypeStruct((2 * n_cls, half), BF16),
        compiler_params=params(),
        cost_estimate=CHEAP,
        name="table",
    )(contrast, noise)


def score_kernel(n_parts, has_acc, nb, wide, *refs):
    parts = refs[:n_parts]
    w_own, w_sib, quads, hot = refs[n_parts : n_parts + 4]
    pos = n_parts + 4
    acc_in = refs[pos] if has_acc else None
    out, acc, qacc = refs[pos + has_acc :]
    j = pl.program_id(0)

    @pl.when(j == 0)
    def _():
        acc[...] = jnp.zeros_like(acc)
        qacc[...] = jnp.zeros_like(qacc)

    rows = w_own.shape[1]
    own, sib, quad = None, None, None
    for i in range(wide):
        cols = slice(i * KB, (i + 1) * KB)
        pieces = [r[:, cols].astype(F32) for r in parts]
        used = sum(p.shape[0] for p in pieces)
        pieces.append(jnp.zeros((LANES - used, KB), F32))
        p32 = jnp.concatenate(pieces, axis=0)
        pb = p32.astype(BF16)
        d_own = lax.dot_general(w_own[i], pb, NT, preferred_element_type=F32)
        d_sib = lax.dot_general(w_sib[i], pb, NT, preferred_element_type=F32)
        sq = p32 * p32
        hi = sq.astype(BF16)
        lo = (sq - hi.astype(F32)).astype(BF16)
        hh = quads[:, cols]
        d_quad = lax.dot_general(hh, hi, NT, preferred_element_type=F32) + lax.dot_general(
            hh, lo, NT, preferred_element_type=F32
        )
        own = d_own if own is None else own + d_own
        sib = d_sib if sib is None else sib + d_sib
        quad = d_quad if quad is None else quad + d_quad
    acc[:rows, :] += own
    acc[rows:, :] += sib
    qacc[...] += quad

    @pl.when(j == nb - 1)
    def _():
        n_cls = qacc.shape[0] // 2
        q = qacc[:n_cls, :] + qacc[n_cls:, :]
        total = acc[...] - jnp.dot(hot[...], q, precision=PRECISE, preferred_element_type=F32)
        turned = jnp.transpose(total)[:used, :]
        if has_acc:
            turned = turned + acc_in[...]
        out[...] = turned


def score(parts, w_own, w_sib, quads, hot, quarter, acc_in):
    part_rows = parts[0].shape[0]
    rows = w_own.shape[1]
    wide = 2
    kb = wide * KB
    nb = w_own.shape[0] // wide
    used = part_rows * len(parts)
    off = quarter * nb
    in_specs = [pl.BlockSpec((part_rows, kb), lambda j: (0, j)) for _ in parts]
    in_specs += [
        pl.BlockSpec((wide, rows, KB), lambda j: (j, 0, 0)),
        pl.BlockSpec((wide, rows, KB), lambda j: (j, 0, 0)),
        pl.BlockSpec((quads.shape[0], kb), lambda j: (0, off + j)),
        full(hot.shape),
    ]
    args = [*parts, w_own, w_sib, quads, hot]
    if acc_in is not None:
        in_specs.append(full((used, 2 * rows)))
        args.append(acc_in)
    return pl.pallas_call(
        functools.partial(score_kernel, len(parts), acc_in is not None, nb, wide),
        grid=(nb,),
        in_specs=in_specs,
        out_specs=full((used, 2 * rows)),
        out_shape=jax.ShapeDtypeStruct((used, 2 * rows), F32),
        scratch_shapes=[
            pltpu.VMEM((2 * rows, LANES), F32),
            pltpu.VMEM((quads.shape[0], LANES), F32),
        ],
        compiler_params=params(),
        cost_estimate=CHEAP,
        name="score",
    )(*args)


def stat_kernel(mine, recv, cnt, out, st_out):
    rows = mine.shape[1] // 2
    r = recv[...]
    total = mine[...] + jnp.concatenate([r[:, rows:], r[:, :rows]], axis=1)
    out[...] = total
    peak = jnp.max(total, axis=0, keepdims=True)
    st_out[0:1, :] = peak
    st_out[1:2, :] = jnp.sum(jnp.exp(total - peak) * cnt[...], axis=0, keepdims=True)


def merge(stats):
    peak = stats[0][0:1, :]
    for s in stats[1:]:
        peak = jnp.maximum(peak, s[0:1, :])
    mass = jnp.zeros_like(peak)
    for s in stats:
        mass = mass + s[1:2, :] * jnp.exp(s[0:1, :] - peak)
    return peak, mass


def merge_kernel(*refs):
    peak, mass = merge(refs[:-1])
    refs[-1][0:1, :] = peak
    refs[-1][1:2, :] = mass


def chance_kernel(n, *refs):
    scores, cnt, hot = refs[:3]
    p_out, t_out, l_out = refs[3 + n :]
    peak, mass = merge(refs[3 : 3 + n])
    shift = peak + jnp.log(mass)
    own = l_out.shape[1]
    lw = scores[...] - shift
    l_out[...] = lw[:, :own]
    chance = jnp.exp(lw).astype(BF16).astype(F32)
    per = (chance * cnt[...]).astype(BF16)
    p_out[...] = per
    tot = jnp.dot(per, hot[...], preferred_element_type=F32)
    hi = tot.astype(BF16).astype(F32)
    t_out[...] = hi + pltpu.roll(tot - hi, 32, 1)


def whole(kernel, out_shape, name, *args):
    return pl.pallas_call(
        kernel,
        out_shape=out_shape,
        compiler_params=pltpu.CompilerParams(vmem_limit_bytes=VMEM_LIMIT),
        cost_estimate=CHEAP,
        name=name,
    )(*args)


def back_kernel(n_parts, nb, wide, tail, *refs):
    per, w_own, w_sib, tot = refs[:4]
    outs = refs[4:]
    j = pl.program_id(0)
    rows = w_own.shape[1]
    h = per.shape[0] // n_parts
    for i in range(wide):
        res = lax.dot_general(
            per[:, :rows], w_own[i], NN, preferred_element_type=F32
        ) + lax.dot_general(per[:, rows:], w_sib[i], NN, preferred_element_type=F32)
        at = pl.ds(pl.multiple_of(j * wide * KB + i * KB, KB), KB)
        for k, o in enumerate(outs):
            o[:, at] = res[k * h : (k + 1) * h, :].astype(BF16)
    if tail:

        @pl.when(j == nb - 1)
        def _():
            for k, o in enumerate(outs):
                o[:, nb * wide * KB :] = tot[k * h : (k + 1) * h, :].astype(BF16)


def back(per, w_own, w_sib, tot, quarter, n_parts):
    blocks, rows, _ = w_own.shape
    wide = 2
    nb = blocks // wide
    h = per.shape[0] // n_parts
    tail = quarter == 0
    width = nb * wide * KB + (TAIL if tail else 0)
    return pl.pallas_call(
        functools.partial(back_kernel, n_parts, nb, wide, tail),
        grid=(nb,),
        in_specs=[
            full(per.shape),
            pl.BlockSpec((wide, rows, KB), lambda j: (j, 0, 0)),
            pl.BlockSpec((wide, rows, KB), lambda j: (j, 0, 0)),
            full(tot.shape),
        ],
        out_specs=[full((h, width))] * n_parts,
        out_shape=[jax.ShapeDtypeStruct((h, width), BF16)] * n_parts,
        compiler_params=params(),
        cost_estimate=CHEAP,
        name="back",
    )(per, w_own, w_sib, tot)


def add_tail(tail):
    tot = tail + pltpu.roll(tail, TAIL - 32, 1)
    lane = lax.broadcasted_iota(jnp.int32, tail.shape, 1)
    tot = jnp.where(lane < 32, tot, 0.0)
    hi = tot.astype(BF16).astype(F32)
    return hi + pltpu.roll(tot - hi, 32, 1)


def add_kernel(n, tail, *refs):
    out = refs[n]
    width = out.shape[1] - (TAIL if tail else 0)
    total = refs[0][...].astype(F32)
    for r in refs[1:n]:
        total = total + r[...].astype(F32)
    if tail:
        out[:, :width] = total[:, :width].astype(BF16)
        out[:, width:] = add_tail(total[:, width:]).astype(BF16)
    else:
        out[...] = total.astype(BF16)


def add(*arrays, tail):
    return whole(
        functools.partial(add_kernel, len(arrays), tail),
        jax.ShapeDtypeStruct(arrays[0].shape, BF16),
        "add",
        *arrays,
    )


def tie(value, *others):
    return lax.optimization_barrier((value, *others))[0]


def shards(images, classes, contrast, noise_weight, projections, proj_index):
    half = contrast.shape[1]
    quart = half // 2
    n_cls = contrast.shape[0]
    own_rows = projections.shape[1]
    h = 2 * own_rows
    me = lax.axis_index("img")
    core = (me % NC).astype(jnp.int32)
    chip = (me // NC).astype(jnp.int32)
    first = core == 0
    noise = noise_weight[None, :]

    mine = projections[0]
    low, high = mine[:, :half], mine[:, half:]
    got = to_core(jnp.where(first, high, low))
    kept = jnp.where(first, low, high)
    shard = jnp.where(
        first, jnp.concatenate([kept, got], axis=0), jnp.concatenate([got, kept], axis=0)
    )
    own_a, own_b = shard[:, :quart], shard[:, quart:]
    xm_a, xp_a, zz = to_xp(own_a), to_xm(own_a), to_z(shard)
    xm_b, xp_b = to_xp(own_b), to_xm(own_b)
    zz_a, zz_b = zz[:, :quart], zz[:, quart:]
    x2_a, x2_b = to_xp(xm_a), to_xm(xp_b)
    fz_a, fz_b = tie(zz_a, x2_a, x2_b), tie(zz_b, x2_a, x2_b)
    zm_a, zp_a, z2_a = to_xp(fz_a), to_xm(fz_a), to_z(x2_a)
    zm_b, zp_b, z2_b = to_xp(fz_b), to_xm(fz_b), to_z(x2_b)

    sib_classes = to_core(classes)
    ids = jnp.arange(n_cls, dtype=jnp.int32)[None, :]
    hot_own = (classes[:, None] == ids).astype(BF16)
    both_classes = jnp.concatenate([classes, sib_classes])
    hot = (both_classes[:, None] == ids).astype(F32)
    hot_wide = (both_classes[:, None] == jnp.arange(TAIL, dtype=jnp.int32)[None, :]).astype(BF16)
    hot3 = jnp.concatenate([hot_own] * 3, axis=1)
    w_own, w_sib = [], []
    for quarter in range(2):
        before = (xm_b, xp_b) if quarter else (shard,)
        after = (x2_a, x2_b) if quarter else (xm_b, xp_b, zz)
        at = tie(core.reshape(1), *before)
        keep, give = weigh(at, images, hot3, contrast, noise, quarter)
        w_own.append(keep)
        w_sib.append(to_core(tie(give, *after)))
    quads = quad_table(contrast, noise)

    target = proj_index // h
    dz = (target // NX) ^ (chip // NX)
    dx = (target - chip) % NX
    near = jnp.where(dx == 0, 0, jnp.where(dx == 1, 1, jnp.where(dx == 3, 2, 4)))
    far = jnp.where(dx == 0, 3, jnp.where(dx == 1, 5, jnp.where(dx == 3, 6, 7)))
    rel = jnp.where(dz == 0, near, far) * h + proj_index % h
    block_width = 8 * h
    choose = (jnp.arange(block_width, dtype=jnp.int32)[:, None] == rel[None, :]).astype(F32)
    counts = jnp.sum(choose, axis=1, keepdims=True)

    table = (quads, hot)
    part = [own_a, xp_a, xm_a, zz_a, x2_a, zp_a, zm_a, z2_a]
    mine = score(part, w_own[0], w_sib[0], *table, 0, None)
    part = [own_b, xp_b, xm_b, zz_b, x2_b, zp_b, zm_b, z2_b]
    mine = score(part, w_own[1], w_sib[1], *table, 1, mine)
    stat_shape = jax.ShapeDtypeStruct((2, mine.shape[1]), F32)
    scores, stat = whole(
        stat_kernel,
        [jax.ShapeDtypeStruct(mine.shape, F32), stat_shape],
        "stat",
        mine,
        to_core(mine),
        counts,
    )
    stat = whole(
        merge_kernel,
        stat_shape,
        "merge",
        stat,
        lax.ppermute(stat, "ori", ori_perm(1, 0)),
    )
    stats = [stat] + [lax.ppermute(stat, "ori", ori_perm(0, y)) for y in range(1, 4)]
    per, tot, local = whole(
        functools.partial(chance_kernel, len(stats)),
        [
            jax.ShapeDtypeStruct((block_width, stat.shape[1]), BF16),
            jax.ShapeDtypeStruct((block_width, TAIL), F32),
            jax.ShapeDtypeStruct((block_width, stat.shape[1] // 2), F32),
        ],
        "chance",
        scores,
        counts,
        hot_wide,
        *stats,
    )
    log_weights = lax.dot_general(
        local, choose, (((0,), (0,)), ((), ())), precision=PRECISE
    )

    bo_a, bxp_a, bxm_a, bzz_a, bx2_a, bzp_a, bzm_a, bz2_a = back(
        per, w_own[0], w_sib[0], tot, 0, 8
    )
    bo_b, bxp_b, bxm_b, bzz_b, bx2_b, bzp_b, bzm_b, bz2_b = back(
        per, w_own[1], w_sib[1], tot, 1, 8
    )
    r_z2a, r_zma, r_zpa = to_z(bz2_a), to_xm(bzm_a), to_xp(bzp_a)
    r_z2b, r_zmb = to_z(bz2_b), to_xm(bzm_b)
    r_zpb = to_xp(tie(bzp_b, r_z2a))
    r_x2a = to_xm(tie(add(bx2_a, r_z2a, tail=True), r_zma))
    r_x2b = to_xp(tie(add(bx2_b, r_z2b, tail=False), r_zpa))
    r_zza = to_z(add(bzz_a, r_zma, r_zpa, tail=True))
    r_zzb = to_z(add(bzz_b, r_zmb, r_zpb, tail=False))
    r_xmb, r_xpa = to_xm(tie(bxm_b, r_zmb)), to_xp(tie(bxp_a, r_zpb))
    r_xma = to_xm(add(bxm_a, r_x2a, tail=True))
    r_xpb = to_xp(add(bxp_b, r_x2b, tail=False))
    fin_a = add(bo_a, r_xpa, r_xma, r_zza, tail=True)
    fin_b = add(bo_b, r_xpb, r_xmb, r_zzb, tail=False)

    fin = jnp.concatenate([fin_a[:, :quart], fin_b], axis=1)
    got = to_core(jnp.where(first, fin[own_rows:], fin[:own_rows]))
    kept = jnp.where(first, fin[:own_rows], fin[own_rows:])
    back_sums = jnp.where(
        first, jnp.concatenate([kept, got], axis=1), jnp.concatenate([got, kept], axis=1)
    )
    ends = fin_a[:, quart:].astype(F32)
    totals = ends[:, :n_cls] + ends[:, n_cls : 2 * n_cls]
    totals = jnp.where(first, totals[:own_rows], totals[own_rows:])
    contrast_mass = jnp.dot(totals, contrast * contrast, precision=PRECISE)
    return log_weights, back_sums[None], contrast_mass[None]


def solution(mesh):
    in_specs = (P("img", None), P("img"), P(), P(), P("ori", "img", None), P("ori"))
    out_specs = (P("img", "ori"), P("ori", "img", None), P("ori", "img", None))
    return jax.shard_map(shards, mesh=mesh, in_specs=in_specs, out_specs=out_specs, check_vma=False)
```

time: 198 us -> 161 us (0.81)
  Pallas kernels: 69.9 us -> 43.3 us
  starting transfers between devices: 64.6 us -> 55.9 us
    pallas_call x4 -> x2, Pallas kernels: 34.3 us -> 16.6 us  [score(): pl.pallas_call(functools.partial(score_kernel, len(parts), acc_in is not...]
    ppermute x10, waiting for transfers between devices: 12 us -> 24 us  [to_xm(): return lax.ppermute(v, 'img', img_perm(0, -1, 0))]
    ppermute x8 -> x7, waiting for transfers between devices: 16.8 us -> 8.56 us  [to_z(): return lax.ppermute(v, 'img', img_perm(1, 0, 0))]
    ppermute x8 -> x7, starting transfers between devices: 17.3 us -> 11.1 us  [to_z(): return lax.ppermute(v, 'img', img_perm(1, 0, 0))]
    pallas_call x1 -> x2, Pallas kernels: 19.2 us -> 13.5 us  [weigh(): pl.pallas_call(weigh_kernel, grid_spec=pltpu.PrefetchScalarGridSpec(num_s...]
    ppermute x7 -> x4, starting transfers between devices: 10 us -> 5.86 us  [the longest x3 5.05 us: shards(): lax.ppermute(stat, 'ori', ori_perm(0, y))]
    ppermute x6, waiting for transfers between devices: 10.2 us -> 6.48 us  [to_core(): return lax.ppermute(v, 'img', img_perm(0, 0, 1))]
    pallas_call x2 -> x3, Pallas kernels: 14.1 us -> 11 us  [the longest x2 10.2 us: back(): pl.pallas_call(functools.partial(back_kernel, n_parts, nb, wide, tail), g...]
  transfers between devices with their start and end apart: 41 -> 37, of which waited for: 15 -> 17; matrix products, arithmetic and copies ran while one was open for 3% -> 4% of each run, Pallas kernels for 22% -> 18%
where the time goes in v2:
time: 161 us
  starting transfers between devices  55.9 us (35%)
  waiting for transfers between devices  50.4 us (31%)
  Pallas kernels  43.3 us (27%)
  other arithmetic  3.89 us (2%)
  local copies, waits for them, and re-layouts  3.61 us (2%)
  matrix products  2.39 us (1%)
    ppermute x10, waiting for transfers between devices, to_xm(): return lax.ppermute(v, 'img', img_perm(0, -1, 0))  24 us
    ppermute x10, starting transfers between devices, to_xm(): return lax.ppermute(v, 'img', img_perm(0, -1, 0))  22.6 us
    pallas_call x2, Pallas kernels, score(): pl.pallas_call(functools.partial(score_kernel, len(parts), acc_in is not...  16.6 us
    ppermute x6, starting transfers between devices, to_core(): return lax.ppermute(v, 'img', img_perm(0, 0, 1))  14.5 us
    pallas_call x2, Pallas kernels, weigh(): pl.pallas_call(weigh_kernel, grid_spec=pltpu.PrefetchScalarGridSpec(num_s...  13.5 us
    ppermute x7, starting transfers between devices, to_z(): return lax.ppermute(v, 'img', img_perm(1, 0, 0))  11.1 us
    pallas_call x2, Pallas kernels, back(): pl.pallas_call(functools.partial(back_kernel, n_parts, nb, wide, tail), g...  10.2 us
    ppermute x7, waiting for transfers between devices, to_z(): return lax.ppermute(v, 'img', img_perm(1, 0, 0))  8.56 us
  transfers between devices with their start and end apart: 37, of which 17 were waited for; matrix products, arithmetic and copies ran while one was open for 4% of the time, Pallas kernels for 18%

profile of v2, /device:TPU:1, one launch (start us, length us, event | category | flops | bytes accessed | tf_op | source)
XLA Modules:
  0.0 160.5 jit_solution(13238263969339087761)
XLA Ops:
  0.6 1.3 broadcast_select_fusion.2
  2.0 1.5 collective-permute-start
  3.5 1.5 collective-permute-done
  5.0 0.4 maximum_select_fusion.1
  5.4 3.8 %collective-permute-start.3 = (bf16[24,16384]{1,0:T(8,128)(2,1)S(1)}, bf16[24,16384]{1,0:T(8,128)(2,1)S(1)}, u32[]{:S(2)}, u32[]{:S(2)}) collective-permute-start(bf16[24,16384]{1,0:T(8,128)(2,1)S(1)} %maximum_select_fusion.1), channel_id=1, source_target_pairs={{0,64},{8,72},{16,80},{24,88},{32,96},{40,104},{48,112},{56,120},{... | collective-permute-start | bytes 2359304 | tf_op jit(solution)/shard_map/ppermute | solution.py:47
  9.2 2.5 %collective-permute-start.1 = (bf16[24,8192]{1,0:T(8,128)(2,1)S(1)}, bf16[24,8192]{1,0:T(8,128)(2,1)S(1)}, u32[]{:S(2)}, u32[]{:S(2)}) collective-permute-start(bf16[24,8192]{1,0:T(8,128)(2,1)S(1)} %get-tuple-element.91.refs_0_), channel_id=1, source_target_pairs={{0,48},{8,56},{16,0},{24,8},{32,16},{40,24},{48,32},{56,40},{64,11... | collective-permute-start | bytes 1179656 | tf_op jit(solution)/shard_map/ppermute | solution.py:43
  11.8 0.2 collective-permute-start.2
  11.9 7.6 %collective-permute-done.1.refs_1_ = bf16[24,8192]{1,0:T(8,128)(2,1)S(1)} collective-permute-done((bf16[24,8192]{1,0:T(8,128)(2,1)S(1)}, bf16[24,8192]{1,0:T(8,128)(2,1)S(1)}, u32[]{:S(2)}, u32[]{:S(2)}) %collective-permute-start.1) | collective-permute-done | bytes 393248 | tf_op jit(solution)/shard_map/ppermute | solution.py:43
  19.6 3.4 %collective-permute-start.4 = (bf16[24,8192]{1,0:T(8,128)(2,1)S(1)}, bf16[24,8192]{1,0:T(8,128)(2,1)S(1)}, u32[]{:S(2)}, u32[]{:S(2)}) collective-permute-start(bf16[24,8192]{1,0:T(8,128)(2,1)S(1)} %collective-permute-done.1.refs_1_), channel_id=1, source_target_pairs={{0,48},{8,56},{16,0},{24,8},{32,16},{40,24},{48,32},{56,40},{64,11... | collective-permute-start | bytes 1179656 | tf_op jit(solution)/shard_map/ppermute | solution.py:43
  23.3 6.7 %weigh.3 = (bf16[8,256,1024]{2,1,0:T(8,128)(2,1)}, bf16[8,256,1024]{2,1,0:T(8,128)(2,1)}) custom-call(s32[1]{0:T(128)} %bitcast.1.core, bf16[256,32768]{1,0:T(8,128)(2,1)} %give.3, bf16[256,32768]{1,0:T(8,128)(2,1)} %give.3, bf16[256,96]{1,0:T(8,128)(2,1)S(1)} %add_convert_fusion.hot3, f32[32,16384]{1,0:T(8,128)S(1)} %copy-done, f32[1,16384]{1,0:T(1,128)S(1)} %bitcast.10), custom_call_target="tpu_custom_call" | custom-call | flops 1024 | bytes 1024 | tf_op jit(solution)/shard_map/weigh/pallas_call | solution.py:86
  29.9 1.1 collective-permute-done.2.refs_2_
  31.1 6.8 %weigh.2 = (bf16[8,256,1024]{2,1,0:T(8,128)(2,1)}, bf16[8,256,1024]{2,1,0:T(8,128)(2,1)}) custom-call(s32[1]{0:T(128)} %bitcast.1.core, bf16[256,32768]{1,0:T(8,128)(2,1)} %give.3, bf16[256,32768]{1,0:T(8,128)(2,1)} %give.3, bf16[256,96]{1,0:T(8,128)(2,1)S(1)} %add_convert_fusion.hot3, f32[32,16384]{1,0:T(8,128)S(1)} %copy-done, f32[1,16384]{1,0:T(1,128)S(1)} %bitcast.11), custom_call_target="tpu_custom_call" | custom-call | flops 1024 | bytes 1024 | tf_op jit(solution)/shard_map/weigh/pallas_call | solution.py:86
  37.9 3.4 %collective-permute-start.16 = (bf16[8,256,1024]{2,1,0:T(8,128)(2,1)}, bf16[8,256,1024]{2,1,0:T(8,128)(2,1)}, u32[]{:S(2)}, u32[]{:S(2)}) collective-permute-start(bf16[8,256,1024]{2,1,0:T(8,128)(2,1)} %get-tuple-element.48), channel_id=1, source_target_pairs={{0,8},{8,0},{16,24},{24,16},{32,40},{40,32},{48,56},{56,48},{64,72... | collective-permute-start | bytes 12582920 | tf_op jit(solution)/shard_map/ppermute | solution.py:51
  41.3 0.2 collective-permute-start.10
  41.4 0.4 collective-permute-start.11
  41.9 1.5 collective-permute-start.12
  43.4 0.8 fusion.15
  44.2 3.9 %collective-permute-done.11 = s32[256]{0:T(256)S(1)} collective-permute-done((s32[256]{0:T(256)S(1)}, s32[256]{0:T(256)S(1)}, u32[]{:S(2)}, u32[]{:S(2)}) %collective-permute-start.11) | collective-permute-done | bytes 1056 | tf_op jit(solution)/shard_map/ppermute | solution.py:51
  48.1 4.5 %collective-permute-done.12.refs_1_ = bf16[24,8192]{1,0:T(8,128)(2,1)S(1)} collective-permute-done((bf16[24,8192]{1,0:T(8,128)(2,1)S(1)}, bf16[24,8192]{1,0:T(8,128)(2,1)S(1)}, u32[]{:S(2)}, u32[]{:S(2)}) %collective-permute-start.12) | collective-permute-done | bytes 393248 | tf_op jit(solution)/shard_map/ppermute | solution.py:43
  52.5 0.7 copy-done.6
  53.3 7.8 %collective-permute-done.13.refs_5_ = bf16[24,8192]{1,0:T(8,128)(2,1)} collective-permute-done((bf16[24,8192]{1,0:T(8,128)(2,1)S(1)}, bf16[24,8192]{1,0:T(8,128)(2,1)}, u32[]{:S(2)}, u32[]{:S(2)}) %collective-permute-start.13) | collective-permute-done | bytes 393248 | tf_op jit(solution)/shard_map/ppermute | solution.py:43
  61.1 2.7 %collective-permute-start.7 = (bf16[24,8192]{1,0:T(8,128)(2,1)}, bf16[24,8192]{1,0:T(8,128)(2,1)S(1)}, u32[]{:S(2)}, u32[]{:S(2)}) collective-permute-start(bf16[24,8192]{1,0:T(8,128)(2,1)} %get-tuple-element.39.refs_3_), channel_id=1, source_target_pairs={{0,48},{8,56},{16,0},{24,8},{32,16},{40,24},{48,32},{56,40},{64,11... | collective-permute-start | bytes 1179656 | tf_op jit(solution)/shard_map/ppermute | solution.py:43
  63.8 0.6 collective-permute-done.15.refs_7_
  64.4 0.8 table.1.refs_10_
  65.5 8.6 %score.2.refs_12_ = f32[192,512]{1,0:T(8,128)S(1)} custom-call(bf16[24,8192]{1,0:T(8,128)(2,1)S(1)} %get-tuple-element.90.refs_0_, bf16[24,8192]{1,0:T(8,128)(2,1)S(1)} %copy-done.7, bf16[24,8192]{1,0:T(8,128)(2,1)S(1)} %copy-done.5, bf16[24,8192]{1,0:T(8,128)(2,1)S(1)} %get-tuple-element.44.refs_3_, bf16[24,8192]{1,0:T(8,128)(2,1)} %collective-permute-done.6.refs_4_, ...), custom_call_target="tpu_custom_call" | custom-call | flops 1024 | bytes 1024 | tf_op jit(solution)/shard_map/score/pallas_call | solution.py:200
  74.2 0.5 collective-permute-done.8.refs_6_
  74.7 8.0 %score.3.mine = f32[192,512]{1,0:T(8,128)S(1)} custom-call(bf16[24,8192]{1,0:T(8,128)(2,1)S(1)} %get-tuple-element.91.refs_0_, bf16[24,8192]{1,0:T(8,128)(2,1)S(1)} %copy-done.9, bf16[24,8192]{1,0:T(8,128)(2,1)S(1)} %copy-done.11, bf16[24,8192]{1,0:T(8,128)(2,1)S(1)} %copy-done.2, bf16[24,8192]{1,0:T(8,128)(2,1)S(1)} %copy-done.13, ...), custom_call_target="tpu_custom_call" | custom-call | flops 1024 | bytes 1024 | tf_op jit(solution)/shard_map/score/pallas_call | solution.py:200
  82.7 3.0 %collective-permute-start.17 = (f32[192,512]{1,0:T(8,128)S(1)}, f32[192,512]{1,0:T(8,128)S(1)}, u32[]{:S(2)}, u32[]{:S(2)}) collective-permute-start(f32[192,512]{1,0:T(8,128)S(1)} %score.3.mine), channel_id=1, source_target_pairs={{0,8},{8,0},{16,24},{24,16},{32,40},{40,32},{48,56},{56,48},{64,72... | collective-permute-start | bytes 1179656 | tf_op jit(solution)/shard_map/ppermute | solution.py:51
  86.0 1.1 collective-permute-done.17.recv
  87.1 0.1 stat.1
  87.2 0.8 collective-permute-start.18
  88.0 1.7 %collective-permute-done.18.refs_1_ = f32[2,512]{1,0:T(2,128)S(1)} collective-permute-done((f32[2,512]{1,0:T(2,128)S(1)}, f32[2,512]{1,0:T(2,128)S(1)}, u32[]{:S(2)}, u32[]{:S(2)}) %collective-permute-start.18) | collective-permute-done | bytes 4128 | tf_op jit(solution)/shard_map/ppermute | solution.py:421
  89.8 1.4 collective-permute-start.19
  91.2 2.6 %collective-permute-start.20 = (f32[2,512]{1,0:T(2,128)S(1)}, f32[2,512]{1,0:T(2,128)S(1)}, u32[]{:S(2)}, u32[]{:S(2)}) collective-permute-start(f32[2,512]{1,0:T(2,128)S(1)} %merge.1.refs_3_), channel_id=1, source_target_pairs={{0,2},{1,3},{2,0},{3,1},{4,6},{5,7},{6,4},{7,5},{8,10},{9,11},{10,... | collective-permute-start | bytes 12296 | tf_op jit(solution)/shard_map/ppermute | solution.py:423
  93.8 1.1 collective-permute-start.21
  95.1 1.1 collective-permute-done.21.refs_6_
  96.2 0.3 chance.1
  96.6 5.1 %back.2 = (bf16[24,8320]{1,0:T(8,128)(2,1)S(1)}, bf16[24,8320]{1,0:T(8,128)(2,1)S(1)}, bf16[24,8320]{1,0:T(8,128)(2,1)S(1)}, bf16[24,8320]{1,0:T(8,128)(2,1)S(1)...) custom-call(bf16[192,512]{1,0:T(8,128)(2,1)S(1)} %get-tuple-element., ...), custom_call_target="tpu_custom_call" | custom-call | flops 1024 | bytes 1024 | tf_op jit(solution)/shard_map/back/pallas_call | solution.py:296
  101.7 2.2 %collective-permute-start.22 = (bf16[24,8320]{1,0:T(8,128)(2,1)S(1)}, bf16[24,8320]{1,0:T(8,128)(2,1)S(1)}, u32[]{:S(2)}, u32[]{:S(2)}) collective-permute-start(bf16[24,8320]{1,0:T(8,128)(2,1)S(1)} %get-tuple-element.57), channel_id=1, source_target_pairs={{0,64},{8,72},{16,80},{24,88},{32,96},{40,104},{48,112},{56,120},{... | collective-permute-start | bytes 1198088 | tf_op jit(solution)/shard_map/ppermute | solution.py:47
  103.9 2.7 %collective-permute-start.25 = (bf16[24,8320]{1,0:T(8,128)(2,1)S(1)}, bf16[24,8320]{1,0:T(8,128)(2,1)S(1)}, u32[]{:S(2)}, u32[]{:S(2)}) collective-permute-start(bf16[24,8320]{1,0:T(8,128)(2,1)S(1)} %get-tuple-element.62), channel_id=1, source_target_pairs={{0,48},{8,56},{16,0},{24,8},{32,16},{40,24},{48,32},{56,40},{64,11... | collective-permute-start | bytes 1198088 | tf_op jit(solution)/shard_map/ppermute | solution.py:43
  106.6 5.1 %back.3 = (bf16[24,8192]{1,0:T(8,128)(2,1)S(1)}, bf16[24,8192]{1,0:T(8,128)(2,1)S(1)}, bf16[24,8192]{1,0:T(8,128)(2,1)S(1)}, bf16[24,8192]{1,0:T(8,128)(2,1)S(1)...) custom-call(bf16[192,512]{1,0:T(8,128)(2,1)S(1)} %get-tuple-element., ...), custom_call_target="tpu_custom_call" | custom-call | flops 1024 | bytes 1024 | tf_op jit(solution)/shard_map/back/pallas_call | solution.py:296
  111.7 0.9 collective-permute-start.30
  112.6 2.7 %collective-permute-start.33 = (bf16[24,8192]{1,0:T(8,128)(2,1)S(1)}, bf16[24,8192]{1,0:T(8,128)(2,1)S(1)}, u32[]{:S(2)}, u32[]{:S(2)}) collective-permute-start(bf16[24,8192]{1,0:T(8,128)(2,1)S(1)} %get-tuple-element.72), channel_id=1, source_target_pairs={{0,48},{8,56},{16,0},{24,8},{32,16},{40,24},{48,32},{56,40},{64,11... | collective-permute-start | bytes 1179656 | tf_op jit(solution)/shard_map/ppermute | solution.py:43
  115.3 0.2 add.49
  115.6 1.5 collective-permute-start.23
  117.1 2.8 %collective-permute-done.30.refs_1_ = bf16[24,8192]{1,0:T(8,128)(2,1)S(1)} collective-permute-done((bf16[24,8192]{1,0:T(8,128)(2,1)S(1)}, bf16[24,8192]{1,0:T(8,128)(2,1)S(1)}, u32[]{:S(2)}, u32[]{:S(2)}) %collective-permute-start.30) | collective-permute-done | bytes 393248 | tf_op jit(solution)/shard_map/ppermute | solution.py:47
  120.1 3.3 %collective-permute-start.34 = (bf16[24,8192]{1,0:T(8,128)(2,1)S(1)}, bf16[24,8192]{1,0:T(8,128)(2,1)S(1)}, u32[]{:S(2)}, u32[]{:S(2)}) collective-permute-start(bf16[24,8192]{1,0:T(8,128)(2,1)S(1)} %get-tuple-element.73), channel_id=1, source_target_pairs={{0,48},{8,56},{16,0},{24,8},{32,16},{40,24},{48,32},{56,40},{64,11... | collective-permute-start | bytes 1179656 | tf_op jit(solution)/shard_map/ppermute | solution.py:43
  123.4 0.3 add.51
  123.7 2.0 %collective-permute-start.29 = (bf16[24,8320]{1,0:T(8,128)(2,1)S(1)}, bf16[24,8320]{1,0:T(8,128)(2,1)S(1)}, u32[]{:S(2)}, u32[]{:S(2)}) collective-permute-start(bf16[24,8320]{1,0:T(8,128)(2,1)S(1)} %add.51), channel_id=1, source_target_pairs={{0,64},{8,72},{16,80},{24,88},{32,96},{40,104},{48,112},{56,120},{... | collective-permute-start | bytes 1198088 | tf_op jit(solution)/shard_map/ppermute | solution.py:47
  125.8 2.1 %collective-permute-done.26.refs_1_ = bf16[24,8320]{1,0:T(8,128)(2,1)S(1)} collective-permute-done((bf16[24,8320]{1,0:T(8,128)(2,1)S(1)}, bf16[24,8320]{1,0:T(8,128)(2,1)S(1)}, u32[]{:S(2)}, u32[]{:S(2)}) %collective-permute-start.26) | collective-permute-done | bytes 399392 | tf_op jit(solution)/shard_map/ppermute | solution.py:43
  127.9 0.2 add.50
  128.1 3.7 %collective-permute-start.27 = (bf16[24,8320]{1,0:T(8,128)(2,1)S(1)}, bf16[24,8320]{1,0:T(8,128)(2,1)S(1)}, u32[]{:S(2)}, u32[]{:S(2)}) collective-permute-start(bf16[24,8320]{1,0:T(8,128)(2,1)S(1)} %add.50), channel_id=1, source_target_pairs={{0,48},{8,56},{16,0},{24,8},{32,16},{40,24},{48,32},{56,40},{64,11... | collective-permute-start | bytes 1198088 | tf_op jit(solution)/shard_map/ppermute | solution.py:43
  132.0 2.2 %collective-permute-start.35 = (bf16[24,8192]{1,0:T(8,128)(2,1)S(1)}, bf16[24,8192]{1,0:T(8,128)(2,1)S(1)}, u32[]{:S(2)}, u32[]{:S(2)}) collective-permute-start(bf16[24,8192]{1,0:T(8,128)(2,1)S(1)} %add.55), channel_id=1, source_target_pairs={{0,64},{8,72},{16,80},{24,88},{32,96},{40,104},{48,112},{56,120},{... | collective-permute-start | bytes 1179656 | tf_op jit(solution)/shard_map/ppermute | solution.py:47
  134.3 2.0 %collective-permute-done.34.refs_2_ = bf16[24,8192]{1,0:T(8,128)(2,1)S(1)} collective-permute-done((bf16[24,8192]{1,0:T(8,128)(2,1)S(1)}, bf16[24,8192]{1,0:T(8,128)(2,1)S(1)}, u32[]{:S(2)}, u32[]{:S(2)}) %collective-permute-start.34) | collective-permute-done | bytes 393248 | tf_op jit(solution)/shard_map/ppermute | solution.py:43
  136.3 1.2 fusion.2
  137.5 5.1 %collective-permute-done.35.refs_3_ = bf16[24,8192]{1,0:T(8,128)(2,1)S(1)} collective-permute-done((bf16[24,8192]{1,0:T(8,128)(2,1)S(1)}, bf16[24,8192]{1,0:T(8,128)(2,1)S(1)}, u32[]{:S(2)}, u32[]{:S(2)}) %collective-permute-start.35) | collective-permute-done | bytes 393248 | tf_op jit(solution)/shard_map/ppermute | solution.py:47
  142.7 6.7 %collective-permute-done.32.refs_1_ = bf16[24,8192]{1,0:T(8,128)(2,1)S(1)} collective-permute-done((bf16[24,8192]{1,0:T(8,128)(2,1)S(1)}, bf16[24,8192]{1,0:T(8,128)(2,1)S(1)}, u32[]{:S(2)}, u32[]{:S(2)}) %collective-permute-start.32) | collective-permute-done | bytes 393248 | tf_op jit(solution)/shard_map/ppermute | solution.py:39
  149.4 0.2 add.56
  149.6 0.4 add.52
  150.1 0.2 select_bitcast_fusion
  150.3 6.0 %collective-permute-start.36 = (bf16[12,16384]{1,0:T(8,128)(2,1)S(1)}, bf16[12,16384]{1,0:T(8,128)(2,1)S(1)}, u32[]{:S(2)}, u32[]{:S(2)}) collective-permute-start(bf16[12,16384]{1,0:T(8,128)(2,1)S(1)} %get-tuple-element.87), channel_id=1, source_target_pairs={{0,8},{8,0},{16,24},{24,16},{32,40},{40,32},{48,56},{56,48},{64,72... | collective-permute-start | bytes 1179656 | tf_op jit(solution)/shard_map/ppermute | solution.py:51
  156.4 1.2 convolution_bitcast_fusion
  157.6 1.7 %copy.15 = f32[1,12,16384]{2,0,1:T(1,128)} copy(f32[1,12,16384]{2,1,0:T(8,128)S(1)} %convolution_bitcast_fusion) | data formatting | bytes 1572864
  159.3 1.3 maximum_select_fusion
  (82 shorter events, 1.8 us)
Async XLA Ops:
  1.9 21.1 %copy-start.14 = (s32[256]{0:T(256)S(1)}, s32[256]{0:T(256)}, u32[]{:S(2)}) copy-start(s32[256]{0:T(256)} %param.7) | copy-start | bytes 3076
  1.9 21.3 %copy-start = (f32[32,16384]{1,0:T(8,128)S(1)}, f32[32,16384]{1,0:T(8,128)}, u32[]{:S(2)}) copy-start(f32[32,16384]{1,0:T(8,128)} %contrast.5) | copy-start | bytes 6291460
  1.9 21.3 %copy-start.3 = (f32[16384]{0:T(1024)S(1)}, f32[16384]{0:T(1024)}, u32[]{:S(2)}) copy-start(f32[16384]{0:T(1024)} %param.9) | copy-start | bytes 196612
  2.0 3.0 %collective-permute-start = (bf16[12,16384]{1,0:T(8,128)(2,1)S(1)}, bf16[12,16384]{1,0:T(8,128)(2,1)S(1)}, u32[]{:S(2)}, u32[]{:S(2)}) collective-permute-start(bf16[12,16384]{1,0:T(8,128)(2,1)S(1)} %get-tuple-element.85), channel_id=1, source_target_pairs={{0,8},{8,0},{16,24},{24,16},{32,40},{40,32},{48,56},{56,48},{64,72... | collective-permute-start | bytes 1179656 | tf_op jit(solution)/shard_map/ppermute | solution.py:51
  5.4 32.5 %collective-permute-start.3 = (bf16[24,16384]{1,0:T(8,128)(2,1)S(1)}, bf16[24,16384]{1,0:T(8,128)(2,1)S(1)}, u32[]{:S(2)}, u32[]{:S(2)}) collective-permute-start(bf16[24,16384]{1,0:T(8,128)(2,1)S(1)} %maximum_select_fusion.1), channel_id=1, source_target_pairs={{0,64},{8,72},{16,80},{24,88},{32,96},{40,104},{48,112},{56,120},{... | collective-permute-start | bytes 2359304 | tf_op jit(solution)/shard_map/ppermute | solution.py:47
  9.2 10.4 %collective-permute-start.1 = (bf16[24,8192]{1,0:T(8,128)(2,1)S(1)}, bf16[24,8192]{1,0:T(8,128)(2,1)S(1)}, u32[]{:S(2)}, u32[]{:S(2)}) collective-permute-start(bf16[24,8192]{1,0:T(8,128)(2,1)S(1)} %get-tuple-element.91.refs_0_), channel_id=1, source_target_pairs={{0,48},{8,56},{16,0},{24,8},{32,16},{40,24},{48,32},{56,40},{64,11... | collective-permute-start | bytes 1179656 | tf_op jit(solution)/shard_map/ppermute | solution.py:43
  11.7 11.2 %collective-permute-start.5 = (bf16[24,8192]{1,0:T(8,128)(2,1)S(1)}, bf16[24,8192]{1,0:T(8,128)(2,1)S(1)}, u32[]{:S(2)}, u32[]{:S(2)}) collective-permute-start(bf16[24,8192]{1,0:T(8,128)(2,1)S(1)} %get-tuple-element.90.refs_0_), channel_id=1, source_target_pairs={{0,16},{8,24},{16,32},{24,40},{32,48},{40,56},{48,0},{56,8},{64,80... | collective-permute-start | bytes 1179656 | tf_op jit(solution)/shard_map/ppermute | solution.py:39
  11.8 19.3 %collective-permute-start.2 = (bf16[24,8192]{1,0:T(8,128)(2,1)S(1)}, bf16[24,8192]{1,0:T(8,128)(2,1)S(1)}, u32[]{:S(2)}, u32[]{:S(2)}) collective-permute-start(bf16[24,8192]{1,0:T(8,128)(2,1)S(1)} %get-tuple-element.91.refs_0_), channel_id=1, source_target_pairs={{0,16},{8,24},{16,32},{24,40},{32,48},{40,56},{48,0},{56,8},{64,80... | collective-permute-start | bytes 1179656 | tf_op jit(solution)/shard_map/ppermute | solution.py:39
  19.6 10.4 %copy-start.8 = (bf16[24,8192]{1,0:T(8,128)(2,1)}, bf16[24,8192]{1,0:T(8,128)(2,1)S(1)}, u32[]{:S(2)}) copy-start(bf16[24,8192]{1,0:T(8,128)(2,1)S(1)} %collective-permute-done.1.refs_1_) | copy-start | bytes 1179652
  19.6 21.7 %collective-permute-start.4 = (bf16[24,8192]{1,0:T(8,128)(2,1)S(1)}, bf16[24,8192]{1,0:T(8,128)(2,1)S(1)}, u32[]{:S(2)}, u32[]{:S(2)}) collective-permute-start(bf16[24,8192]{1,0:T(8,128)(2,1)S(1)} %collective-permute-done.1.refs_1_), channel_id=1, source_target_pairs={{0,48},{8,56},{16,0},{24,8},{32,16},{40,24},{48,32},{56,40},{64,11... | collective-permute-start | bytes 1179656 | tf_op jit(solution)/shard_map/ppermute | solution.py:43
  23.0 6.9 %copy-start.4 = (bf16[24,8192]{1,0:T(8,128)(2,1)}, bf16[24,8192]{1,0:T(8,128)(2,1)S(1)}, u32[]{:S(2)}) copy-start(bf16[24,8192]{1,0:T(8,128)(2,1)S(1)} %collective-permute-done.5.refs_2_) | copy-start | bytes 1179652
  23.0 18.3 %collective-permute-start.6 = (bf16[24,8192]{1,0:T(8,128)(2,1)S(1)}, bf16[24,8192]{1,0:T(8,128)(2,1)}, u32[]{:S(2)}, u32[]{:S(2)}) collective-permute-start(bf16[24,8192]{1,0:T(8,128)(2,1)S(1)} %collective-permute-done.5.refs_2_), channel_id=1, source_target_pairs={{0,16},{8,24},{16,32},{24,40},{32,48},{40,56},{48,0},{56,8},{64,80... | collective-permute-start | bytes 1179656 | tf_op jit(solution)/shard_map/ppermute | solution.py:39
  31.1 6.8 %copy-start.10 = (bf16[24,8192]{1,0:T(8,128)(2,1)}, bf16[24,8192]{1,0:T(8,128)(2,1)S(1)}, u32[]{:S(2)}) copy-start(bf16[24,8192]{1,0:T(8,128)(2,1)S(1)} %collective-permute-done.2.refs_2_) | copy-start | bytes 1179652
  37.9 27.5 %collective-permute-start.16 = (bf16[8,256,1024]{2,1,0:T(8,128)(2,1)}, bf16[8,256,1024]{2,1,0:T(8,128)(2,1)}, u32[]{:S(2)}, u32[]{:S(2)}) collective-permute-start(bf16[8,256,1024]{2,1,0:T(8,128)(2,1)} %get-tuple-element.48), channel_id=1, source_target_pairs={{0,8},{8,0},{16,24},{24,16},{32,40},{40,32},{48,56},{56,48},{64,72... | collective-permute-start | bytes 12582920 | tf_op jit(solution)/shard_map/ppermute | solution.py:51
  41.3 11.3 %copy-start.12 = (bf16[24,8192]{1,0:T(8,128)(2,1)}, bf16[24,8192]{1,0:T(8,128)(2,1)S(1)}, u32[]{:S(2)}) copy-start(bf16[24,8192]{1,0:T(8,128)(2,1)S(1)} %collective-permute-done.4.refs_4_) | copy-start | bytes 1179652
  41.3 33.4 %collective-permute-start.10 = (bf16[8,256,1024]{2,1,0:T(8,128)(2,1)}, bf16[8,256,1024]{2,1,0:T(8,128)(2,1)}, u32[]{:S(2)}, u32[]{:S(2)}) collective-permute-start(bf16[8,256,1024]{2,1,0:T(8,128)(2,1)} %get-tuple-element.43), channel_id=1, source_target_pairs={{0,8},{8,0},{16,24},{24,16},{32,40},{40,32},{48,56},{56,48},{64,72... | collective-permute-start | bytes 12582920 | tf_op jit(solution)/shard_map/ppermute | solution.py:51
  41.4 6.6 %collective-permute-start.11 = (s32[256]{0:T(256)S(1)}, s32[256]{0:T(256)S(1)}, u32[]{:S(2)}, u32[]{:S(2)}) collective-permute-start(s32[256]{0:T(256)S(1)} %copy-done.14), channel_id=1, source_target_pairs={{0,8},{8,0},{16,24},{24,16},{32,40},{40,32},{48,56},{56,48},{64,72... | collective-permute-start | bytes 3080 | tf_op jit(solution)/shard_map/ppermute | solution.py:51
  41.9 10.7 %collective-permute-start.12 = (bf16[24,8192]{1,0:T(8,128)(2,1)S(1)}, bf16[24,8192]{1,0:T(8,128)(2,1)S(1)}, u32[]{:S(2)}, u32[]{:S(2)}) collective-permute-start(bf16[24,8192]{1,0:T(8,128)(2,1)S(1)} %get-tuple-element.90.refs_0_), channel_id=1, source_target_pairs={{0,48},{8,56},{16,0},{24,8},{32,16},{40,24},{48,32},{56,40},{64,11... | collective-permute-start | bytes 1179656 | tf_op jit(solution)/shard_map/ppermute | solution.py:43
  44.2 16.9 %collective-permute-start.13 = (bf16[24,8192]{1,0:T(8,128)(2,1)S(1)}, bf16[24,8192]{1,0:T(8,128)(2,1)}, u32[]{:S(2)}, u32[]{:S(2)}) collective-permute-start(bf16[24,8192]{1,0:T(8,128)(2,1)S(1)} %get-tuple-element.44.refs_3_), channel_id=1, source_target_pairs={{0,48},{8,56},{16,0},{24,8},{32,16},{40,24},{48,32},{56,40},{64,11... | collective-permute-start | bytes 1179656 | tf_op jit(solution)/shard_map/ppermute | solution.py:43
  48.0 15.7 %collective-permute-start.14 = (bf16[24,8192]{1,0:T(8,128)(2,1)S(1)}, bf16[24,8192]{1,0:T(8,128)(2,1)}, u32[]{:S(2)}, u32[]{:S(2)}) collective-permute-start(bf16[24,8192]{1,0:T(8,128)(2,1)S(1)} %get-tuple-element.44.refs_3_), channel_id=1, source_target_pairs={{0,16},{8,24},{16,32},{24,40},{32,48},{40,56},{48,0},{56,8},{64,80... | collective-permute-start | bytes 1179656 | tf_op jit(solution)/shard_map/ppermute | solution.py:39
  52.5 0.7 copy-start.6
  53.3 11.1 %collective-permute-start.15 = (bf16[24,8192]{1,0:T(8,128)(2,1)}, bf16[24,8192]{1,0:T(8,128)(2,1)}, u32[]{:S(2)}, u32[]{:S(2)}) collective-permute-start(bf16[24,8192]{1,0:T(8,128)(2,1)} %collective-permute-done.6.refs_4_), channel_id=1, source_target_pairs={{0,64},{8,72},{16,80},{24,88},{32,96},{40,104},{48,112},{56,120},{... | collective-permute-start | bytes 1179656 | tf_op jit(solution)/shard_map/ppermute | solution.py:47
  61.1 13.1 %collective-permute-start.7 = (bf16[24,8192]{1,0:T(8,128)(2,1)}, bf16[24,8192]{1,0:T(8,128)(2,1)S(1)}, u32[]{:S(2)}, u32[]{:S(2)}) collective-permute-start(bf16[24,8192]{1,0:T(8,128)(2,1)} %get-tuple-element.39.refs_3_), channel_id=1, source_target_pairs={{0,48},{8,56},{16,0},{24,8},{32,16},{40,24},{48,32},{56,40},{64,11... | collective-permute-start | bytes 1179656 | tf_op jit(solution)/shard_map/ppermute | solution.py:43
  63.8 10.9 %collective-permute-start.8 = (bf16[24,8192]{1,0:T(8,128)(2,1)}, bf16[24,8192]{1,0:T(8,128)(2,1)S(1)}, u32[]{:S(2)}, u32[]{:S(2)}) collective-permute-start(bf16[24,8192]{1,0:T(8,128)(2,1)} %get-tuple-element.39.refs_3_), channel_id=1, source_target_pairs={{0,16},{8,24},{16,32},{24,40},{32,48},{40,56},{48,0},{56,8},{64,80... | collective-permute-start | bytes 1179656 | tf_op jit(solution)/shard_map/ppermute | solution.py:39
  64.4 10.3 %collective-permute-start.9 = (bf16[24,8192]{1,0:T(8,128)(2,1)}, bf16[24,8192]{1,0:T(8,128)(2,1)S(1)}, u32[]{:S(2)}, u32[]{:S(2)}) collective-permute-start(bf16[24,8192]{1,0:T(8,128)(2,1)} %copy-done.12), channel_id=1, source_target_pairs={{0,64},{8,72},{16,80},{24,88},{32,96},{40,104},{48,112},{56,120},{... | collective-permute-start | bytes 1179656 | tf_op jit(solution)/shard_map/ppermute | solution.py:47
  64.4 1.0 copy-start.5
  64.4 1.1 copy-start.7
  65.2 8.9 %copy-start.1 = (bf16[64,16384]{1,0:T(8,128)(2,1)}, bf16[64,16384]{1,0:T(8,128)(2,1)S(1)}, u32[]{:S(2)}) copy-start(bf16[64,16384]{1,0:T(8,128)(2,1)S(1)} %table.1.refs_10_) | copy-start | bytes 6291460
  65.5 9.2 %copy-start.2 = (bf16[24,8192]{1,0:T(8,128)(2,1)S(1)}, bf16[24,8192]{1,0:T(8,128)(2,1)}, u32[]{:S(2)}) copy-start(bf16[24,8192]{1,0:T(8,128)(2,1)} %get-tuple-element.39.refs_3_) | copy-start | bytes 1179652
  65.5 9.2 %copy-start.9 = (bf16[24,8192]{1,0:T(8,128)(2,1)S(1)}, bf16[24,8192]{1,0:T(8,128)(2,1)}, u32[]{:S(2)}) copy-start(bf16[24,8192]{1,0:T(8,128)(2,1)} %copy-done.8) | copy-start | bytes 1179652
  65.5 9.2 %copy-start.11 = (bf16[24,8192]{1,0:T(8,128)(2,1)S(1)}, bf16[24,8192]{1,0:T(8,128)(2,1)}, u32[]{:S(2)}) copy-start(bf16[24,8192]{1,0:T(8,128)(2,1)} %copy-done.10) | copy-start | bytes 1179652
  65.5 9.2 %copy-start.13 = (bf16[24,8192]{1,0:T(8,128)(2,1)S(1)}, bf16[24,8192]{1,0:T(8,128)(2,1)}, u32[]{:S(2)}) copy-start(bf16[24,8192]{1,0:T(8,128)(2,1)} %copy-done.12) | copy-start | bytes 1179652
  74.7 11.0 %copy-start.15 = (s32[512]{0:T(512)S(1)}, s32[512]{0:T(512)}, u32[]{:S(2)}) copy-start(s32[512]{0:T(512)} %param.11) | copy-start | bytes 6148
  82.7 4.4 %collective-permute-start.17 = (f32[192,512]{1,0:T(8,128)S(1)}, f32[192,512]{1,0:T(8,128)S(1)}, u32[]{:S(2)}, u32[]{:S(2)}) collective-permute-start(f32[192,512]{1,0:T(8,128)S(1)} %score.3.mine), channel_id=1, source_target_pairs={{0,8},{8,0},{16,24},{24,16},{32,40},{40,32},{48,56},{56,48},{64,72... | collective-permute-start | bytes 1179656 | tf_op jit(solution)/shard_map/ppermute | solution.py:51
  87.2 2.5 %collective-permute-start.18 = (f32[2,512]{1,0:T(2,128)S(1)}, f32[2,512]{1,0:T(2,128)S(1)}, u32[]{:S(2)}, u32[]{:S(2)}) collective-permute-start(f32[2,512]{1,0:T(2,128)S(1)} %get-tuple-element.50.refs_0_), channel_id=1, source_target_pairs={{0,4},{1,5},{2,6},{3,7},{4,0},{5,1},{6,2},{7,3},{8,12},{9,13},{10,... | collective-permute-start | bytes 12296 | tf_op jit(solution)/shard_map/ppermute | solution.py:421
  89.8 5.2 %collective-permute-start.19 = (f32[2,512]{1,0:T(2,128)S(1)}, f32[2,512]{1,0:T(2,128)S(1)}, u32[]{:S(2)}, u32[]{:S(2)}) collective-permute-start(f32[2,512]{1,0:T(2,128)S(1)} %merge.1.refs_3_), channel_id=1, source_target_pairs={{0,1},{1,2},{2,3},{3,0},{4,5},{5,6},{6,7},{7,4},{8,9},{9,10},{10,1... | collective-permute-start | bytes 12296 | tf_op jit(solution)/shard_map/ppermute | solution.py:423
  91.2 4.0 %collective-permute-start.20 = (f32[2,512]{1,0:T(2,128)S(1)}, f32[2,512]{1,0:T(2,128)S(1)}, u32[]{:S(2)}, u32[]{:S(2)}) collective-permute-start(f32[2,512]{1,0:T(2,128)S(1)} %merge.1.refs_3_), channel_id=1, source_target_pairs={{0,2},{1,3},{2,0},{3,1},{4,6},{5,7},{6,4},{7,5},{8,10},{9,11},{10,... | collective-permute-start | bytes 12296 | tf_op jit(solution)/shard_map/ppermute | solution.py:423
  93.8 2.5 %collective-permute-start.21 = (f32[2,512]{1,0:T(2,128)S(1)}, f32[2,512]{1,0:T(2,128)S(1)}, u32[]{:S(2)}, u32[]{:S(2)}) collective-permute-start(f32[2,512]{1,0:T(2,128)S(1)} %merge.1.refs_3_), channel_id=1, source_target_pairs={{0,3},{1,0},{2,1},{3,2},{4,7},{5,4},{6,5},{7,6},{8,11},{9,8},{10,9... | collective-permute-start | bytes 12296 | tf_op jit(solution)/shard_map/ppermute | solution.py:423
  101.7 13.6 %collective-permute-start.22 = (bf16[24,8320]{1,0:T(8,128)(2,1)S(1)}, bf16[24,8320]{1,0:T(8,128)(2,1)S(1)}, u32[]{:S(2)}, u32[]{:S(2)}) collective-permute-start(bf16[24,8320]{1,0:T(8,128)(2,1)S(1)} %get-tuple-element.57), channel_id=1, source_target_pairs={{0,64},{8,72},{16,80},{24,88},{32,96},{40,104},{48,112},{56,120},{... | collective-permute-start | bytes 1198088 | tf_op jit(solution)/shard_map/ppermute | solution.py:47
  103.9 11.6 %collective-permute-start.25 = (bf16[24,8320]{1,0:T(8,128)(2,1)S(1)}, bf16[24,8320]{1,0:T(8,128)(2,1)S(1)}, u32[]{:S(2)}, u32[]{:S(2)}) collective-permute-start(bf16[24,8320]{1,0:T(8,128)(2,1)S(1)} %get-tuple-element.62), channel_id=1, source_target_pairs={{0,48},{8,56},{16,0},{24,8},{32,16},{40,24},{48,32},{56,40},{64,11... | collective-permute-start | bytes 1198088 | tf_op jit(solution)/shard_map/ppermute | solution.py:43
  106.6 13.4 %collective-permute-start.28 = (bf16[24,8320]{1,0:T(8,128)(2,1)S(1)}, bf16[24,8320]{1,0:T(8,128)(2,1)S(1)}, u32[]{:S(2)}, u32[]{:S(2)}) collective-permute-start(bf16[24,8320]{1,0:T(8,128)(2,1)S(1)} %get-tuple-element.65), channel_id=1, source_target_pairs={{0,16},{8,24},{16,32},{24,40},{32,48},{40,56},{48,0},{56,8},{64,80... | collective-permute-start | bytes 1198088 | tf_op jit(solution)/shard_map/ppermute | solution.py:39
  111.7 8.2 %collective-permute-start.30 = (bf16[24,8192]{1,0:T(8,128)(2,1)S(1)}, bf16[24,8192]{1,0:T(8,128)(2,1)S(1)}, u32[]{:S(2)}, u32[]{:S(2)}) collective-permute-start(bf16[24,8192]{1,0:T(8,128)(2,1)S(1)} %get-tuple-element.69), channel_id=1, source_target_pairs={{0,64},{8,72},{16,80},{24,88},{32,96},{40,104},{48,112},{56,120},{... | collective-permute-start | bytes 1179656 | tf_op jit(solution)/shard_map/ppermute | solution.py:47
  112.6 7.5 %collective-permute-start.33 = (bf16[24,8192]{1,0:T(8,128)(2,1)S(1)}, bf16[24,8192]{1,0:T(8,128)(2,1)S(1)}, u32[]{:S(2)}, u32[]{:S(2)}) collective-permute-start(bf16[24,8192]{1,0:T(8,128)(2,1)S(1)} %get-tuple-element.72), channel_id=1, source_target_pairs={{0,48},{8,56},{16,0},{24,8},{32,16},{40,24},{48,32},{56,40},{64,11... | collective-permute-start | bytes 1179656 | tf_op jit(solution)/shard_map/ppermute | solution.py:43
  115.5 12.4 %collective-permute-start.26 = (bf16[24,8320]{1,0:T(8,128)(2,1)S(1)}, bf16[24,8320]{1,0:T(8,128)(2,1)S(1)}, u32[]{:S(2)}, u32[]{:S(2)}) collective-permute-start(bf16[24,8320]{1,0:T(8,128)(2,1)S(1)} %add.49), channel_id=1, source_target_pairs={{0,48},{8,56},{16,0},{24,8},{32,16},{40,24},{48,32},{56,40},{64,11... | collective-permute-start | bytes 1198088 | tf_op jit(solution)/shard_map/ppermute | solution.py:43
  115.6 10.2 %collective-permute-start.23 = (bf16[24,8192]{1,0:T(8,128)(2,1)S(1)}, bf16[24,8192]{1,0:T(8,128)(2,1)S(1)}, u32[]{:S(2)}, u32[]{:S(2)}) collective-permute-start(bf16[24,8192]{1,0:T(8,128)(2,1)S(1)} %get-tuple-element.58), channel_id=1, source_target_pairs={{0,16},{8,24},{16,32},{24,40},{32,48},{40,56},{48,0},{56,8},{64,80... | collective-permute-start | bytes 1179656 | tf_op jit(solution)/shard_map/ppermute | solution.py:39
  120.0 12.0 %collective-permute-start.31 = (bf16[24,8192]{1,0:T(8,128)(2,1)S(1)}, bf16[24,8192]{1,0:T(8,128)(2,1)S(1)}, u32[]{:S(2)}, u32[]{:S(2)}) collective-permute-start(bf16[24,8192]{1,0:T(8,128)(2,1)S(1)} %add.53), channel_id=1, source_target_pairs={{0,16},{8,24},{16,32},{24,40},{32,48},{40,56},{48,0},{56,8},{64,80... | collective-permute-start | bytes 1179656 | tf_op jit(solution)/shard_map/ppermute | solution.py:39
  120.1 16.3 %collective-permute-start.34 = (bf16[24,8192]{1,0:T(8,128)(2,1)S(1)}, bf16[24,8192]{1,0:T(8,128)(2,1)S(1)}, u32[]{:S(2)}, u32[]{:S(2)}) collective-permute-start(bf16[24,8192]{1,0:T(8,128)(2,1)S(1)} %get-tuple-element.73), channel_id=1, source_target_pairs={{0,48},{8,56},{16,0},{24,8},{32,16},{40,24},{48,32},{56,40},{64,11... | collective-permute-start | bytes 1179656 | tf_op jit(solution)/shard_map/ppermute | solution.py:43
  123.7 25.8 %collective-permute-start.29 = (bf16[24,8320]{1,0:T(8,128)(2,1)S(1)}, bf16[24,8320]{1,0:T(8,128)(2,1)S(1)}, u32[]{:S(2)}, u32[]{:S(2)}) collective-permute-start(bf16[24,8320]{1,0:T(8,128)(2,1)S(1)} %add.51), channel_id=1, source_target_pairs={{0,64},{8,72},{16,80},{24,88},{32,96},{40,104},{48,112},{56,120},{... | collective-permute-start | bytes 1198088 | tf_op jit(solution)/shard_map/ppermute | solution.py:47
  125.8 23.8 %collective-permute-start.24 = (bf16[24,8320]{1,0:T(8,128)(2,1)S(1)}, bf16[24,8320]{1,0:T(8,128)(2,1)S(1)}, u32[]{:S(2)}, u32[]{:S(2)}) collective-permute-start(bf16[24,8320]{1,0:T(8,128)(2,1)S(1)} %get-tuple-element.59), channel_id=1, source_target_pairs={{0,16},{8,24},{16,32},{24,40},{32,48},{40,56},{48,0},{56,8},{64,80... | collective-permute-start | bytes 1198088 | tf_op jit(solution)/shard_map/ppermute | solution.py:39
  128.1 21.5 %collective-permute-start.27 = (bf16[24,8320]{1,0:T(8,128)(2,1)S(1)}, bf16[24,8320]{1,0:T(8,128)(2,1)S(1)}, u32[]{:S(2)}, u32[]{:S(2)}) collective-permute-start(bf16[24,8320]{1,0:T(8,128)(2,1)S(1)} %add.50), channel_id=1, source_target_pairs={{0,48},{8,56},{16,0},{24,8},{32,16},{40,24},{48,32},{56,40},{64,11... | collective-permute-start | bytes 1198088 | tf_op jit(solution)/shard_map/ppermute | solution.py:43
  132.0 10.7 %collective-permute-start.35 = (bf16[24,8192]{1,0:T(8,128)(2,1)S(1)}, bf16[24,8192]{1,0:T(8,128)(2,1)S(1)}, u32[]{:S(2)}, u32[]{:S(2)}) collective-permute-start(bf16[24,8192]{1,0:T(8,128)(2,1)S(1)} %add.55), channel_id=1, source_target_pairs={{0,64},{8,72},{16,80},{24,88},{32,96},{40,104},{48,112},{56,120},{... | collective-permute-start | bytes 1179656 | tf_op jit(solution)/shard_map/ppermute | solution.py:47
  136.3 13.1 %collective-permute-start.32 = (bf16[24,8192]{1,0:T(8,128)(2,1)S(1)}, bf16[24,8192]{1,0:T(8,128)(2,1)S(1)}, u32[]{:S(2)}, u32[]{:S(2)}) collective-permute-start(bf16[24,8192]{1,0:T(8,128)(2,1)S(1)} %add.54), channel_id=1, source_target_pairs={{0,16},{8,24},{16,32},{24,40},{32,48},{40,56},{48,0},{56,8},{64,80... | collective-permute-start | bytes 1179656 | tf_op jit(solution)/shard_map/ppermute | solution.py:39
  150.3 9.0 %collective-permute-start.36 = (bf16[12,16384]{1,0:T(8,128)(2,1)S(1)}, bf16[12,16384]{1,0:T(8,128)(2,1)S(1)}, u32[]{:S(2)}, u32[]{:S(2)}) collective-permute-start(bf16[12,16384]{1,0:T(8,128)(2,1)S(1)} %get-tuple-element.87), channel_id=1, source_target_pairs={{0,8},{8,0},{16,24},{24,16},{32,40},{40,32},{48,56},{56,48},{64,72... | collective-permute-start | bytes 1179656 | tf_op jit(solution)/shard_map/ppermute | solution.py:51

commit v3 on v2

--- a/solution.py
+++ b/solution.py
@@ -75,29 +75,28 @@
             out[i] = value[:, i * KB : (i + 1) * KB]
 
 
-def weigh(core, images, hot3, contrast, noise, quarter):
+def weigh(core, images, hot3, contrast, noise):
     rows, cols = images.shape
     half = cols // 2
     wide = 4
     kb = wide * KB
     nb = half // kb
     n_cls = contrast.shape[0]
-    off = quarter * nb // 2
     return pl.pallas_call(
         weigh_kernel,
         grid_spec=pltpu.PrefetchScalarGridSpec(
             num_scalar_prefetch=1,
-            grid=(nb // 2,),
+            grid=(nb,),
             in_specs=[
-                pl.BlockSpec((rows, kb), lambda j, s: (0, s[0] * nb + off + j)),
-                pl.BlockSpec((rows, kb), lambda j, s: (0, (1 - s[0]) * nb + off + j)),
+                pl.BlockSpec((rows, kb), lambda j, s: (0, s[0] * nb + j)),
+                pl.BlockSpec((rows, kb), lambda j, s: (0, (1 - s[0]) * nb + j)),
                 pl.BlockSpec(hot3.shape, lambda j, s: (0, 0)),
-                pl.BlockSpec((n_cls, kb), lambda j, s: (0, off + j)),
-                pl.BlockSpec((1, kb), lambda j, s: (0, off + j)),
+                pl.BlockSpec((n_cls, kb), lambda j, s: (0, j)),
+                pl.BlockSpec((1, kb), lambda j, s: (0, j)),
             ],
             out_specs=[pl.BlockSpec((wide, rows, KB), lambda j, s: (j, 0, 0))] * 2,
         ),
-        out_shape=[jax.ShapeDtypeStruct((half // KB // 2, rows, KB), BF16)] * 2,
+        out_shape=[jax.ShapeDtypeStruct((half // KB, rows, KB), BF16)] * 2,
         compiler_params=params(),
         cost_estimate=CHEAP,
         name="weigh",
@@ -181,15 +180,18 @@
 def score(parts, w_own, w_sib, quads, hot, quarter, acc_in):
     part_rows = parts[0].shape[0]
     rows = w_own.shape[1]
-    wide = 2
+    wide = 4
     kb = wide * KB
-    nb = w_own.shape[0] // wide
+    nb = w_own.shape[0] // wide // 2
     used = part_rows * len(parts)
     off = quarter * nb
-    in_specs = [pl.BlockSpec((part_rows, kb), lambda j: (0, j)) for _ in parts]
+    in_specs = []
+    for p in parts:
+        at = off if p.shape[1] > nb * kb else 0
+        in_specs.append(pl.BlockSpec((part_rows, kb), lambda j, at=at: (0, at + j)))
     in_specs += [
-        pl.BlockSpec((wide, rows, KB), lambda j: (j, 0, 0)),
-        pl.BlockSpec((wide, rows, KB), lambda j: (j, 0, 0)),
+        pl.BlockSpec((wide, rows, KB), lambda j: (off + j, 0, 0)),
+        pl.BlockSpec((wide, rows, KB), lambda j: (off + j, 0, 0)),
         pl.BlockSpec((quads.shape[0], kb), lambda j: (0, off + j)),
         full(hot.shape),
     ]
@@ -288,8 +290,9 @@
 
 def back(per, w_own, w_sib, tot, quarter, n_parts):
     blocks, rows, _ = w_own.shape
-    wide = 2
-    nb = blocks // wide
+    wide = 4
+    nb = blocks // wide // 2
+    off = quarter * nb
     h = per.shape[0] // n_parts
     tail = quarter == 0
     width = nb * wide * KB + (TAIL if tail else 0)
@@ -298,8 +301,8 @@
         grid=(nb,),
         in_specs=[
             full(per.shape),
-            pl.BlockSpec((wide, rows, KB), lambda j: (j, 0, 0)),
-            pl.BlockSpec((wide, rows, KB), lambda j: (j, 0, 0)),
+            pl.BlockSpec((wide, rows, KB), lambda j: (off + j, 0, 0)),
+            pl.BlockSpec((wide, rows, KB), lambda j: (off + j, 0, 0)),
             full(tot.shape),
         ],
         out_specs=[full((h, width))] * n_parts,
@@ -360,17 +363,20 @@
     low, high = mine[:, :half], mine[:, half:]
     got = to_core(jnp.where(first, high, low))
     kept = jnp.where(first, low, high)
-    shard = jnp.where(
-        first, jnp.concatenate([kept, got], axis=0), jnp.concatenate([got, kept], axis=0)
-    )
-    own_a, own_b = shard[:, :quart], shard[:, quart:]
-    xm_a, xp_a, zz = to_xp(own_a), to_xm(own_a), to_z(shard)
-    xm_b, xp_b = to_xp(own_b), to_xm(own_b)
-    zz_a, zz_b = zz[:, :quart], zz[:, quart:]
+    own_a, own_b = (
+        jnp.where(
+            first,
+            jnp.concatenate([kept[:, cols], got[:, cols]], axis=0),
+            jnp.concatenate([got[:, cols], kept[:, cols]], axis=0),
+        )
+        for cols in (slice(0, quart), slice(quart, half))
+    )
+    xm_a, xp_b, zz_a = to_xp(own_a), to_xm(own_b), to_z(own_a)
+    xm_b, xp_a = to_xp(own_b), to_xm(own_a)
     x2_a, x2_b = to_xp(xm_a), to_xm(xp_b)
+    zz_b = to_z(tie(own_b, zz_a))
     fz_a, fz_b = tie(zz_a, x2_a, x2_b), tie(zz_b, x2_a, x2_b)
     zm_a, zp_a, z2_a = to_xp(fz_a), to_xm(fz_a), to_z(x2_a)
-    zm_b, zp_b, z2_b = to_xp(fz_b), to_xm(fz_b), to_z(x2_b)
 
     sib_classes = to_core(classes)
     ids = jnp.arange(n_cls, dtype=jnp.int32)[None, :]
@@ -379,15 +385,10 @@
     hot = (both_classes[:, None] == ids).astype(F32)
     hot_wide = (both_classes[:, None] == jnp.arange(TAIL, dtype=jnp.int32)[None, :]).astype(BF16)
     hot3 = jnp.concatenate([hot_own] * 3, axis=1)
-    w_own, w_sib = [], []
-    for quarter in range(2):
-        before = (xm_b, xp_b) if quarter else (shard,)
-        after = (x2_a, x2_b) if quarter else (xm_b, xp_b, zz)
-        at = tie(core.reshape(1), *before)
-        keep, give = weigh(at, images, hot3, contrast, noise, quarter)
-        w_own.append(keep)
-        w_sib.append(to_core(tie(give, *after)))
-    quads = quad_table(contrast, noise)
+    w_own, give = weigh(tie(core.reshape(1), own_a, sib_classes), images, hot3, contrast, noise)
+    w_sib = to_core(tie(give, xm_a, xm_b, xp_a, xp_b, zz_a))
+    quads = quad_table(tie(contrast, xm_a), noise)
+    zm_b, zp_b, z2_b = to_xp(tie(fz_b, quads)), to_xm(tie(fz_b, w_sib)), to_z(tie(x2_b, z2_a))
 
     target = proj_index // h
     dz = (target // NX) ^ (chip // NX)
@@ -401,9 +402,9 @@
 
     table = (quads, hot)
     part = [own_a, xp_a, xm_a, zz_a, x2_a, zp_a, zm_a, z2_a]
-    mine = score(part, w_own[0], w_sib[0], *table, 0, None)
+    mine = score(part, w_own, w_sib, *table, 0, None)
     part = [own_b, xp_b, xm_b, zz_b, x2_b, zp_b, zm_b, z2_b]
-    mine = score(part, w_own[1], w_sib[1], *table, 1, mine)
+    mine = score(part, w_own, w_sib, *table, 1, mine)
     stat_shape = jax.ShapeDtypeStruct((2, mine.shape[1]), F32)
     scores, stat = whole(
         stat_kernel,
@@ -439,10 +440,10 @@
     )
 
     bo_a, bxp_a, bxm_a, bzz_a, bx2_a, bzp_a, bzm_a, bz2_a = back(
-        per, w_own[0], w_sib[0], tot, 0, 8
+        per, w_own, w_sib, tot, 0, 8
     )
     bo_b, bxp_b, bxm_b, bzz_b, bx2_b, bzp_b, bzm_b, bz2_b = back(
-        per, w_own[1], w_sib[1], tot, 1, 8
+        per, w_own, w_sib, tot, 1, 8
     )
     r_z2a, r_zma, r_zpa = to_z(bz2_a), to_xm(bzm_a), to_xp(bzp_a)
     r_z2b, r_zmb = to_z(bz2_b), to_xm(bzm_b)

time: 161 us -> 149 us (0.925)
  starting transfers between devices: 55.9 us -> 50.6 us
  waiting for transfers between devices: 50.4 us -> 45.8 us
  Pallas kernels: 43.3 us -> 40.8 us
    ppermute x10, waiting for transfers between devices: 24 us -> 7.98 us  [to_xm(): return lax.ppermute(v, 'img', img_perm(0, -1, 0))]
    ppermute x7 -> x8, waiting for transfers between devices: 8.56 us -> 18.2 us  [to_z(): return lax.ppermute(v, 'img', img_perm(1, 0, 0))]
    ppermute x10, starting transfers between devices: 22.6 us -> 14.2 us  [to_xm(): return lax.ppermute(v, 'img', img_perm(0, -1, 0))]
    ppermute x10, waiting for transfers between devices: 8.33 us -> 14.2 us  [to_xp(): return lax.ppermute(v, 'img', img_perm(0, 1, 0))]
    ppermute x6 -> x5, waiting for transfers between devices: 6.48 us -> 2.47 us  [to_core(): return lax.ppermute(v, 'img', img_perm(0, 0, 1))]
    ppermute x7 -> x8, starting transfers between devices: 11.1 us -> 14.8 us  [to_z(): return lax.ppermute(v, 'img', img_perm(1, 0, 0))]
    ppermute x6 -> x5, starting transfers between devices: 14.5 us -> 11.4 us  [to_core(): return lax.ppermute(v, 'img', img_perm(0, 0, 1))]
    ppermute x10, starting transfers between devices: 1.74 us -> 4.28 us  [to_xp(): return lax.ppermute(v, 'img', img_perm(0, 1, 0))]
  transfers between devices with their start and end apart: 37 -> 37, of which waited for: 17 -> 18; matrix products, arithmetic and copies ran while one was open for 4% -> 4% of each run, Pallas kernels for 18% -> 18%
where the time goes in v3:
time: 149 us
  starting transfers between devices  50.6 us (34%)
  waiting for transfers between devices  45.8 us (31%)
  Pallas kernels  40.8 us (27%)
  local copies, waits for them, and re-layouts  4.45 us (3%)
  other arithmetic  3.9 us (3%)
  matrix products  2.4 us (2%)
    ppermute x8, waiting for transfers between devices, to_z(): return lax.ppermute(v, 'img', img_perm(1, 0, 0))  18.2 us
    pallas_call x2, Pallas kernels, score(): pl.pallas_call(functools.partial(score_kernel, len(parts), acc_in is not...  15.8 us
    ppermute x8, starting transfers between devices, to_z(): return lax.ppermute(v, 'img', img_perm(1, 0, 0))  14.8 us
    ppermute x10, waiting for transfers between devices, to_xp(): return lax.ppermute(v, 'img', img_perm(0, 1, 0))  14.2 us
    ppermute x10, starting transfers between devices, to_xm(): return lax.ppermute(v, 'img', img_perm(0, -1, 0))  14.2 us
    pallas_call x1, Pallas kernels, weigh(): pl.pallas_call(weigh_kernel, grid_spec=pltpu.PrefetchScalarGridSpec(num_s...  12.9 us
    ppermute x5, starting transfers between devices, to_core(): return lax.ppermute(v, 'img', img_perm(0, 0, 1))  11.4 us
    pallas_call x2, Pallas kernels, back(): pl.pallas_call(functools.partial(back_kernel, n_parts, nb, wide, tail), g...  8.99 us
  transfers between devices with their start and end apart: 37, of which 18 were waited for; matrix products, arithmetic and copies ran while one was open for 4% of the time, Pallas kernels for 18%

profile of v3, /device:TPU:1, one launch (start us, length us, event | category | flops | bytes accessed | tf_op | source)
XLA Modules:
  0.0 148.9 jit_solution(12700223704121580814)
XLA Ops:
  0.7 1.3 broadcast_select_fusion.2
  2.0 1.5 %collective-permute-start = (bf16[12,16384]{1,0:T(8,128)(2,1)S(1)}, bf16[12,16384]{1,0:T(8,128)(2,1)S(1)}, u32[]{:S(2)}, u32[]{:S(2)}) collective-permute-start(bf16[12,16384]{1,0:T(8,128)(2,1)S(1)} %get-tuple-element.87), channel_id=1, source_target_pairs={{0,8},{8,0},{16,24},{24,16},{32,40},{40,32},{48,56},{56,48},{64,72... | collective-permute-start | bytes 1179656 | tf_op jit(solution)/shard_map/ppermute | solution.py:51
  3.6 1.4 collective-permute-done
  5.2 3.8 %collective-permute-start.3 = (bf16[24,8192]{1,0:T(8,128)(2,1)S(1)}, bf16[24,8192]{1,0:T(8,128)(2,1)S(1)}, u32[]{:S(2)}, u32[]{:S(2)}) collective-permute-start(bf16[24,8192]{1,0:T(8,128)(2,1)S(1)} %maximum_select_fusion.2.refs_0_), channel_id=1, source_target_pairs={{0,64},{8,72},{16,80},{24,88},{32,96},{40,104},{48,112},{56,120},{... | collective-permute-start | bytes 1179656 | tf_op jit(solution)/shard_map/ppermute | solution.py:47
  9.0 1.2 collective-permute-start.6
  10.2 1.5 collective-permute-start.9
  11.9 1.3 collective-permute-start.1
  13.7 12.9 %weigh.1 = (bf16[16,256,1024]{2,1,0:T(8,128)(2,1)}, bf16[16,256,1024]{2,1,0:T(8,128)(2,1)}) custom-call(s32[1]{0:T(128)} %bitcast.1.core, bf16[256,32768]{1,0:T(8,128)(2,1)} %give.1, bf16[256,32768]{1,0:T(8,128)(2,1)} %give.1, bf16[256,96]{1,0:T(8,128)(2,1)S(1)} %add_convert_fusion.hot3, f32[32,16384]{1,0:T(8,128)S(1)} %copy-done, f32[1,16384]{1,0:T(1,128)S(1)} %bitcast.10), custom_call_target="tpu_custom_call" | custom-call | flops 1024 | bytes 1024 | tf_op jit(solution)/shard_map/weigh/pallas_call | solution.py:85
  26.6 0.8 copy-done.8
  27.5 0.9 collective-permute-done.1.refs_1_
  28.3 0.3 collective-permute-done.2.refs_2_
  28.6 0.7 copy-done.6
  29.4 1.5 %collective-permute-start.10 = (bf16[16,256,1024]{2,1,0:T(8,128)(2,1)}, bf16[16,256,1024]{2,1,0:T(8,128)(2,1)}, u32[]{:S(2)}, u32[]{:S(2)}) collective-permute-start(bf16[16,256,1024]{2,1,0:T(8,128)(2,1)} %get-tuple-element.44), channel_id=1, source_target_pairs={{0,8},{8,0},{16,24},{24,16},{32,40},{40,32},{48,56},{56,48},{64,72... | collective-permute-start | bytes 25165832 | tf_op jit(solution)/shard_map/ppermute | solution.py:51
  30.9 1.2 collective-permute-start.7
  32.1 0.7 copy-done.4
  32.9 1.5 collective-permute-start.5
  34.4 8.6 %collective-permute-done.7.refs_4_ = bf16[24,8192]{1,0:T(8,128)(2,1)} collective-permute-done((bf16[24,8192]{1,0:T(8,128)(2,1)S(1)}, bf16[24,8192]{1,0:T(8,128)(2,1)}, u32[]{:S(2)}, u32[]{:S(2)}) %collective-permute-start.7) | collective-permute-done | bytes 393248 | tf_op jit(solution)/shard_map/ppermute | solution.py:39
  43.1 0.8 table.1.refs_10_
  44.1 2.0 %collective-permute-start.15 = (bf16[24,8192]{1,0:T(8,128)(2,1)S(1)}, bf16[24,8192]{1,0:T(8,128)(2,1)S(1)}, u32[]{:S(2)}, u32[]{:S(2)}) collective-permute-start(bf16[24,8192]{1,0:T(8,128)(2,1)S(1)} %copy-done.3), channel_id=1, source_target_pairs={{0,48},{8,56},{16,0},{24,8},{32,16},{40,24},{48,32},{56,40},{64,11... | collective-permute-start | bytes 1179656 | tf_op jit(solution)/shard_map/ppermute | solution.py:43
  46.1 8.6 %collective-permute-done.13.refs_7_ = bf16[24,8192]{1,0:T(8,128)(2,1)} collective-permute-done((bf16[24,8192]{1,0:T(8,128)(2,1)}, bf16[24,8192]{1,0:T(8,128)(2,1)}, u32[]{:S(2)}, u32[]{:S(2)}) %collective-permute-start.13) | collective-permute-done | bytes 393248 | tf_op jit(solution)/shard_map/ppermute | solution.py:47
  54.8 1.5 collective-permute-start.11
  56.5 7.9 %score.2.refs_12_ = f32[192,512]{1,0:T(8,128)S(1)} custom-call(bf16[24,8192]{1,0:T(8,128)(2,1)S(1)} %maximum_select_fusion.2.refs_0_, bf16[24,8192]{1,0:T(8,128)(2,1)S(1)} %copy-done.9, bf16[24,8192]{1,0:T(8,128)(2,1)S(1)} %copy-done.5, bf16[24,8192]{1,0:T(8,128)(2,1)S(1)} %copy-done.3, bf16[24,8192]{1,0:T(8,128)(2,1)} %collective-permute-done.7.refs_4_, ...), custom_call_target="tpu_custom_call" | custom-call | flops 1024 | bytes 1024 | tf_op jit(solution)/shard_map/score/pallas_call | solution.py:202
  64.5 0.5 collective-permute-done.12.refs_6_
  65.0 0.4 collective-permute-done.14.refs_7_
  65.3 7.9 %score.3.mine = f32[192,512]{1,0:T(8,128)S(1)} custom-call(bf16[24,8192]{1,0:T(8,128)(2,1)S(1)} %maximum_select_fusion.1.refs_0_, bf16[24,8192]{1,0:T(8,128)(2,1)S(1)} %collective-permute-done.1.refs_1_, bf16[24,8192]{1,0:T(8,128)(2,1)S(1)} %copy-done.7, bf16[24,8192]{1,0:T(8,128)(2,1)} %collective-permute-done.4.refs_3_, ...), custom_call_target="tpu_custom_call" | custom-call | flops 1024 | bytes 1024 | tf_op jit(solution)/shard_map/score/pallas_call | solution.py:202
  73.3 3.5 %collective-permute-start.17 = (f32[192,512]{1,0:T(8,128)S(1)}, f32[192,512]{1,0:T(8,128)S(1)}, u32[]{:S(2)}, u32[]{:S(2)}) collective-permute-start(f32[192,512]{1,0:T(8,128)S(1)} %score.3.mine), channel_id=1, source_target_pairs={{0,8},{8,0},{16,24},{24,16},{32,40},{40,32},{48,56},{56,48},{64,72... | collective-permute-start | bytes 1179656 | tf_op jit(solution)/shard_map/ppermute | solution.py:51
  77.0 1.1 collective-permute-done.17.recv
  78.2 0.8 collective-permute-start.18
  79.0 1.7 %collective-permute-done.18.refs_1_ = f32[2,512]{1,0:T(2,128)S(1)} collective-permute-done((f32[2,512]{1,0:T(2,128)S(1)}, f32[2,512]{1,0:T(2,128)S(1)}, u32[]{:S(2)}, u32[]{:S(2)}) %collective-permute-start.18) | collective-permute-done | bytes 4128 | tf_op jit(solution)/shard_map/ppermute | solution.py:422
  80.8 1.4 collective-permute-start.19
  82.1 2.6 %collective-permute-start.20 = (f32[2,512]{1,0:T(2,128)S(1)}, f32[2,512]{1,0:T(2,128)S(1)}, u32[]{:S(2)}, u32[]{:S(2)}) collective-permute-start(f32[2,512]{1,0:T(2,128)S(1)} %merge.1.refs_3_), channel_id=1, source_target_pairs={{0,2},{1,3},{2,0},{3,1},{4,6},{5,7},{6,4},{7,5},{8,10},{9,11},{10,... | collective-permute-start | bytes 12296 | tf_op jit(solution)/shard_map/ppermute | solution.py:424
  84.8 1.1 collective-permute-start.21
  86.1 1.1 collective-permute-done.21.refs_6_
  87.2 0.3 chance.1
  87.6 4.5 %back.2 = (bf16[24,8320]{1,0:T(8,128)(2,1)S(1)}, bf16[24,8320]{1,0:T(8,128)(2,1)S(1)}, bf16[24,8320]{1,0:T(8,128)(2,1)S(1)}, bf16[24,8320]{1,0:T(8,128)(2,1)S(1)...) custom-call(bf16[192,512]{1,0:T(8,128)(2,1)S(1)} %get-tuple-element., ...), custom_call_target="tpu_custom_call" | custom-call | flops 1024 | bytes 1024 | tf_op jit(solution)/shard_map/back/pallas_call | solution.py:299
  92.1 2.4 %collective-permute-start.22 = (bf16[24,8320]{1,0:T(8,128)(2,1)S(1)}, bf16[24,8320]{1,0:T(8,128)(2,1)S(1)}, u32[]{:S(2)}, u32[]{:S(2)}) collective-permute-start(bf16[24,8320]{1,0:T(8,128)(2,1)S(1)} %get-tuple-element.59), channel_id=1, source_target_pairs={{0,64},{8,72},{16,80},{24,88},{32,96},{40,104},{48,112},{56,120},{... | collective-permute-start | bytes 1198088 | tf_op jit(solution)/shard_map/ppermute | solution.py:47
  94.4 1.0 collective-permute-start.25
  95.5 0.4 collective-permute-start.28
  95.9 4.5 %back.3 = (bf16[24,8192]{1,0:T(8,128)(2,1)S(1)}, bf16[24,8192]{1,0:T(8,128)(2,1)S(1)}, bf16[24,8192]{1,0:T(8,128)(2,1)S(1)}, bf16[24,8192]{1,0:T(8,128)(2,1)S(1)...) custom-call(bf16[192,512]{1,0:T(8,128)(2,1)S(1)} %get-tuple-element., ...), custom_call_target="tpu_custom_call" | custom-call | flops 1024 | bytes 1024 | tf_op jit(solution)/shard_map/back/pallas_call | solution.py:299
  100.4 0.8 collective-permute-start.30
  101.2 1.9 %collective-permute-start.33 = (bf16[24,8192]{1,0:T(8,128)(2,1)S(1)}, bf16[24,8192]{1,0:T(8,128)(2,1)S(1)}, u32[]{:S(2)}, u32[]{:S(2)}) collective-permute-start(bf16[24,8192]{1,0:T(8,128)(2,1)S(1)} %get-tuple-element.74), channel_id=1, source_target_pairs={{0,48},{8,56},{16,0},{24,8},{32,16},{40,24},{48,32},{56,40},{64,11... | collective-permute-start | bytes 1179656 | tf_op jit(solution)/shard_map/ppermute | solution.py:43
  103.0 0.2 add.49
  103.3 0.6 collective-permute-start.26
  103.9 0.9 collective-permute-start.23
  104.8 4.3 %collective-permute-done.30.refs_1_ = bf16[24,8192]{1,0:T(8,128)(2,1)S(1)} collective-permute-done((bf16[24,8192]{1,0:T(8,128)(2,1)S(1)}, bf16[24,8192]{1,0:T(8,128)(2,1)S(1)}, u32[]{:S(2)}, u32[]{:S(2)}) %collective-permute-start.30) | collective-permute-done | bytes 393248 | tf_op jit(solution)/shard_map/ppermute | solution.py:47
  109.3 0.3 collective-permute-start.31
  109.6 1.5 %collective-permute-done.33.refs_1_ = bf16[24,8192]{1,0:T(8,128)(2,1)S(1)} collective-permute-done((bf16[24,8192]{1,0:T(8,128)(2,1)S(1)}, bf16[24,8192]{1,0:T(8,128)(2,1)S(1)}, u32[]{:S(2)}, u32[]{:S(2)}) %collective-permute-start.33) | collective-permute-done | bytes 393248 | tf_op jit(solution)/shard_map/ppermute | solution.py:43
  111.1 1.4 collective-permute-start.34
  112.5 0.3 add.51
  112.8 3.5 %collective-permute-start.29 = (bf16[24,8320]{1,0:T(8,128)(2,1)S(1)}, bf16[24,8320]{1,0:T(8,128)(2,1)S(1)}, u32[]{:S(2)}, u32[]{:S(2)}) collective-permute-start(bf16[24,8320]{1,0:T(8,128)(2,1)S(1)} %add.51), channel_id=1, source_target_pairs={{0,64},{8,72},{16,80},{24,88},{32,96},{40,104},{48,112},{56,120},{... | collective-permute-start | bytes 1198088 | tf_op jit(solution)/shard_map/ppermute | solution.py:47
  116.4 3.3 %collective-permute-done.26.refs_1_ = bf16[24,8320]{1,0:T(8,128)(2,1)S(1)} collective-permute-done((bf16[24,8320]{1,0:T(8,128)(2,1)S(1)}, bf16[24,8320]{1,0:T(8,128)(2,1)S(1)}, u32[]{:S(2)}, u32[]{:S(2)}) %collective-permute-start.26) | collective-permute-done | bytes 399392 | tf_op jit(solution)/shard_map/ppermute | solution.py:43
  119.6 0.2 add.50
  119.9 1.5 %collective-permute-start.27 = (bf16[24,8320]{1,0:T(8,128)(2,1)S(1)}, bf16[24,8320]{1,0:T(8,128)(2,1)S(1)}, u32[]{:S(2)}, u32[]{:S(2)}) collective-permute-start(bf16[24,8320]{1,0:T(8,128)(2,1)S(1)} %add.50), channel_id=1, source_target_pairs={{0,48},{8,56},{16,0},{24,8},{32,16},{40,24},{48,32},{56,40},{64,11... | collective-permute-start | bytes 1198088 | tf_op jit(solution)/shard_map/ppermute | solution.py:43
  121.5 4.1 %collective-permute-start.35 = (bf16[24,8192]{1,0:T(8,128)(2,1)S(1)}, bf16[24,8192]{1,0:T(8,128)(2,1)S(1)}, u32[]{:S(2)}, u32[]{:S(2)}) collective-permute-start(bf16[24,8192]{1,0:T(8,128)(2,1)S(1)} %add.55), channel_id=1, source_target_pairs={{0,64},{8,72},{16,80},{24,88},{32,96},{40,104},{48,112},{56,120},{... | collective-permute-start | bytes 1179656 | tf_op jit(solution)/shard_map/ppermute | solution.py:47
  125.8 2.3 %collective-permute-done.34.refs_2_ = bf16[24,8192]{1,0:T(8,128)(2,1)S(1)} collective-permute-done((bf16[24,8192]{1,0:T(8,128)(2,1)S(1)}, bf16[24,8192]{1,0:T(8,128)(2,1)S(1)}, u32[]{:S(2)}, u32[]{:S(2)}) %collective-permute-start.34) | collective-permute-done | bytes 393248 | tf_op jit(solution)/shard_map/ppermute | solution.py:43
  128.1 1.2 fusion.2
  129.3 4.9 %collective-permute-done.35.refs_3_ = bf16[24,8192]{1,0:T(8,128)(2,1)S(1)} collective-permute-done((bf16[24,8192]{1,0:T(8,128)(2,1)S(1)}, bf16[24,8192]{1,0:T(8,128)(2,1)S(1)}, u32[]{:S(2)}, u32[]{:S(2)}) %collective-permute-start.35) | collective-permute-done | bytes 393248 | tf_op jit(solution)/shard_map/ppermute | solution.py:47
  134.2 4.7 %collective-permute-done.32.refs_1_ = bf16[24,8192]{1,0:T(8,128)(2,1)S(1)} collective-permute-done((bf16[24,8192]{1,0:T(8,128)(2,1)S(1)}, bf16[24,8192]{1,0:T(8,128)(2,1)S(1)}, u32[]{:S(2)}, u32[]{:S(2)}) %collective-permute-start.32) | collective-permute-done | bytes 393248 | tf_op jit(solution)/shard_map/ppermute | solution.py:39
  139.1 0.4 add.52
  139.6 0.2 select_bitcast_fusion
  139.8 4.9 %collective-permute-start.36 = (bf16[12,16384]{1,0:T(8,128)(2,1)S(1)}, bf16[12,16384]{1,0:T(8,128)(2,1)S(1)}, u32[]{:S(2)}, u32[]{:S(2)}) collective-permute-start(bf16[12,16384]{1,0:T(8,128)(2,1)S(1)} %get-tuple-element.89), channel_id=1, source_target_pairs={{0,8},{8,0},{16,24},{24,16},{32,40},{40,32},{48,56},{56,48},{64,72... | collective-permute-start | bytes 1179656 | tf_op jit(solution)/shard_map/ppermute | solution.py:51
  144.8 1.2 convolution_bitcast_fusion
  145.9 1.7 %copy.15 = f32[1,12,16384]{2,0,1:T(1,128)} copy(f32[1,12,16384]{2,1,0:T(8,128)S(1)} %convolution_bitcast_fusion) | data formatting | bytes 1572864
  147.6 1.3 maximum_select_fusion
  (76 shorter events, 3.1 us)
Async XLA Ops:
  0.6 2.8 %copy-start.11 = (s32[256]{0:T(256)S(1)}, s32[256]{0:T(256)}, u32[]{:S(2)}) copy-start(s32[256]{0:T(256)} %param.7) | copy-start | bytes 3076
  1.9 11.7 %copy-start = (f32[32,16384]{1,0:T(8,128)S(1)}, f32[32,16384]{1,0:T(8,128)}, u32[]{:S(2)}) copy-start(f32[32,16384]{1,0:T(8,128)} %contrast.2) | copy-start | bytes 6291460
  1.9 11.7 %copy-start.10 = (f32[16384]{0:T(1024)S(1)}, f32[16384]{0:T(1024)}, u32[]{:S(2)}) copy-start(f32[16384]{0:T(1024)} %param.9) | copy-start | bytes 196612
  2.0 3.0 %collective-permute-start = (bf16[12,16384]{1,0:T(8,128)(2,1)S(1)}, bf16[12,16384]{1,0:T(8,128)(2,1)S(1)}, u32[]{:S(2)}, u32[]{:S(2)}) collective-permute-start(bf16[12,16384]{1,0:T(8,128)(2,1)S(1)} %get-tuple-element.87), channel_id=1, source_target_pairs={{0,8},{8,0},{16,24},{24,16},{32,40},{40,32},{48,56},{56,48},{64,72... | collective-permute-start | bytes 1179656 | tf_op jit(solution)/shard_map/ppermute | solution.py:51
  3.5 9.8 %collective-permute-start.8 = (s32[256]{0:T(256)S(1)}, s32[256]{0:T(256)S(1)}, u32[]{:S(2)}, u32[]{:S(2)}) collective-permute-start(s32[256]{0:T(256)S(1)} %copy-done.11), channel_id=1, source_target_pairs={{0,8},{8,0},{16,24},{24,16},{32,40},{40,32},{48,56},{56,48},{64,72... | collective-permute-start | bytes 3080 | tf_op jit(solution)/shard_map/ppermute | solution.py:51
  5.2 21.4 %collective-permute-start.3 = (bf16[24,8192]{1,0:T(8,128)(2,1)S(1)}, bf16[24,8192]{1,0:T(8,128)(2,1)S(1)}, u32[]{:S(2)}, u32[]{:S(2)}) collective-permute-start(bf16[24,8192]{1,0:T(8,128)(2,1)S(1)} %maximum_select_fusion.2.refs_0_), channel_id=1, source_target_pairs={{0,64},{8,72},{16,80},{24,88},{32,96},{40,104},{48,112},{56,120},{... | collective-permute-start | bytes 1179656 | tf_op jit(solution)/shard_map/ppermute | solution.py:47
  9.0 17.6 %collective-permute-start.6 = (bf16[24,8192]{1,0:T(8,128)(2,1)S(1)}, bf16[24,8192]{1,0:T(8,128)(2,1)S(1)}, u32[]{:S(2)}, u32[]{:S(2)}) collective-permute-start(bf16[24,8192]{1,0:T(8,128)(2,1)S(1)} %maximum_select_fusion.2.refs_0_), channel_id=1, source_target_pairs={{0,16},{8,24},{16,32},{24,40},{32,48},{40,56},{48,0},{56,8},{64,80... | collective-permute-start | bytes 1179656 | tf_op jit(solution)/shard_map/ppermute | solution.py:39
  10.2 16.4 %collective-permute-start.9 = (bf16[24,8192]{1,0:T(8,128)(2,1)S(1)}, bf16[24,8192]{1,0:T(8,128)(2,1)S(1)}, u32[]{:S(2)}, u32[]{:S(2)}) collective-permute-start(bf16[24,8192]{1,0:T(8,128)(2,1)S(1)} %maximum_select_fusion.2.refs_0_), channel_id=1, source_target_pairs={{0,48},{8,56},{16,0},{24,8},{32,16},{40,24},{48,32},{56,40},{64,11... | collective-permute-start | bytes 1179656 | tf_op jit(solution)/shard_map/ppermute | solution.py:43
  11.9 16.4 %collective-permute-start.1 = (bf16[24,8192]{1,0:T(8,128)(2,1)S(1)}, bf16[24,8192]{1,0:T(8,128)(2,1)S(1)}, u32[]{:S(2)}, u32[]{:S(2)}) collective-permute-start(bf16[24,8192]{1,0:T(8,128)(2,1)S(1)} %maximum_select_fusion.1.refs_0_), channel_id=1, source_target_pairs={{0,48},{8,56},{16,0},{24,8},{32,16},{40,24},{48,32},{56,40},{64,11... | collective-permute-start | bytes 1179656 | tf_op jit(solution)/shard_map/ppermute | solution.py:43
  13.2 15.4 %collective-permute-start.2 = (bf16[24,8192]{1,0:T(8,128)(2,1)S(1)}, bf16[24,8192]{1,0:T(8,128)(2,1)S(1)}, u32[]{:S(2)}, u32[]{:S(2)}) collective-permute-start(bf16[24,8192]{1,0:T(8,128)(2,1)S(1)} %maximum_select_fusion.1.refs_0_), channel_id=1, source_target_pairs={{0,16},{8,24},{16,32},{24,40},{32,48},{40,56},{48,0},{56,8},{64,80... | collective-permute-start | bytes 1179656 | tf_op jit(solution)/shard_map/ppermute | solution.py:39
  26.6 5.5 %copy-start.2 = (bf16[24,8192]{1,0:T(8,128)(2,1)}, bf16[24,8192]{1,0:T(8,128)(2,1)S(1)}, u32[]{:S(2)}) copy-start(bf16[24,8192]{1,0:T(8,128)(2,1)S(1)} %collective-permute-done.3.refs_3_) | copy-start | bytes 1179652
  26.6 0.8 copy-start.8
  28.6 0.7 copy-start.6
  29.4 25.4 %collective-permute-start.10 = (bf16[16,256,1024]{2,1,0:T(8,128)(2,1)}, bf16[16,256,1024]{2,1,0:T(8,128)(2,1)}, u32[]{:S(2)}, u32[]{:S(2)}) collective-permute-start(bf16[16,256,1024]{2,1,0:T(8,128)(2,1)} %get-tuple-element.44), channel_id=1, source_target_pairs={{0,8},{8,0},{16,24},{24,16},{32,40},{40,32},{48,56},{56,48},{64,72... | collective-permute-start | bytes 25165832 | tf_op jit(solution)/shard_map/ppermute | solution.py:51
  30.9 12.1 %collective-permute-start.7 = (bf16[24,8192]{1,0:T(8,128)(2,1)S(1)}, bf16[24,8192]{1,0:T(8,128)(2,1)}, u32[]{:S(2)}, u32[]{:S(2)}) collective-permute-start(bf16[24,8192]{1,0:T(8,128)(2,1)S(1)} %collective-permute-done.6.refs_2_), channel_id=1, source_target_pairs={{0,16},{8,24},{16,32},{24,40},{32,48},{40,56},{48,0},{56,8},{64,80... | collective-permute-start | bytes 1179656 | tf_op jit(solution)/shard_map/ppermute | solution.py:39
  32.1 0.7 copy-start.4
  32.9 11.0 %collective-permute-start.5 = (bf16[24,8192]{1,0:T(8,128)(2,1)S(1)}, bf16[24,8192]{1,0:T(8,128)(2,1)}, u32[]{:S(2)}, u32[]{:S(2)}) collective-permute-start(bf16[24,8192]{1,0:T(8,128)(2,1)S(1)} %collective-permute-done.1.refs_1_), channel_id=1, source_target_pairs={{0,48},{8,56},{16,0},{24,8},{32,16},{40,24},{48,32},{56,40},{64,11... | collective-permute-start | bytes 1179656 | tf_op jit(solution)/shard_map/ppermute | solution.py:43
  34.3 11.8 %collective-permute-start.4 = (bf16[24,8192]{1,0:T(8,128)(2,1)S(1)}, bf16[24,8192]{1,0:T(8,128)(2,1)}, u32[]{:S(2)}, u32[]{:S(2)}) collective-permute-start(bf16[24,8192]{1,0:T(8,128)(2,1)S(1)} %maximum_select_fusion.1.refs_0_), channel_id=1, source_target_pairs={{0,64},{8,72},{16,80},{24,88},{32,96},{40,104},{48,112},{56,120},{... | collective-permute-start | bytes 1179656 | tf_op jit(solution)/shard_map/ppermute | solution.py:47
  43.0 11.7 %collective-permute-start.13 = (bf16[24,8192]{1,0:T(8,128)(2,1)}, bf16[24,8192]{1,0:T(8,128)(2,1)}, u32[]{:S(2)}, u32[]{:S(2)}) collective-permute-start(bf16[24,8192]{1,0:T(8,128)(2,1)} %collective-permute-done.7.refs_4_), channel_id=1, source_target_pairs={{0,64},{8,72},{16,80},{24,88},{32,96},{40,104},{48,112},{56,120},{... | collective-permute-start | bytes 1179656 | tf_op jit(solution)/shard_map/ppermute | solution.py:47
  43.1 1.0 copy-start.3
  43.1 13.5 %copy-start.5 = (bf16[24,8192]{1,0:T(8,128)(2,1)S(1)}, bf16[24,8192]{1,0:T(8,128)(2,1)}, u32[]{:S(2)}) copy-start(bf16[24,8192]{1,0:T(8,128)(2,1)} %copy-done.4) | copy-start | bytes 1179652
  43.1 13.5 %copy-start.9 = (bf16[24,8192]{1,0:T(8,128)(2,1)S(1)}, bf16[24,8192]{1,0:T(8,128)(2,1)}, u32[]{:S(2)}) copy-start(bf16[24,8192]{1,0:T(8,128)(2,1)} %copy-done.8) | copy-start | bytes 1179652
  43.9 20.6 %copy-start.1 = (bf16[64,16384]{1,0:T(8,128)(2,1)}, bf16[64,16384]{1,0:T(8,128)(2,1)S(1)}, u32[]{:S(2)}) copy-start(bf16[64,16384]{1,0:T(8,128)(2,1)S(1)} %table.1.refs_10_) | copy-start | bytes 6291460
  44.1 12.3 %collective-permute-start.15 = (bf16[24,8192]{1,0:T(8,128)(2,1)S(1)}, bf16[24,8192]{1,0:T(8,128)(2,1)S(1)}, u32[]{:S(2)}, u32[]{:S(2)}) collective-permute-start(bf16[24,8192]{1,0:T(8,128)(2,1)S(1)} %copy-done.3), channel_id=1, source_target_pairs={{0,48},{8,56},{16,0},{24,8},{32,16},{40,24},{48,32},{56,40},{64,11... | collective-permute-start | bytes 1179656 | tf_op jit(solution)/shard_map/ppermute | solution.py:43
  46.1 10.4 %collective-permute-start.16 = (bf16[24,8192]{1,0:T(8,128)(2,1)S(1)}, bf16[24,8192]{1,0:T(8,128)(2,1)S(1)}, u32[]{:S(2)}, u32[]{:S(2)}) collective-permute-start(bf16[24,8192]{1,0:T(8,128)(2,1)S(1)} %copy-done.3), channel_id=1, source_target_pairs={{0,16},{8,24},{16,32},{24,40},{32,48},{40,56},{48,0},{56,8},{64,80... | collective-permute-start | bytes 1179656 | tf_op jit(solution)/shard_map/ppermute | solution.py:39
  46.1 18.9 %collective-permute-start.12 = (bf16[24,8192]{1,0:T(8,128)(2,1)}, bf16[24,8192]{1,0:T(8,128)(2,1)S(1)}, u32[]{:S(2)}, u32[]{:S(2)}) collective-permute-start(bf16[24,8192]{1,0:T(8,128)(2,1)} %collective-permute-done.4.refs_3_), channel_id=1, source_target_pairs={{0,16},{8,24},{16,32},{24,40},{32,48},{40,56},{48,0},{56,8},{64,80... | collective-permute-start | bytes 1179656 | tf_op jit(solution)/shard_map/ppermute | solution.py:39
  54.7 10.7 %collective-permute-start.14 = (bf16[24,8192]{1,0:T(8,128)(2,1)}, bf16[24,8192]{1,0:T(8,128)(2,1)S(1)}, u32[]{:S(2)}, u32[]{:S(2)}) collective-permute-start(bf16[24,8192]{1,0:T(8,128)(2,1)} %collective-permute-done.5.refs_4_), channel_id=1, source_target_pairs={{0,64},{8,72},{16,80},{24,88},{32,96},{40,104},{48,112},{56,120},{... | collective-permute-start | bytes 1179656 | tf_op jit(solution)/shard_map/ppermute | solution.py:47
  54.8 10.6 %collective-permute-start.11 = (bf16[24,8192]{1,0:T(8,128)(2,1)}, bf16[24,8192]{1,0:T(8,128)(2,1)S(1)}, u32[]{:S(2)}, u32[]{:S(2)}) collective-permute-start(bf16[24,8192]{1,0:T(8,128)(2,1)} %collective-permute-done.4.refs_3_), channel_id=1, source_target_pairs={{0,48},{8,56},{16,0},{24,8},{32,16},{40,24},{48,32},{56,40},{64,11... | collective-permute-start | bytes 1179656 | tf_op jit(solution)/shard_map/ppermute | solution.py:43
  56.5 8.8 %copy-start.7 = (bf16[24,8192]{1,0:T(8,128)(2,1)S(1)}, bf16[24,8192]{1,0:T(8,128)(2,1)}, u32[]{:S(2)}) copy-start(bf16[24,8192]{1,0:T(8,128)(2,1)} %copy-done.6) | copy-start | bytes 1179652
  64.4 12.3 %copy-start.12 = (s32[512]{0:T(512)S(1)}, s32[512]{0:T(512)}, u32[]{:S(2)}) copy-start(s32[512]{0:T(512)} %param.11) | copy-start | bytes 6148
  73.3 4.8 %collective-permute-start.17 = (f32[192,512]{1,0:T(8,128)S(1)}, f32[192,512]{1,0:T(8,128)S(1)}, u32[]{:S(2)}, u32[]{:S(2)}) collective-permute-start(f32[192,512]{1,0:T(8,128)S(1)} %score.3.mine), channel_id=1, source_target_pairs={{0,8},{8,0},{16,24},{24,16},{32,40},{40,32},{48,56},{56,48},{64,72... | collective-permute-start | bytes 1179656 | tf_op jit(solution)/shard_map/ppermute | solution.py:51
  78.2 2.5 %collective-permute-start.18 = (f32[2,512]{1,0:T(2,128)S(1)}, f32[2,512]{1,0:T(2,128)S(1)}, u32[]{:S(2)}, u32[]{:S(2)}) collective-permute-start(f32[2,512]{1,0:T(2,128)S(1)} %get-tuple-element.52.refs_0_), channel_id=1, source_target_pairs={{0,4},{1,5},{2,6},{3,7},{4,0},{5,1},{6,2},{7,3},{8,12},{9,13},{10,... | collective-permute-start | bytes 12296 | tf_op jit(solution)/shard_map/ppermute | solution.py:422
  80.8 5.2 %collective-permute-start.19 = (f32[2,512]{1,0:T(2,128)S(1)}, f32[2,512]{1,0:T(2,128)S(1)}, u32[]{:S(2)}, u32[]{:S(2)}) collective-permute-start(f32[2,512]{1,0:T(2,128)S(1)} %merge.1.refs_3_), channel_id=1, source_target_pairs={{0,1},{1,2},{2,3},{3,0},{4,5},{5,6},{6,7},{7,4},{8,9},{9,10},{10,1... | collective-permute-start | bytes 12296 | tf_op jit(solution)/shard_map/ppermute | solution.py:424
  82.1 4.0 %collective-permute-start.20 = (f32[2,512]{1,0:T(2,128)S(1)}, f32[2,512]{1,0:T(2,128)S(1)}, u32[]{:S(2)}, u32[]{:S(2)}) collective-permute-start(f32[2,512]{1,0:T(2,128)S(1)} %merge.1.refs_3_), channel_id=1, source_target_pairs={{0,2},{1,3},{2,0},{3,1},{4,6},{5,7},{6,4},{7,5},{8,10},{9,11},{10,... | collective-permute-start | bytes 12296 | tf_op jit(solution)/shard_map/ppermute | solution.py:424
  84.8 2.5 %collective-permute-start.21 = (f32[2,512]{1,0:T(2,128)S(1)}, f32[2,512]{1,0:T(2,128)S(1)}, u32[]{:S(2)}, u32[]{:S(2)}) collective-permute-start(f32[2,512]{1,0:T(2,128)S(1)} %merge.1.refs_3_), channel_id=1, source_target_pairs={{0,3},{1,0},{2,1},{3,2},{4,7},{5,4},{6,5},{7,6},{8,11},{9,8},{10,9... | collective-permute-start | bytes 12296 | tf_op jit(solution)/shard_map/ppermute | solution.py:424
  92.1 11.0 %collective-permute-start.22 = (bf16[24,8320]{1,0:T(8,128)(2,1)S(1)}, bf16[24,8320]{1,0:T(8,128)(2,1)S(1)}, u32[]{:S(2)}, u32[]{:S(2)}) collective-permute-start(bf16[24,8320]{1,0:T(8,128)(2,1)S(1)} %get-tuple-element.59), channel_id=1, source_target_pairs={{0,64},{8,72},{16,80},{24,88},{32,96},{40,104},{48,112},{56,120},{... | collective-permute-start | bytes 1198088 | tf_op jit(solution)/shard_map/ppermute | solution.py:47
  94.4 8.9 %collective-permute-start.25 = (bf16[24,8320]{1,0:T(8,128)(2,1)S(1)}, bf16[24,8320]{1,0:T(8,128)(2,1)S(1)}, u32[]{:S(2)}, u32[]{:S(2)}) collective-permute-start(bf16[24,8320]{1,0:T(8,128)(2,1)S(1)} %get-tuple-element.64), channel_id=1, source_target_pairs={{0,48},{8,56},{16,0},{24,8},{32,16},{40,24},{48,32},{56,40},{64,11... | collective-permute-start | bytes 1198088 | tf_op jit(solution)/shard_map/ppermute | solution.py:43
  95.5 13.8 %collective-permute-start.28 = (bf16[24,8320]{1,0:T(8,128)(2,1)S(1)}, bf16[24,8320]{1,0:T(8,128)(2,1)S(1)}, u32[]{:S(2)}, u32[]{:S(2)}) collective-permute-start(bf16[24,8320]{1,0:T(8,128)(2,1)S(1)} %get-tuple-element.67), channel_id=1, source_target_pairs={{0,16},{8,24},{16,32},{24,40},{32,48},{40,56},{48,0},{56,8},{64,80... | collective-permute-start | bytes 1198088 | tf_op jit(solution)/shard_map/ppermute | solution.py:39
  100.4 8.8 %collective-permute-start.30 = (bf16[24,8192]{1,0:T(8,128)(2,1)S(1)}, bf16[24,8192]{1,0:T(8,128)(2,1)S(1)}, u32[]{:S(2)}, u32[]{:S(2)}) collective-permute-start(bf16[24,8192]{1,0:T(8,128)(2,1)S(1)} %get-tuple-element.71), channel_id=1, source_target_pairs={{0,64},{8,72},{16,80},{24,88},{32,96},{40,104},{48,112},{56,120},{... | collective-permute-start | bytes 1179656 | tf_op jit(solution)/shard_map/ppermute | solution.py:47
  101.2 9.9 %collective-permute-start.33 = (bf16[24,8192]{1,0:T(8,128)(2,1)S(1)}, bf16[24,8192]{1,0:T(8,128)(2,1)S(1)}, u32[]{:S(2)}, u32[]{:S(2)}) collective-permute-start(bf16[24,8192]{1,0:T(8,128)(2,1)S(1)} %get-tuple-element.74), channel_id=1, source_target_pairs={{0,48},{8,56},{16,0},{24,8},{32,16},{40,24},{48,32},{56,40},{64,11... | collective-permute-start | bytes 1179656 | tf_op jit(solution)/shard_map/ppermute | solution.py:43
  103.3 16.3 %collective-permute-start.26 = (bf16[24,8320]{1,0:T(8,128)(2,1)S(1)}, bf16[24,8320]{1,0:T(8,128)(2,1)S(1)}, u32[]{:S(2)}, u32[]{:S(2)}) collective-permute-start(bf16[24,8320]{1,0:T(8,128)(2,1)S(1)} %add.49), channel_id=1, source_target_pairs={{0,48},{8,56},{16,0},{24,8},{32,16},{40,24},{48,32},{56,40},{64,11... | collective-permute-start | bytes 1198088 | tf_op jit(solution)/shard_map/ppermute | solution.py:43
  103.9 12.4 %collective-permute-start.23 = (bf16[24,8192]{1,0:T(8,128)(2,1)S(1)}, bf16[24,8192]{1,0:T(8,128)(2,1)S(1)}, u32[]{:S(2)}, u32[]{:S(2)}) collective-permute-start(bf16[24,8192]{1,0:T(8,128)(2,1)S(1)} %get-tuple-element.60), channel_id=1, source_target_pairs={{0,16},{8,24},{16,32},{24,40},{32,48},{40,56},{48,0},{56,8},{64,80... | collective-permute-start | bytes 1179656 | tf_op jit(solution)/shard_map/ppermute | solution.py:39
  109.3 12.3 %collective-permute-start.31 = (bf16[24,8192]{1,0:T(8,128)(2,1)S(1)}, bf16[24,8192]{1,0:T(8,128)(2,1)S(1)}, u32[]{:S(2)}, u32[]{:S(2)}) collective-permute-start(bf16[24,8192]{1,0:T(8,128)(2,1)S(1)} %add.53), channel_id=1, source_target_pairs={{0,16},{8,24},{16,32},{24,40},{32,48},{40,56},{48,0},{56,8},{64,80... | collective-permute-start | bytes 1179656 | tf_op jit(solution)/shard_map/ppermute | solution.py:39
  111.1 17.0 %collective-permute-start.34 = (bf16[24,8192]{1,0:T(8,128)(2,1)S(1)}, bf16[24,8192]{1,0:T(8,128)(2,1)S(1)}, u32[]{:S(2)}, u32[]{:S(2)}) collective-permute-start(bf16[24,8192]{1,0:T(8,128)(2,1)S(1)} %get-tuple-element.75), channel_id=1, source_target_pairs={{0,48},{8,56},{16,0},{24,8},{32,16},{40,24},{48,32},{56,40},{64,11... | collective-permute-start | bytes 1179656 | tf_op jit(solution)/shard_map/ppermute | solution.py:43
  112.8 26.3 %collective-permute-start.29 = (bf16[24,8320]{1,0:T(8,128)(2,1)S(1)}, bf16[24,8320]{1,0:T(8,128)(2,1)S(1)}, u32[]{:S(2)}, u32[]{:S(2)}) collective-permute-start(bf16[24,8320]{1,0:T(8,128)(2,1)S(1)} %add.51), channel_id=1, source_target_pairs={{0,64},{8,72},{16,80},{24,88},{32,96},{40,104},{48,112},{56,120},{... | collective-permute-start | bytes 1198088 | tf_op jit(solution)/shard_map/ppermute | solution.py:47
  116.3 22.8 %collective-permute-start.24 = (bf16[24,8320]{1,0:T(8,128)(2,1)S(1)}, bf16[24,8320]{1,0:T(8,128)(2,1)S(1)}, u32[]{:S(2)}, u32[]{:S(2)}) collective-permute-start(bf16[24,8320]{1,0:T(8,128)(2,1)S(1)} %get-tuple-element.61), channel_id=1, source_target_pairs={{0,16},{8,24},{16,32},{24,40},{32,48},{40,56},{48,0},{56,8},{64,80... | collective-permute-start | bytes 1198088 | tf_op jit(solution)/shard_map/ppermute | solution.py:39
  119.9 19.2 %collective-permute-start.27 = (bf16[24,8320]{1,0:T(8,128)(2,1)S(1)}, bf16[24,8320]{1,0:T(8,128)(2,1)S(1)}, u32[]{:S(2)}, u32[]{:S(2)}) collective-permute-start(bf16[24,8320]{1,0:T(8,128)(2,1)S(1)} %add.50), channel_id=1, source_target_pairs={{0,48},{8,56},{16,0},{24,8},{32,16},{40,24},{48,32},{56,40},{64,11... | collective-permute-start | bytes 1198088 | tf_op jit(solution)/shard_map/ppermute | solution.py:43
  121.5 12.7 %collective-permute-start.35 = (bf16[24,8192]{1,0:T(8,128)(2,1)S(1)}, bf16[24,8192]{1,0:T(8,128)(2,1)S(1)}, u32[]{:S(2)}, u32[]{:S(2)}) collective-permute-start(bf16[24,8192]{1,0:T(8,128)(2,1)S(1)} %add.55), channel_id=1, source_target_pairs={{0,64},{8,72},{16,80},{24,88},{32,96},{40,104},{48,112},{56,120},{... | collective-permute-start | bytes 1179656 | tf_op jit(solution)/shard_map/ppermute | solution.py:47
  128.1 10.8 %collective-permute-start.32 = (bf16[24,8192]{1,0:T(8,128)(2,1)S(1)}, bf16[24,8192]{1,0:T(8,128)(2,1)S(1)}, u32[]{:S(2)}, u32[]{:S(2)}) collective-permute-start(bf16[24,8192]{1,0:T(8,128)(2,1)S(1)} %add.54), channel_id=1, source_target_pairs={{0,16},{8,24},{16,32},{24,40},{32,48},{40,56},{48,0},{56,8},{64,80... | collective-permute-start | bytes 1179656 | tf_op jit(solution)/shard_map/ppermute | solution.py:39
  139.8 7.8 %collective-permute-start.36 = (bf16[12,16384]{1,0:T(8,128)(2,1)S(1)}, bf16[12,16384]{1,0:T(8,128)(2,1)S(1)}, u32[]{:S(2)}, u32[]{:S(2)}) collective-permute-start(bf16[12,16384]{1,0:T(8,128)(2,1)S(1)} %get-tuple-element.89), channel_id=1, source_target_pairs={{0,8},{8,0},{16,24},{24,16},{32,40},{40,32},{48,56},{56,48},{64,72... | collective-permute-start | bytes 1179656 | tf_op jit(solution)/shard_map/ppermute | solution.py:51

commit v4 on v3

--- a/solution.py
+++ b/solution.py
@@ -61,8 +61,12 @@
     return pl.BlockSpec(shape, lambda j: (0,) * len(shape))
 
 
-def weigh_kernel(core, keep, give, hot3, contrast, noise, keep_out, give_out):
+def weigh_kernel(core, keep, give, hot3, contrast, noise, keep_out, give_out, quad_out):
     amp = contrast[...] * noise[...]
+    hq = 0.5 * contrast[...] * amp
+    h1 = hq.astype(BF16)
+    h2 = (hq - h1.astype(F32)).astype(BF16)
+    quad_out[...] = jnp.concatenate([h1, h2], axis=0)
     a1 = amp.astype(BF16)
     rest = amp - a1.astype(F32)
     a2 = rest.astype(BF16)
@@ -94,38 +98,21 @@
                 pl.BlockSpec((n_cls, kb), lambda j, s: (0, j)),
                 pl.BlockSpec((1, kb), lambda j, s: (0, j)),
             ],
-            out_specs=[pl.BlockSpec((wide, rows, KB), lambda j, s: (j, 0, 0))] * 2,
+            out_specs=[
+                pl.BlockSpec((wide, rows, KB), lambda j, s: (j, 0, 0)),
+                pl.BlockSpec((wide, rows, KB), lambda j, s: (j, 0, 0)),
+                pl.BlockSpec((2 * n_cls, kb), lambda j, s: (0, j)),
+            ],
         ),
-        out_shape=[jax.ShapeDtypeStruct((half // KB, rows, KB), BF16)] * 2,
-        compiler_params=params(),
+        out_shape=[
+            jax.ShapeDtypeStruct((half // KB, rows, KB), BF16),
+            jax.ShapeDtypeStruct((half // KB, rows, KB), BF16),
+            jax.ShapeDtypeStruct((2 * n_cls, half), BF16),
+        ],
+        compiler_params=params(56),
         cost_estimate=CHEAP,
         name="weigh",
     )(core, images, images, hot3, contrast, noise)
-
-
-def table_kernel(contrast, noise, out):
-    hq = 0.5 * contrast[...] * contrast[...] * noise[...]
-    h1 = hq.astype(BF16)
-    h2 = (hq - h1.astype(F32)).astype(BF16)
-    out[...] = jnp.concatenate([h1, h2], axis=0)
-
-
-def quad_table(contrast, noise):
-    n_cls, half = contrast.shape
-    kb = 4 * KB
-    return pl.pallas_call(
-        table_kernel,
-        grid=(half // kb,),
-        in_specs=[
-            pl.BlockSpec((n_cls, kb), lambda j: (0, j)),
-            pl.BlockSpec((1, kb), lambda j: (0, j)),
-        ],
-        out_specs=pl.BlockSpec((2 * n_cls, kb), lambda j: (0, j)),
-        out_shape=jax.ShapeDtypeStruct((2 * n_cls, half), BF16),
-        compiler_params=params(),
-        cost_estimate=CHEAP,
-        name="table",
-    )(contrast, noise)
 
 
 def score_kernel(n_parts, has_acc, nb, wide, *refs):
@@ -195,6 +182,7 @@
         pl.BlockSpec((quads.shape[0], kb), lambda j: (0, off + j)),
         full(hot.shape),
     ]
+    quads = pltpu.with_memory_space_constraint(quads, pltpu.HBM)
     args = [*parts, w_own, w_sib, quads, hot]
     if acc_in is not None:
         in_specs.append(full((used, 2 * rows)))
@@ -371,24 +359,23 @@
         )
         for cols in (slice(0, quart), slice(quart, half))
     )
-    xm_a, xp_b, zz_a = to_xp(own_a), to_xm(own_b), to_z(own_a)
+    sib_classes = to_core(tie(classes, got))
+    xm_a, xp_b, zz_a = to_xp(own_a), to_xm(own_b), to_z(tie(own_a, sib_classes))
     xm_b, xp_a = to_xp(own_b), to_xm(own_a)
     x2_a, x2_b = to_xp(xm_a), to_xm(xp_b)
     zz_b = to_z(tie(own_b, zz_a))
     fz_a, fz_b = tie(zz_a, x2_a, x2_b), tie(zz_b, x2_a, x2_b)
     zm_a, zp_a, z2_a = to_xp(fz_a), to_xm(fz_a), to_z(x2_a)
 
-    sib_classes = to_core(classes)
     ids = jnp.arange(n_cls, dtype=jnp.int32)[None, :]
     hot_own = (classes[:, None] == ids).astype(BF16)
     both_classes = jnp.concatenate([classes, sib_classes])
     hot = (both_classes[:, None] == ids).astype(F32)
     hot_wide = (both_classes[:, None] == jnp.arange(TAIL, dtype=jnp.int32)[None, :]).astype(BF16)
     hot3 = jnp.concatenate([hot_own] * 3, axis=1)
-    w_own, give = weigh(tie(core.reshape(1), own_a, sib_classes), images, hot3, contrast, noise)
+    w_own, give, quads = weigh(tie(core.reshape(1), own_a, sib_classes), images, hot3, contrast, noise)
     w_sib = to_core(tie(give, xm_a, xm_b, xp_a, xp_b, zz_a))
-    quads = quad_table(tie(contrast, xm_a), noise)
-    zm_b, zp_b, z2_b = to_xp(tie(fz_b, quads)), to_xm(tie(fz_b, w_sib)), to_z(tie(x2_b, z2_a))
+    zm_b, zp_b, z2_b = to_xp(tie(fz_b, w_sib)), to_xm(tie(fz_b, w_sib)), to_z(tie(x2_b, z2_a, w_sib))
 
     target = proj_index // h
     dz = (target // NX) ^ (chip // NX)

time: 149 us -> 148 us (level)
  local copies, waits for them, and re-layouts: 4.45 us -> 1.96 us
    ppermute x8, starting transfers between devices: 14.8 us -> 12 us  [to_z(): return lax.ppermute(v, 'img', img_perm(1, 0, 0))]
    unnamed x28 -> x8, local copies, waits for them, and re-layouts: 4.21 us -> 1.72 us
    pallas_call x1, Pallas kernels: 12.9 us -> 14.5 us  [weigh(): pl.pallas_call(weigh_kernel, grid_spec=pltpu.PrefetchScalarGridSpec(num_s...]
  transfers between devices with their start and end apart: 37 -> 37, of which waited for: 18 -> 16; matrix products, arithmetic and copies ran while one was open for 4% -> 4% of each run, Pallas kernels for 18% -> 19%
where the time goes in v4:
time: 148 us
  starting transfers between devices  49.6 us (34%)
  waiting for transfers between devices  46.7 us (32%)
  Pallas kernels  41.4 us (28%)
  other arithmetic  4.54 us (3%)
  matrix products  2.39 us (2%)
  local copies, waits for them, and re-layouts  1.96 us (1%)
    ppermute x8, waiting for transfers between devices, to_z(): return lax.ppermute(v, 'img', img_perm(1, 0, 0))  18.3 us
    pallas_call x2, Pallas kernels, score(): pl.pallas_call(functools.partial(score_kernel, len(parts), acc_in is not...  15.7 us
    ppermute x10, waiting for transfers between devices, to_xp(): return lax.ppermute(v, 'img', img_perm(0, 1, 0))  15.7 us
    ppermute x10, starting transfers between devices, to_xm(): return lax.ppermute(v, 'img', img_perm(0, -1, 0))  15.1 us
    pallas_call x1, Pallas kernels, weigh(): pl.pallas_call(weigh_kernel, grid_spec=pltpu.PrefetchScalarGridSpec(num_s...  14.5 us
    ppermute x8, starting transfers between devices, to_z(): return lax.ppermute(v, 'img', img_perm(1, 0, 0))  12 us
    ppermute x5, starting transfers between devices, to_core(): return lax.ppermute(v, 'img', img_perm(0, 0, 1))  11.9 us
    pallas_call x2, Pallas kernels, back(): pl.pallas_call(functools.partial(back_kernel, n_parts, nb, wide, tail), g...  8.98 us
  transfers between devices with their start and end apart: 37, of which 16 were waited for; matrix products, arithmetic and copies ran while one was open for 4% of the time, Pallas kernels for 19%

profile of v4, /device:TPU:1, one launch (start us, length us, event | category | flops | bytes accessed | tf_op | source)
XLA Modules:
  0.0 147.5 jit_solution(17944535475906944560)
XLA Ops:
  0.7 1.3 broadcast_select_fusion.2
  1.9 1.5 %collective-permute-start = (bf16[12,16384]{1,0:T(8,128)(2,1)S(1)}, bf16[12,16384]{1,0:T(8,128)(2,1)S(1)}, u32[]{:S(2)}, u32[]{:S(2)}) collective-permute-start(bf16[12,16384]{1,0:T(8,128)(2,1)S(1)} %get-tuple-element.89), channel_id=1, source_target_pairs={{0,8},{8,0},{16,24},{24,16},{32,40},{40,32},{48,56},{56,48},{64,72... | collective-permute-start | bytes 1179656 | tf_op jit(solution)/shard_map/ppermute | solution.py:51
  3.5 1.5 %collective-permute-done = bf16[12,16384]{1,0:T(8,128)(2,1)S(1)} collective-permute-done((bf16[12,16384]{1,0:T(8,128)(2,1)S(1)}, bf16[12,16384]{1,0:T(8,128)(2,1)S(1)}, u32[]{:S(2)}, u32[]{:S(2)}) %collective-permute-start) | collective-permute-done | bytes 393248 | tf_op jit(solution)/shard_map/ppermute | solution.py:51
  5.0 0.2 maximum_select_fusion.2.refs_0_
  5.2 1.4 collective-permute-start.7
  6.6 1.4 collective-permute-start.9
  8.0 0.9 collective-permute-start.3
  8.9 0.2 maximum_select_fusion.1.refs_0_
  9.1 1.4 collective-permute-start.1
  10.6 3.7 %collective-permute-start.4 = (bf16[24,8192]{1,0:T(8,128)(2,1)S(1)}, bf16[24,8192]{1,0:T(8,128)(2,1)S(1)}, u32[]{:S(2)}, u32[]{:S(2)}) collective-permute-start(bf16[24,8192]{1,0:T(8,128)(2,1)S(1)} %maximum_select_fusion.2.refs_0_), channel_id=1, source_target_pairs={{0,64},{8,72},{16,80},{24,88},{32,96},{40,104},{48,112},{56,120},{... | collective-permute-start | bytes 1179656 | tf_op jit(solution)/shard_map/ppermute | solution.py:47
  14.4 0.8 add_convert_fusion.hot3
  15.2 14.5 %weigh.1 = (bf16[16,256,1024]{2,1,0:T(8,128)(2,1)}, bf16[16,256,1024]{2,1,0:T(8,128)(2,1)}, bf16[64,16384]{1,0:T(8,128)(2,1)}) custom-call(s32[1]{0:T(128)} %bitcast.1.core, bf16[256,32768]{1,0:T(8,128)(2,1)} %give.1, bf16[256,32768]{1,0:T(8,128)(2,1)} %give.1, bf16[256,96]{1,0:T(8,128)(2,1)} %add_convert_fusion.hot3, f32[32,16384]{1,0:T(8,128)} %contrast.1, ...), custom_call_target="tpu_custom_call" | custom-call | flops 1024 | bytes 1024 | tf_op jit(solution)/shard_map/weigh/pallas_call | solution.py:89
  29.7 0.9 collective-permute-start.10
  30.6 2.7 %collective-permute-start.6 = (bf16[24,8192]{1,0:T(8,128)(2,1)S(1)}, bf16[24,8192]{1,0:T(8,128)(2,1)S(1)}, u32[]{:S(2)}, u32[]{:S(2)}) collective-permute-start(bf16[24,8192]{1,0:T(8,128)(2,1)S(1)} %collective-permute-done.1.refs_1_), channel_id=1, source_target_pairs={{0,48},{8,56},{16,0},{24,8},{32,16},{40,24},{48,32},{56,40},{64,11... | collective-permute-start | bytes 1179656 | tf_op jit(solution)/shard_map/ppermute | solution.py:43
  33.3 9.3 %collective-permute-done.8.refs_4_ = bf16[24,8192]{1,0:T(8,128)(2,1)} collective-permute-done((bf16[24,8192]{1,0:T(8,128)(2,1)S(1)}, bf16[24,8192]{1,0:T(8,128)(2,1)}, u32[]{:S(2)}, u32[]{:S(2)}) %collective-permute-start.8) | collective-permute-done | bytes 393248 | tf_op jit(solution)/shard_map/ppermute | solution.py:39
  42.6 2.2 %collective-permute-start.15 = (bf16[24,8192]{1,0:T(8,128)(2,1)S(1)}, bf16[24,8192]{1,0:T(8,128)(2,1)S(1)}, u32[]{:S(2)}, u32[]{:S(2)}) collective-permute-start(bf16[24,8192]{1,0:T(8,128)(2,1)S(1)} %collective-permute-done.4.refs_3_), channel_id=1, source_target_pairs={{0,48},{8,56},{16,0},{24,8},{32,16},{40,24},{48,32},{56,40},{64,11... | collective-permute-start | bytes 1179656 | tf_op jit(solution)/shard_map/ppermute | solution.py:43
  44.9 2.7 %collective-permute-start.11 = (bf16[24,8192]{1,0:T(8,128)(2,1)S(1)}, bf16[24,8192]{1,0:T(8,128)(2,1)S(1)}, u32[]{:S(2)}, u32[]{:S(2)}) collective-permute-start(bf16[24,8192]{1,0:T(8,128)(2,1)S(1)} %collective-permute-done.5.refs_3_), channel_id=1, source_target_pairs={{0,48},{8,56},{16,0},{24,8},{32,16},{40,24},{48,32},{56,40},{64,11... | collective-permute-start | bytes 1179656 | tf_op jit(solution)/shard_map/ppermute | solution.py:43
  47.6 6.6 %collective-permute-done.13.refs_7_ = bf16[24,8192]{1,0:T(8,128)(2,1)} collective-permute-done((bf16[24,8192]{1,0:T(8,128)(2,1)}, bf16[24,8192]{1,0:T(8,128)(2,1)}, u32[]{:S(2)}, u32[]{:S(2)}) %collective-permute-start.13) | collective-permute-done | bytes 393248 | tf_op jit(solution)/shard_map/ppermute | solution.py:47
  54.2 0.3 collective-permute-start.14
  54.7 0.6 collective-permute-done.16.refs_6_
  55.3 7.9 %score.2.refs_12_ = f32[192,512]{1,0:T(8,128)S(1)} custom-call(bf16[24,8192]{1,0:T(8,128)(2,1)S(1)} %maximum_select_fusion.2.refs_0_, bf16[24,8192]{1,0:T(8,128)(2,1)S(1)} %collective-permute-done.9.refs_1_, bf16[24,8192]{1,0:T(8,128)(2,1)S(1)} %collective-permute-done.7.refs_2_, bf16[24,8192]{1,0:T(8,128)(2,1)S(1)} %collective-permute-done.4.refs_3_, ...), custom_call_target="tpu_custom_call" | custom-call | flops 1024 | bytes 1024 | tf_op jit(solution)/shard_map/score/pallas_call | solution.py:190
  63.3 1.3 collective-permute-done.14.refs_7_
  64.6 7.8 %score.3.mine = f32[192,512]{1,0:T(8,128)S(1)} custom-call(bf16[24,8192]{1,0:T(8,128)(2,1)S(1)} %maximum_select_fusion.1.refs_0_, bf16[24,8192]{1,0:T(8,128)(2,1)S(1)} %collective-permute-done.1.refs_1_, bf16[24,8192]{1,0:T(8,128)(2,1)S(1)} %collective-permute-done.2.refs_2_, bf16[24,8192]{1,0:T(8,128)(2,1)S(1)} %collective-permute-done.5.refs_3_, ...), custom_call_target="tpu_custom_call" | custom-call | flops 1024 | bytes 1024 | tf_op jit(solution)/shard_map/score/pallas_call | solution.py:190
  72.4 3.1 %collective-permute-start.17 = (f32[192,512]{1,0:T(8,128)S(1)}, f32[192,512]{1,0:T(8,128)S(1)}, u32[]{:S(2)}, u32[]{:S(2)}) collective-permute-start(f32[192,512]{1,0:T(8,128)S(1)} %score.3.mine), channel_id=1, source_target_pairs={{0,8},{8,0},{16,24},{24,16},{32,40},{40,32},{48,56},{56,48},{64,72... | collective-permute-start | bytes 1179656 | tf_op jit(solution)/shard_map/ppermute | solution.py:51
  75.7 1.1 collective-permute-done.17.recv
  76.8 0.1 stat.1
  76.9 0.8 collective-permute-start.18
  77.8 1.7 %collective-permute-done.18.refs_1_ = f32[2,512]{1,0:T(2,128)S(1)} collective-permute-done((f32[2,512]{1,0:T(2,128)S(1)}, f32[2,512]{1,0:T(2,128)S(1)}, u32[]{:S(2)}, u32[]{:S(2)}) %collective-permute-start.18) | collective-permute-done | bytes 4128 | tf_op jit(solution)/shard_map/ppermute | solution.py:409
  79.5 1.4 collective-permute-start.19
  80.9 2.6 %collective-permute-start.20 = (f32[2,512]{1,0:T(2,128)S(1)}, f32[2,512]{1,0:T(2,128)S(1)}, u32[]{:S(2)}, u32[]{:S(2)}) collective-permute-start(f32[2,512]{1,0:T(2,128)S(1)} %merge.1.refs_3_), channel_id=1, source_target_pairs={{0,2},{1,3},{2,0},{3,1},{4,6},{5,7},{6,4},{7,5},{8,10},{9,11},{10,... | collective-permute-start | bytes 12296 | tf_op jit(solution)/shard_map/ppermute | solution.py:411
  83.5 1.1 collective-permute-start.21
  84.8 1.1 collective-permute-done.21.refs_6_
  86.0 0.3 chance.1
  86.3 4.5 %back.2 = (bf16[24,8320]{1,0:T(8,128)(2,1)S(1)}, bf16[24,8320]{1,0:T(8,128)(2,1)S(1)}, bf16[24,8320]{1,0:T(8,128)(2,1)S(1)}, bf16[24,8320]{1,0:T(8,128)(2,1)S(1)...) custom-call(bf16[192,512]{1,0:T(8,128)(2,1)S(1)} %get-tuple-element., ...), custom_call_target="tpu_custom_call" | custom-call | flops 1024 | bytes 1024 | tf_op jit(solution)/shard_map/back/pallas_call | solution.py:287
  90.8 2.0 %collective-permute-start.22 = (bf16[24,8320]{1,0:T(8,128)(2,1)S(1)}, bf16[24,8320]{1,0:T(8,128)(2,1)S(1)}, u32[]{:S(2)}, u32[]{:S(2)}) collective-permute-start(bf16[24,8320]{1,0:T(8,128)(2,1)S(1)} %get-tuple-element.61), channel_id=1, source_target_pairs={{0,64},{8,72},{16,80},{24,88},{32,96},{40,104},{48,112},{56,120},{... | collective-permute-start | bytes 1198088 | tf_op jit(solution)/shard_map/ppermute | solution.py:47
  92.8 1.5 collective-permute-start.28
  94.3 4.5 %back.3 = (bf16[24,8192]{1,0:T(8,128)(2,1)S(1)}, bf16[24,8192]{1,0:T(8,128)(2,1)S(1)}, bf16[24,8192]{1,0:T(8,128)(2,1)S(1)}, bf16[24,8192]{1,0:T(8,128)(2,1)S(1)...) custom-call(bf16[192,512]{1,0:T(8,128)(2,1)S(1)} %get-tuple-element., ...), custom_call_target="tpu_custom_call" | custom-call | flops 1024 | bytes 1024 | tf_op jit(solution)/shard_map/back/pallas_call | solution.py:287
  98.8 1.1 collective-permute-start.30
  99.9 2.1 %collective-permute-start.33 = (bf16[24,8192]{1,0:T(8,128)(2,1)S(1)}, bf16[24,8192]{1,0:T(8,128)(2,1)S(1)}, u32[]{:S(2)}, u32[]{:S(2)}) collective-permute-start(bf16[24,8192]{1,0:T(8,128)(2,1)S(1)} %get-tuple-element.76), channel_id=1, source_target_pairs={{0,48},{8,56},{16,0},{24,8},{32,16},{40,24},{48,32},{56,40},{64,11... | collective-permute-start | bytes 1179656 | tf_op jit(solution)/shard_map/ppermute | solution.py:43
  102.0 0.2 add.49
  102.4 1.5 collective-permute-start.23
  103.8 4.2 %collective-permute-done.30.refs_1_ = bf16[24,8192]{1,0:T(8,128)(2,1)S(1)} collective-permute-done((bf16[24,8192]{1,0:T(8,128)(2,1)S(1)}, bf16[24,8192]{1,0:T(8,128)(2,1)S(1)}, u32[]{:S(2)}, u32[]{:S(2)}) %collective-permute-start.30) | collective-permute-done | bytes 393248 | tf_op jit(solution)/shard_map/ppermute | solution.py:47
  108.2 0.3 collective-permute-start.31
  108.5 0.6 collective-permute-done.33.refs_1_
  109.1 2.0 %collective-permute-start.34 = (bf16[24,8192]{1,0:T(8,128)(2,1)S(1)}, bf16[24,8192]{1,0:T(8,128)(2,1)S(1)}, u32[]{:S(2)}, u32[]{:S(2)}) collective-permute-start(bf16[24,8192]{1,0:T(8,128)(2,1)S(1)} %get-tuple-element.77), channel_id=1, source_target_pairs={{0,48},{8,56},{16,0},{24,8},{32,16},{40,24},{48,32},{56,40},{64,11... | collective-permute-start | bytes 1179656 | tf_op jit(solution)/shard_map/ppermute | solution.py:43
  111.1 0.3 add.51
  111.5 2.9 %collective-permute-start.29 = (bf16[24,8320]{1,0:T(8,128)(2,1)S(1)}, bf16[24,8320]{1,0:T(8,128)(2,1)S(1)}, u32[]{:S(2)}, u32[]{:S(2)}) collective-permute-start(bf16[24,8320]{1,0:T(8,128)(2,1)S(1)} %add.51), channel_id=1, source_target_pairs={{0,64},{8,72},{16,80},{24,88},{32,96},{40,104},{48,112},{56,120},{... | collective-permute-start | bytes 1198088 | tf_op jit(solution)/shard_map/ppermute | solution.py:47
  114.4 3.3 %collective-permute-done.26.refs_1_ = bf16[24,8320]{1,0:T(8,128)(2,1)S(1)} collective-permute-done((bf16[24,8320]{1,0:T(8,128)(2,1)S(1)}, bf16[24,8320]{1,0:T(8,128)(2,1)S(1)}, u32[]{:S(2)}, u32[]{:S(2)}) %collective-permute-start.26) | collective-permute-done | bytes 399392 | tf_op jit(solution)/shard_map/ppermute | solution.py:43
  117.7 0.2 add.50
  117.9 0.5 collective-permute-start.27
  118.4 0.1 add.55
  118.5 2.3 %collective-permute-done.31.refs_1_ = bf16[24,8192]{1,0:T(8,128)(2,1)S(1)} collective-permute-done((bf16[24,8192]{1,0:T(8,128)(2,1)S(1)}, bf16[24,8192]{1,0:T(8,128)(2,1)S(1)}, u32[]{:S(2)}, u32[]{:S(2)}) %collective-permute-start.31) | collective-permute-done | bytes 393248 | tf_op jit(solution)/shard_map/ppermute | solution.py:39
  120.8 1.9 %collective-permute-start.35 = (bf16[24,8192]{1,0:T(8,128)(2,1)S(1)}, bf16[24,8192]{1,0:T(8,128)(2,1)S(1)}, u32[]{:S(2)}, u32[]{:S(2)}) collective-permute-start(bf16[24,8192]{1,0:T(8,128)(2,1)S(1)} %add.55), channel_id=1, source_target_pairs={{0,64},{8,72},{16,80},{24,88},{32,96},{40,104},{48,112},{56,120},{... | collective-permute-start | bytes 1179656 | tf_op jit(solution)/shard_map/ppermute | solution.py:47
  122.8 3.3 %collective-permute-done.34.refs_2_ = bf16[24,8192]{1,0:T(8,128)(2,1)S(1)} collective-permute-done((bf16[24,8192]{1,0:T(8,128)(2,1)S(1)}, bf16[24,8192]{1,0:T(8,128)(2,1)S(1)}, u32[]{:S(2)}, u32[]{:S(2)}) %collective-permute-start.34) | collective-permute-done | bytes 393248 | tf_op jit(solution)/shard_map/ppermute | solution.py:43
  126.1 1.2 fusion.2
  127.3 6.1 %collective-permute-done.35.refs_3_ = bf16[24,8192]{1,0:T(8,128)(2,1)S(1)} collective-permute-done((bf16[24,8192]{1,0:T(8,128)(2,1)S(1)}, bf16[24,8192]{1,0:T(8,128)(2,1)S(1)}, u32[]{:S(2)}, u32[]{:S(2)}) %collective-permute-start.35) | collective-permute-done | bytes 393248 | tf_op jit(solution)/shard_map/ppermute | solution.py:47
  133.4 3.4 %collective-permute-done.32.refs_1_ = bf16[24,8192]{1,0:T(8,128)(2,1)S(1)} collective-permute-done((bf16[24,8192]{1,0:T(8,128)(2,1)S(1)}, bf16[24,8192]{1,0:T(8,128)(2,1)S(1)}, u32[]{:S(2)}, u32[]{:S(2)}) %collective-permute-start.32) | collective-permute-done | bytes 393248 | tf_op jit(solution)/shard_map/ppermute | solution.py:39
  136.9 0.2 add.56
  137.1 0.4 add.52
  137.6 0.2 select_bitcast_fusion
  137.8 5.5 %collective-permute-start.36 = (bf16[12,16384]{1,0:T(8,128)(2,1)S(1)}, bf16[12,16384]{1,0:T(8,128)(2,1)S(1)}, u32[]{:S(2)}, u32[]{:S(2)}) collective-permute-start(bf16[12,16384]{1,0:T(8,128)(2,1)S(1)} %get-tuple-element.91), channel_id=1, source_target_pairs={{0,8},{8,0},{16,24},{24,16},{32,40},{40,32},{48,56},{56,48},{64,72... | collective-permute-start | bytes 1179656 | tf_op jit(solution)/shard_map/ppermute | solution.py:51
  143.4 1.2 convolution_bitcast_fusion
  144.6 1.7 %copy.15 = f32[1,12,16384]{2,0,1:T(1,128)} copy(f32[1,12,16384]{2,1,0:T(8,128)S(1)} %convolution_bitcast_fusion) | data formatting | bytes 1572864
  146.3 1.3 maximum_select_fusion
  (55 shorter events, 1.5 us)
Async XLA Ops:
  0.6 7.3 %copy-start.1 = (s32[256]{0:T(256)S(1)}, s32[256]{0:T(256)}, u32[]{:S(2)}) copy-start(s32[256]{0:T(256)} %param.7) | copy-start | bytes 3076
  1.9 3.0 %collective-permute-start = (bf16[12,16384]{1,0:T(8,128)(2,1)S(1)}, bf16[12,16384]{1,0:T(8,128)(2,1)S(1)}, u32[]{:S(2)}, u32[]{:S(2)}) collective-permute-start(bf16[12,16384]{1,0:T(8,128)(2,1)S(1)} %get-tuple-element.89), channel_id=1, source_target_pairs={{0,8},{8,0},{16,24},{24,16},{32,40},{40,32},{48,56},{56,48},{64,72... | collective-permute-start | bytes 1179656 | tf_op jit(solution)/shard_map/ppermute | solution.py:51
  5.2 24.4 %collective-permute-start.7 = (bf16[24,8192]{1,0:T(8,128)(2,1)S(1)}, bf16[24,8192]{1,0:T(8,128)(2,1)S(1)}, u32[]{:S(2)}, u32[]{:S(2)}) collective-permute-start(bf16[24,8192]{1,0:T(8,128)(2,1)S(1)} %maximum_select_fusion.2.refs_0_), channel_id=1, source_target_pairs={{0,16},{8,24},{16,32},{24,40},{32,48},{40,56},{48,0},{56,8},{64,80... | collective-permute-start | bytes 1179656 | tf_op jit(solution)/shard_map/ppermute | solution.py:39
  6.6 23.1 %collective-permute-start.9 = (bf16[24,8192]{1,0:T(8,128)(2,1)S(1)}, bf16[24,8192]{1,0:T(8,128)(2,1)S(1)}, u32[]{:S(2)}, u32[]{:S(2)}) collective-permute-start(bf16[24,8192]{1,0:T(8,128)(2,1)S(1)} %maximum_select_fusion.2.refs_0_), channel_id=1, source_target_pairs={{0,48},{8,56},{16,0},{24,8},{32,16},{40,24},{48,32},{56,40},{64,11... | collective-permute-start | bytes 1179656 | tf_op jit(solution)/shard_map/ppermute | solution.py:43
  8.0 2.7 %collective-permute-start.3 = (s32[256]{0:T(256)S(1)}, s32[256]{0:T(256)S(1)}, u32[]{:S(2)}, u32[]{:S(2)}) collective-permute-start(s32[256]{0:T(256)S(1)} %copy-done.1), channel_id=1, source_target_pairs={{0,8},{8,0},{16,24},{24,16},{32,40},{40,32},{48,56},{56,48},{64,72... | collective-permute-start | bytes 3080 | tf_op jit(solution)/shard_map/ppermute | solution.py:51
  9.1 20.6 %collective-permute-start.1 = (bf16[24,8192]{1,0:T(8,128)(2,1)S(1)}, bf16[24,8192]{1,0:T(8,128)(2,1)S(1)}, u32[]{:S(2)}, u32[]{:S(2)}) collective-permute-start(bf16[24,8192]{1,0:T(8,128)(2,1)S(1)} %maximum_select_fusion.1.refs_0_), channel_id=1, source_target_pairs={{0,48},{8,56},{16,0},{24,8},{32,16},{40,24},{48,32},{56,40},{64,11... | collective-permute-start | bytes 1179656 | tf_op jit(solution)/shard_map/ppermute | solution.py:43
  10.5 19.2 %collective-permute-start.2 = (bf16[24,8192]{1,0:T(8,128)(2,1)S(1)}, bf16[24,8192]{1,0:T(8,128)(2,1)S(1)}, u32[]{:S(2)}, u32[]{:S(2)}) collective-permute-start(bf16[24,8192]{1,0:T(8,128)(2,1)S(1)} %maximum_select_fusion.1.refs_0_), channel_id=1, source_target_pairs={{0,16},{8,24},{16,32},{24,40},{32,48},{40,56},{48,0},{56,8},{64,80... | collective-permute-start | bytes 1179656 | tf_op jit(solution)/shard_map/ppermute | solution.py:39
  10.6 19.1 %collective-permute-start.4 = (bf16[24,8192]{1,0:T(8,128)(2,1)S(1)}, bf16[24,8192]{1,0:T(8,128)(2,1)S(1)}, u32[]{:S(2)}, u32[]{:S(2)}) collective-permute-start(bf16[24,8192]{1,0:T(8,128)(2,1)S(1)} %maximum_select_fusion.2.refs_0_), channel_id=1, source_target_pairs={{0,64},{8,72},{16,80},{24,88},{32,96},{40,104},{48,112},{56,120},{... | collective-permute-start | bytes 1179656 | tf_op jit(solution)/shard_map/ppermute | solution.py:47
  29.7 15.2 %collective-permute-start.10 = (bf16[16,256,1024]{2,1,0:T(8,128)(2,1)}, bf16[16,256,1024]{2,1,0:T(8,128)(2,1)}, u32[]{:S(2)}, u32[]{:S(2)}) collective-permute-start(bf16[16,256,1024]{2,1,0:T(8,128)(2,1)} %get-tuple-element.47), channel_id=1, source_target_pairs={{0,8},{8,0},{16,24},{24,16},{32,40},{40,32},{48,56},{56,48},{64,72... | collective-permute-start | bytes 25165832 | tf_op jit(solution)/shard_map/ppermute | solution.py:51
  30.6 12.0 %collective-permute-start.8 = (bf16[24,8192]{1,0:T(8,128)(2,1)S(1)}, bf16[24,8192]{1,0:T(8,128)(2,1)}, u32[]{:S(2)}, u32[]{:S(2)}) collective-permute-start(bf16[24,8192]{1,0:T(8,128)(2,1)S(1)} %collective-permute-done.7.refs_2_), channel_id=1, source_target_pairs={{0,16},{8,24},{16,32},{24,40},{32,48},{40,56},{48,0},{56,8},{64,80... | collective-permute-start | bytes 1179656 | tf_op jit(solution)/shard_map/ppermute | solution.py:39
  30.6 12.0 %collective-permute-start.6 = (bf16[24,8192]{1,0:T(8,128)(2,1)S(1)}, bf16[24,8192]{1,0:T(8,128)(2,1)S(1)}, u32[]{:S(2)}, u32[]{:S(2)}) collective-permute-start(bf16[24,8192]{1,0:T(8,128)(2,1)S(1)} %collective-permute-done.1.refs_1_), channel_id=1, source_target_pairs={{0,48},{8,56},{16,0},{24,8},{32,16},{40,24},{48,32},{56,40},{64,11... | collective-permute-start | bytes 1179656 | tf_op jit(solution)/shard_map/ppermute | solution.py:43
  33.3 11.6 %collective-permute-start.5 = (bf16[24,8192]{1,0:T(8,128)(2,1)S(1)}, bf16[24,8192]{1,0:T(8,128)(2,1)S(1)}, u32[]{:S(2)}, u32[]{:S(2)}) collective-permute-start(bf16[24,8192]{1,0:T(8,128)(2,1)S(1)} %maximum_select_fusion.1.refs_0_), channel_id=1, source_target_pairs={{0,64},{8,72},{16,80},{24,88},{32,96},{40,104},{48,112},{56,120},{... | collective-permute-start | bytes 1179656 | tf_op jit(solution)/shard_map/ppermute | solution.py:47
  42.6 11.6 %collective-permute-start.13 = (bf16[24,8192]{1,0:T(8,128)(2,1)}, bf16[24,8192]{1,0:T(8,128)(2,1)}, u32[]{:S(2)}, u32[]{:S(2)}) collective-permute-start(bf16[24,8192]{1,0:T(8,128)(2,1)} %collective-permute-done.8.refs_4_), channel_id=1, source_target_pairs={{0,64},{8,72},{16,80},{24,88},{32,96},{40,104},{48,112},{56,120},{... | collective-permute-start | bytes 1179656 | tf_op jit(solution)/shard_map/ppermute | solution.py:47
  42.6 12.1 %collective-permute-start.15 = (bf16[24,8192]{1,0:T(8,128)(2,1)S(1)}, bf16[24,8192]{1,0:T(8,128)(2,1)S(1)}, u32[]{:S(2)}, u32[]{:S(2)}) collective-permute-start(bf16[24,8192]{1,0:T(8,128)(2,1)S(1)} %collective-permute-done.4.refs_3_), channel_id=1, source_target_pairs={{0,48},{8,56},{16,0},{24,8},{32,16},{40,24},{48,32},{56,40},{64,11... | collective-permute-start | bytes 1179656 | tf_op jit(solution)/shard_map/ppermute | solution.py:43
  44.9 10.5 %collective-permute-start.16 = (bf16[24,8192]{1,0:T(8,128)(2,1)S(1)}, bf16[24,8192]{1,0:T(8,128)(2,1)S(1)}, u32[]{:S(2)}, u32[]{:S(2)}) collective-permute-start(bf16[24,8192]{1,0:T(8,128)(2,1)S(1)} %collective-permute-done.4.refs_3_), channel_id=1, source_target_pairs={{0,16},{8,24},{16,32},{24,40},{32,48},{40,56},{48,0},{56,8},{64,80... | collective-permute-start | bytes 1179656 | tf_op jit(solution)/shard_map/ppermute | solution.py:39
  44.9 19.7 %collective-permute-start.11 = (bf16[24,8192]{1,0:T(8,128)(2,1)S(1)}, bf16[24,8192]{1,0:T(8,128)(2,1)S(1)}, u32[]{:S(2)}, u32[]{:S(2)}) collective-permute-start(bf16[24,8192]{1,0:T(8,128)(2,1)S(1)} %collective-permute-done.5.refs_3_), channel_id=1, source_target_pairs={{0,48},{8,56},{16,0},{24,8},{32,16},{40,24},{48,32},{56,40},{64,11... | collective-permute-start | bytes 1179656 | tf_op jit(solution)/shard_map/ppermute | solution.py:43
  47.6 17.0 %collective-permute-start.12 = (bf16[24,8192]{1,0:T(8,128)(2,1)S(1)}, bf16[24,8192]{1,0:T(8,128)(2,1)S(1)}, u32[]{:S(2)}, u32[]{:S(2)}) collective-permute-start(bf16[24,8192]{1,0:T(8,128)(2,1)S(1)} %collective-permute-done.5.refs_3_), channel_id=1, source_target_pairs={{0,16},{8,24},{16,32},{24,40},{32,48},{40,56},{48,0},{56,8},{64,80... | collective-permute-start | bytes 1179656 | tf_op jit(solution)/shard_map/ppermute | solution.py:39
  54.2 10.4 %collective-permute-start.14 = (bf16[24,8192]{1,0:T(8,128)(2,1)S(1)}, bf16[24,8192]{1,0:T(8,128)(2,1)S(1)}, u32[]{:S(2)}, u32[]{:S(2)}) collective-permute-start(bf16[24,8192]{1,0:T(8,128)(2,1)S(1)} %collective-permute-done.6.refs_4_), channel_id=1, source_target_pairs={{0,64},{8,72},{16,80},{24,88},{32,96},{40,104},{48,112},{56,120},{... | collective-permute-start | bytes 1179656 | tf_op jit(solution)/shard_map/ppermute | solution.py:47
  63.2 12.2 %copy-start.2 = (s32[512]{0:T(512)S(1)}, s32[512]{0:T(512)}, u32[]{:S(2)}) copy-start(s32[512]{0:T(512)} %param.11) | copy-start | bytes 6148
  72.4 4.4 %collective-permute-start.17 = (f32[192,512]{1,0:T(8,128)S(1)}, f32[192,512]{1,0:T(8,128)S(1)}, u32[]{:S(2)}, u32[]{:S(2)}) collective-permute-start(f32[192,512]{1,0:T(8,128)S(1)} %score.3.mine), channel_id=1, source_target_pairs={{0,8},{8,0},{16,24},{24,16},{32,40},{40,32},{48,56},{56,48},{64,72... | collective-permute-start | bytes 1179656 | tf_op jit(solution)/shard_map/ppermute | solution.py:51
  76.9 2.5 %collective-permute-start.18 = (f32[2,512]{1,0:T(2,128)S(1)}, f32[2,512]{1,0:T(2,128)S(1)}, u32[]{:S(2)}, u32[]{:S(2)}) collective-permute-start(f32[2,512]{1,0:T(2,128)S(1)} %get-tuple-element.54.refs_0_), channel_id=1, source_target_pairs={{0,4},{1,5},{2,6},{3,7},{4,0},{5,1},{6,2},{7,3},{8,12},{9,13},{10,... | collective-permute-start | bytes 12296 | tf_op jit(solution)/shard_map/ppermute | solution.py:409
  79.5 5.2 %collective-permute-start.19 = (f32[2,512]{1,0:T(2,128)S(1)}, f32[2,512]{1,0:T(2,128)S(1)}, u32[]{:S(2)}, u32[]{:S(2)}) collective-permute-start(f32[2,512]{1,0:T(2,128)S(1)} %merge.1.refs_3_), channel_id=1, source_target_pairs={{0,1},{1,2},{2,3},{3,0},{4,5},{5,6},{6,7},{7,4},{8,9},{9,10},{10,1... | collective-permute-start | bytes 12296 | tf_op jit(solution)/shard_map/ppermute | solution.py:411
  80.9 4.0 %collective-permute-start.20 = (f32[2,512]{1,0:T(2,128)S(1)}, f32[2,512]{1,0:T(2,128)S(1)}, u32[]{:S(2)}, u32[]{:S(2)}) collective-permute-start(f32[2,512]{1,0:T(2,128)S(1)} %merge.1.refs_3_), channel_id=1, source_target_pairs={{0,2},{1,3},{2,0},{3,1},{4,6},{5,7},{6,4},{7,5},{8,10},{9,11},{10,... | collective-permute-start | bytes 12296 | tf_op jit(solution)/shard_map/ppermute | solution.py:411
  83.5 2.5 %collective-permute-start.21 = (f32[2,512]{1,0:T(2,128)S(1)}, f32[2,512]{1,0:T(2,128)S(1)}, u32[]{:S(2)}, u32[]{:S(2)}) collective-permute-start(f32[2,512]{1,0:T(2,128)S(1)} %merge.1.refs_3_), channel_id=1, source_target_pairs={{0,3},{1,0},{2,1},{3,2},{4,7},{5,4},{6,5},{7,6},{8,11},{9,8},{10,9... | collective-permute-start | bytes 12296 | tf_op jit(solution)/shard_map/ppermute | solution.py:411
  90.8 11.2 %collective-permute-start.22 = (bf16[24,8320]{1,0:T(8,128)(2,1)S(1)}, bf16[24,8320]{1,0:T(8,128)(2,1)S(1)}, u32[]{:S(2)}, u32[]{:S(2)}) collective-permute-start(bf16[24,8320]{1,0:T(8,128)(2,1)S(1)} %get-tuple-element.61), channel_id=1, source_target_pairs={{0,64},{8,72},{16,80},{24,88},{32,96},{40,104},{48,112},{56,120},{... | collective-permute-start | bytes 1198088 | tf_op jit(solution)/shard_map/ppermute | solution.py:47
  92.8 9.5 %collective-permute-start.25 = (bf16[24,8320]{1,0:T(8,128)(2,1)S(1)}, bf16[24,8320]{1,0:T(8,128)(2,1)S(1)}, u32[]{:S(2)}, u32[]{:S(2)}) collective-permute-start(bf16[24,8320]{1,0:T(8,128)(2,1)S(1)} %get-tuple-element.66), channel_id=1, source_target_pairs={{0,48},{8,56},{16,0},{24,8},{32,16},{40,24},{48,32},{56,40},{64,11... | collective-permute-start | bytes 1198088 | tf_op jit(solution)/shard_map/ppermute | solution.py:43
  92.8 15.3 %collective-permute-start.28 = (bf16[24,8320]{1,0:T(8,128)(2,1)S(1)}, bf16[24,8320]{1,0:T(8,128)(2,1)S(1)}, u32[]{:S(2)}, u32[]{:S(2)}) collective-permute-start(bf16[24,8320]{1,0:T(8,128)(2,1)S(1)} %get-tuple-element.69), channel_id=1, source_target_pairs={{0,16},{8,24},{16,32},{24,40},{32,48},{40,56},{48,0},{56,8},{64,80... | collective-permute-start | bytes 1198088 | tf_op jit(solution)/shard_map/ppermute | solution.py:39
  98.8 9.3 %collective-permute-start.30 = (bf16[24,8192]{1,0:T(8,128)(2,1)S(1)}, bf16[24,8192]{1,0:T(8,128)(2,1)S(1)}, u32[]{:S(2)}, u32[]{:S(2)}) collective-permute-start(bf16[24,8192]{1,0:T(8,128)(2,1)S(1)} %get-tuple-element.73), channel_id=1, source_target_pairs={{0,64},{8,72},{16,80},{24,88},{32,96},{40,104},{48,112},{56,120},{... | collective-permute-start | bytes 1179656 | tf_op jit(solution)/shard_map/ppermute | solution.py:47
  99.9 9.2 %collective-permute-start.33 = (bf16[24,8192]{1,0:T(8,128)(2,1)S(1)}, bf16[24,8192]{1,0:T(8,128)(2,1)S(1)}, u32[]{:S(2)}, u32[]{:S(2)}) collective-permute-start(bf16[24,8192]{1,0:T(8,128)(2,1)S(1)} %get-tuple-element.76), channel_id=1, source_target_pairs={{0,48},{8,56},{16,0},{24,8},{32,16},{40,24},{48,32},{56,40},{64,11... | collective-permute-start | bytes 1179656 | tf_op jit(solution)/shard_map/ppermute | solution.py:43
  102.3 15.4 %collective-permute-start.26 = (bf16[24,8320]{1,0:T(8,128)(2,1)S(1)}, bf16[24,8320]{1,0:T(8,128)(2,1)S(1)}, u32[]{:S(2)}, u32[]{:S(2)}) collective-permute-start(bf16[24,8320]{1,0:T(8,128)(2,1)S(1)} %add.49), channel_id=1, source_target_pairs={{0,48},{8,56},{16,0},{24,8},{32,16},{40,24},{48,32},{56,40},{64,11... | collective-permute-start | bytes 1198088 | tf_op jit(solution)/shard_map/ppermute | solution.py:43
  102.4 12.0 %collective-permute-start.23 = (bf16[24,8192]{1,0:T(8,128)(2,1)S(1)}, bf16[24,8192]{1,0:T(8,128)(2,1)S(1)}, u32[]{:S(2)}, u32[]{:S(2)}) collective-permute-start(bf16[24,8192]{1,0:T(8,128)(2,1)S(1)} %get-tuple-element.62), channel_id=1, source_target_pairs={{0,16},{8,24},{16,32},{24,40},{32,48},{40,56},{48,0},{56,8},{64,80... | collective-permute-start | bytes 1179656 | tf_op jit(solution)/shard_map/ppermute | solution.py:39
  108.2 12.6 %collective-permute-start.31 = (bf16[24,8192]{1,0:T(8,128)(2,1)S(1)}, bf16[24,8192]{1,0:T(8,128)(2,1)S(1)}, u32[]{:S(2)}, u32[]{:S(2)}) collective-permute-start(bf16[24,8192]{1,0:T(8,128)(2,1)S(1)} %add.53), channel_id=1, source_target_pairs={{0,16},{8,24},{16,32},{24,40},{32,48},{40,56},{48,0},{56,8},{64,80... | collective-permute-start | bytes 1179656 | tf_op jit(solution)/shard_map/ppermute | solution.py:39
  109.1 17.0 %collective-permute-start.34 = (bf16[24,8192]{1,0:T(8,128)(2,1)S(1)}, bf16[24,8192]{1,0:T(8,128)(2,1)S(1)}, u32[]{:S(2)}, u32[]{:S(2)}) collective-permute-start(bf16[24,8192]{1,0:T(8,128)(2,1)S(1)} %get-tuple-element.77), channel_id=1, source_target_pairs={{0,48},{8,56},{16,0},{24,8},{32,16},{40,24},{48,32},{56,40},{64,11... | collective-permute-start | bytes 1179656 | tf_op jit(solution)/shard_map/ppermute | solution.py:43
  111.5 25.6 %collective-permute-start.29 = (bf16[24,8320]{1,0:T(8,128)(2,1)S(1)}, bf16[24,8320]{1,0:T(8,128)(2,1)S(1)}, u32[]{:S(2)}, u32[]{:S(2)}) collective-permute-start(bf16[24,8320]{1,0:T(8,128)(2,1)S(1)} %add.51), channel_id=1, source_target_pairs={{0,64},{8,72},{16,80},{24,88},{32,96},{40,104},{48,112},{56,120},{... | collective-permute-start | bytes 1198088 | tf_op jit(solution)/shard_map/ppermute | solution.py:47
  114.4 22.7 %collective-permute-start.24 = (bf16[24,8320]{1,0:T(8,128)(2,1)S(1)}, bf16[24,8320]{1,0:T(8,128)(2,1)S(1)}, u32[]{:S(2)}, u32[]{:S(2)}) collective-permute-start(bf16[24,8320]{1,0:T(8,128)(2,1)S(1)} %get-tuple-element.63), channel_id=1, source_target_pairs={{0,16},{8,24},{16,32},{24,40},{32,48},{40,56},{48,0},{56,8},{64,80... | collective-permute-start | bytes 1198088 | tf_op jit(solution)/shard_map/ppermute | solution.py:39
  117.9 19.2 %collective-permute-start.27 = (bf16[24,8320]{1,0:T(8,128)(2,1)S(1)}, bf16[24,8320]{1,0:T(8,128)(2,1)S(1)}, u32[]{:S(2)}, u32[]{:S(2)}) collective-permute-start(bf16[24,8320]{1,0:T(8,128)(2,1)S(1)} %add.50), channel_id=1, source_target_pairs={{0,48},{8,56},{16,0},{24,8},{32,16},{40,24},{48,32},{56,40},{64,11... | collective-permute-start | bytes 1198088 | tf_op jit(solution)/shard_map/ppermute | solution.py:43
  120.8 12.6 %collective-permute-start.35 = (bf16[24,8192]{1,0:T(8,128)(2,1)S(1)}, bf16[24,8192]{1,0:T(8,128)(2,1)S(1)}, u32[]{:S(2)}, u32[]{:S(2)}) collective-permute-start(bf16[24,8192]{1,0:T(8,128)(2,1)S(1)} %add.55), channel_id=1, source_target_pairs={{0,64},{8,72},{16,80},{24,88},{32,96},{40,104},{48,112},{56,120},{... | collective-permute-start | bytes 1179656 | tf_op jit(solution)/shard_map/ppermute | solution.py:47
  126.1 10.8 %collective-permute-start.32 = (bf16[24,8192]{1,0:T(8,128)(2,1)S(1)}, bf16[24,8192]{1,0:T(8,128)(2,1)S(1)}, u32[]{:S(2)}, u32[]{:S(2)}) collective-permute-start(bf16[24,8192]{1,0:T(8,128)(2,1)S(1)} %add.54), channel_id=1, source_target_pairs={{0,16},{8,24},{16,32},{24,40},{32,48},{40,56},{48,0},{56,8},{64,80... | collective-permute-start | bytes 1179656 | tf_op jit(solution)/shard_map/ppermute | solution.py:39
  137.1 6.3 %copy-start = (f32[32,16384]{1,0:T(8,128)S(1)}, f32[32,16384]{1,0:T(8,128)}, u32[]{:S(2)}) copy-start(f32[32,16384]{1,0:T(8,128)} %contrast.1) | copy-start | bytes 6291460
  137.8 8.5 %collective-permute-start.36 = (bf16[12,16384]{1,0:T(8,128)(2,1)S(1)}, bf16[12,16384]{1,0:T(8,128)(2,1)S(1)}, u32[]{:S(2)}, u32[]{:S(2)}) collective-permute-start(bf16[12,16384]{1,0:T(8,128)(2,1)S(1)} %get-tuple-element.91), channel_id=1, source_target_pairs={{0,8},{8,0},{16,24},{24,16},{32,40},{40,32},{48,56},{56,48},{64,72... | collective-permute-start | bytes 1179656 | tf_op jit(solution)/shard_map/ppermute | solution.py:51

commit v5 on v4

--- a/solution.py
+++ b/solution.py
@@ -350,7 +350,10 @@
     mine = projections[0]
     low, high = mine[:, :half], mine[:, half:]
     got = to_core(jnp.where(first, high, low))
-    kept = jnp.where(first, low, high)
+    ids = jnp.arange(n_cls, dtype=jnp.int32)[None, :]
+    hot_own = (classes[:, None] == ids).astype(BF16)
+    hot3 = jnp.concatenate([hot_own] * 3, axis=1)
+    kept = tie(jnp.where(first, low, high), hot3)
     own_a, own_b = (
         jnp.where(
             first,
@@ -367,12 +370,9 @@
     fz_a, fz_b = tie(zz_a, x2_a, x2_b), tie(zz_b, x2_a, x2_b)
     zm_a, zp_a, z2_a = to_xp(fz_a), to_xm(fz_a), to_z(x2_a)
 
-    ids = jnp.arange(n_cls, dtype=jnp.int32)[None, :]
-    hot_own = (classes[:, None] == ids).astype(BF16)
     both_classes = jnp.concatenate([classes, sib_classes])
     hot = (both_classes[:, None] == ids).astype(F32)
     hot_wide = (both_classes[:, None] == jnp.arange(TAIL, dtype=jnp.int32)[None, :]).astype(BF16)
-    hot3 = jnp.concatenate([hot_own] * 3, axis=1)
     w_own, give, quads = weigh(tie(core.reshape(1), own_a, sib_classes), images, hot3, contrast, noise)
     w_sib = to_core(tie(give, xm_a, xm_b, xp_a, xp_b, zz_a))
     zm_b, zp_b, z2_b = to_xp(tie(fz_b, w_sib)), to_xm(tie(fz_b, w_sib)), to_z(tie(x2_b, z2_a, w_sib))

time: 148 us -> 147 us (level)
  no operation moved by 1% of the time
where the time goes in v5:
time: 147 us
  starting transfers between devices  50.2 us (34%)
  waiting for transfers between devices  45.3 us (31%)
  Pallas kernels  41.3 us (28%)
  other arithmetic  4.53 us (3%)
  matrix products  2.39 us (2%)
  local copies, waits for them, and re-layouts  1.96 us (1%)
    ppermute x8, waiting for transfers between devices, to_z(): return lax.ppermute(v, 'img', img_perm(1, 0, 0))  18.1 us
    pallas_call x2, Pallas kernels, score(): pl.pallas_call(functools.partial(score_kernel, len(parts), acc_in is not...  15.7 us
    ppermute x10, waiting for transfers between devices, to_xp(): return lax.ppermute(v, 'img', img_perm(0, 1, 0))  15.2 us
    ppermute x10, starting transfers between devices, to_xm(): return lax.ppermute(v, 'img', img_perm(0, -1, 0))  14.6 us
    pallas_call x1, Pallas kernels, weigh(): pl.pallas_call(weigh_kernel, grid_spec=pltpu.PrefetchScalarGridSpec(num_s...  14.4 us
    ppermute x8, starting transfers between devices, to_z(): return lax.ppermute(v, 'img', img_perm(1, 0, 0))  13 us
    ppermute x5, starting transfers between devices, to_core(): return lax.ppermute(v, 'img', img_perm(0, 0, 1))  11.9 us
    pallas_call x2, Pallas kernels, back(): pl.pallas_call(functools.partial(back_kernel, n_parts, nb, wide, tail), g...  8.98 us
  transfers between devices with their start and end apart: 37, of which 16 were waited for; matrix products, arithmetic and copies ran while one was open for 4% of the time, Pallas kernels for 19%

profile of v5, /device:TPU:1, one launch (start us, length us, event | category | flops | bytes accessed | tf_op | source)
XLA Modules:
  0.0 146.6 jit_solution(2751563403398566651)
XLA Ops:
  0.7 1.3 broadcast_select_fusion.2
  1.9 1.5 %collective-permute-start = (bf16[12,16384]{1,0:T(8,128)(2,1)S(1)}, bf16[12,16384]{1,0:T(8,128)(2,1)S(1)}, u32[]{:S(2)}, u32[]{:S(2)}) collective-permute-start(bf16[12,16384]{1,0:T(8,128)(2,1)S(1)} %get-tuple-element.91), channel_id=1, source_target_pairs={{0,8},{8,0},{16,24},{24,16},{32,40},{40,32},{48,56},{56,48},{64,72... | collective-permute-start | bytes 1179656 | tf_op jit(solution)/shard_map/ppermute | solution.py:51
  3.5 0.8 add_convert_fusion.hot3
  4.4 0.6 collective-permute-done
  5.0 0.2 maximum_select_fusion.2.refs_0_
  5.2 1.4 collective-permute-start.7
  6.6 1.4 collective-permute-start.9
  8.0 0.9 collective-permute-start.3
  8.9 0.2 maximum_select_fusion.1.refs_0_
  9.1 1.4 collective-permute-start.1
  10.6 3.7 %collective-permute-start.4 = (bf16[24,8192]{1,0:T(8,128)(2,1)S(1)}, bf16[24,8192]{1,0:T(8,128)(2,1)S(1)}, u32[]{:S(2)}, u32[]{:S(2)}) collective-permute-start(bf16[24,8192]{1,0:T(8,128)(2,1)S(1)} %maximum_select_fusion.2.refs_0_), channel_id=1, source_target_pairs={{0,64},{8,72},{16,80},{24,88},{32,96},{40,104},{48,112},{56,120},{... | collective-permute-start | bytes 1179656 | tf_op jit(solution)/shard_map/ppermute | solution.py:47
  14.3 14.4 %weigh.1 = (bf16[16,256,1024]{2,1,0:T(8,128)(2,1)}, bf16[16,256,1024]{2,1,0:T(8,128)(2,1)}, bf16[64,16384]{1,0:T(8,128)(2,1)}) custom-call(s32[1]{0:T(128)} %bitcast.1.core, bf16[256,32768]{1,0:T(8,128)(2,1)} %give.1, bf16[256,32768]{1,0:T(8,128)(2,1)} %give.1, bf16[256,96]{1,0:T(8,128)(2,1)} %add_convert_fusion.hot3, f32[32,16384]{1,0:T(8,128)} %contrast.1, ...), custom_call_target="tpu_custom_call" | custom-call | flops 1024 | bytes 1024 | tf_op jit(solution)/shard_map/weigh/pallas_call | solution.py:89
  28.8 0.9 collective-permute-start.10
  29.8 2.7 %collective-permute-start.6 = (bf16[24,8192]{1,0:T(8,128)(2,1)S(1)}, bf16[24,8192]{1,0:T(8,128)(2,1)S(1)}, u32[]{:S(2)}, u32[]{:S(2)}) collective-permute-start(bf16[24,8192]{1,0:T(8,128)(2,1)S(1)} %collective-permute-done.1.refs_1_), channel_id=1, source_target_pairs={{0,48},{8,56},{16,0},{24,8},{32,16},{40,24},{48,32},{56,40},{64,11... | collective-permute-start | bytes 1179656 | tf_op jit(solution)/shard_map/ppermute | solution.py:43
  32.4 0.4 collective-permute-start.5
  32.8 8.9 %collective-permute-done.8.refs_4_ = bf16[24,8192]{1,0:T(8,128)(2,1)} collective-permute-done((bf16[24,8192]{1,0:T(8,128)(2,1)S(1)}, bf16[24,8192]{1,0:T(8,128)(2,1)}, u32[]{:S(2)}, u32[]{:S(2)}) %collective-permute-start.8) | collective-permute-done | bytes 393248 | tf_op jit(solution)/shard_map/ppermute | solution.py:39
  41.7 0.4 collective-permute-start.13
  42.2 1.8 %collective-permute-start.15 = (bf16[24,8192]{1,0:T(8,128)(2,1)S(1)}, bf16[24,8192]{1,0:T(8,128)(2,1)S(1)}, u32[]{:S(2)}, u32[]{:S(2)}) collective-permute-start(bf16[24,8192]{1,0:T(8,128)(2,1)S(1)} %collective-permute-done.4.refs_3_), channel_id=1, source_target_pairs={{0,48},{8,56},{16,0},{24,8},{32,16},{40,24},{48,32},{56,40},{64,11... | collective-permute-start | bytes 1179656 | tf_op jit(solution)/shard_map/ppermute | solution.py:43
  44.0 2.7 %collective-permute-start.11 = (bf16[24,8192]{1,0:T(8,128)(2,1)S(1)}, bf16[24,8192]{1,0:T(8,128)(2,1)S(1)}, u32[]{:S(2)}, u32[]{:S(2)}) collective-permute-start(bf16[24,8192]{1,0:T(8,128)(2,1)S(1)} %collective-permute-done.5.refs_3_), channel_id=1, source_target_pairs={{0,48},{8,56},{16,0},{24,8},{32,16},{40,24},{48,32},{56,40},{64,11... | collective-permute-start | bytes 1179656 | tf_op jit(solution)/shard_map/ppermute | solution.py:43
  46.7 6.6 %collective-permute-done.13.refs_7_ = bf16[24,8192]{1,0:T(8,128)(2,1)} collective-permute-done((bf16[24,8192]{1,0:T(8,128)(2,1)}, bf16[24,8192]{1,0:T(8,128)(2,1)}, u32[]{:S(2)}, u32[]{:S(2)}) %collective-permute-start.13) | collective-permute-done | bytes 393248 | tf_op jit(solution)/shard_map/ppermute | solution.py:47
  53.3 0.4 collective-permute-start.14
  53.9 0.5 collective-permute-done.16.refs_6_
  54.5 7.9 %score.2.refs_12_ = f32[192,512]{1,0:T(8,128)S(1)} custom-call(bf16[24,8192]{1,0:T(8,128)(2,1)S(1)} %maximum_select_fusion.2.refs_0_, bf16[24,8192]{1,0:T(8,128)(2,1)S(1)} %collective-permute-done.9.refs_1_, bf16[24,8192]{1,0:T(8,128)(2,1)S(1)} %collective-permute-done.7.refs_2_, bf16[24,8192]{1,0:T(8,128)(2,1)S(1)} %collective-permute-done.4.refs_3_, ...), custom_call_target="tpu_custom_call" | custom-call | flops 1024 | bytes 1024 | tf_op jit(solution)/shard_map/score/pallas_call | solution.py:190
  62.4 1.3 collective-permute-done.14.refs_7_
  63.7 7.8 %score.3.mine = f32[192,512]{1,0:T(8,128)S(1)} custom-call(bf16[24,8192]{1,0:T(8,128)(2,1)S(1)} %maximum_select_fusion.1.refs_0_, bf16[24,8192]{1,0:T(8,128)(2,1)S(1)} %collective-permute-done.1.refs_1_, bf16[24,8192]{1,0:T(8,128)(2,1)S(1)} %collective-permute-done.2.refs_2_, bf16[24,8192]{1,0:T(8,128)(2,1)S(1)} %collective-permute-done.5.refs_3_, ...), custom_call_target="tpu_custom_call" | custom-call | flops 1024 | bytes 1024 | tf_op jit(solution)/shard_map/score/pallas_call | solution.py:190
  71.5 3.1 %collective-permute-start.17 = (f32[192,512]{1,0:T(8,128)S(1)}, f32[192,512]{1,0:T(8,128)S(1)}, u32[]{:S(2)}, u32[]{:S(2)}) collective-permute-start(f32[192,512]{1,0:T(8,128)S(1)} %score.3.mine), channel_id=1, source_target_pairs={{0,8},{8,0},{16,24},{24,16},{32,40},{40,32},{48,56},{56,48},{64,72... | collective-permute-start | bytes 1179656 | tf_op jit(solution)/shard_map/ppermute | solution.py:51
  74.9 1.1 collective-permute-done.17.recv
  76.1 0.8 collective-permute-start.18
  76.9 1.7 %collective-permute-done.18.refs_1_ = f32[2,512]{1,0:T(2,128)S(1)} collective-permute-done((f32[2,512]{1,0:T(2,128)S(1)}, f32[2,512]{1,0:T(2,128)S(1)}, u32[]{:S(2)}, u32[]{:S(2)}) %collective-permute-start.18) | collective-permute-done | bytes 4128 | tf_op jit(solution)/shard_map/ppermute | solution.py:409
  78.6 1.4 collective-permute-start.19
  80.0 2.6 %collective-permute-start.20 = (f32[2,512]{1,0:T(2,128)S(1)}, f32[2,512]{1,0:T(2,128)S(1)}, u32[]{:S(2)}, u32[]{:S(2)}) collective-permute-start(f32[2,512]{1,0:T(2,128)S(1)} %merge.1.refs_3_), channel_id=1, source_target_pairs={{0,2},{1,3},{2,0},{3,1},{4,6},{5,7},{6,4},{7,5},{8,10},{9,11},{10,... | collective-permute-start | bytes 12296 | tf_op jit(solution)/shard_map/ppermute | solution.py:411
  82.6 1.1 collective-permute-start.21
  83.9 1.1 collective-permute-done.21.refs_6_
  85.1 0.3 chance.1
  85.4 4.5 %back.2 = (bf16[24,8320]{1,0:T(8,128)(2,1)S(1)}, bf16[24,8320]{1,0:T(8,128)(2,1)S(1)}, bf16[24,8320]{1,0:T(8,128)(2,1)S(1)}, bf16[24,8320]{1,0:T(8,128)(2,1)S(1)...) custom-call(bf16[192,512]{1,0:T(8,128)(2,1)S(1)} %get-tuple-element., ...), custom_call_target="tpu_custom_call" | custom-call | flops 1024 | bytes 1024 | tf_op jit(solution)/shard_map/back/pallas_call | solution.py:287
  89.9 2.0 %collective-permute-start.22 = (bf16[24,8320]{1,0:T(8,128)(2,1)S(1)}, bf16[24,8320]{1,0:T(8,128)(2,1)S(1)}, u32[]{:S(2)}, u32[]{:S(2)}) collective-permute-start(bf16[24,8320]{1,0:T(8,128)(2,1)S(1)} %get-tuple-element.63), channel_id=1, source_target_pairs={{0,64},{8,72},{16,80},{24,88},{32,96},{40,104},{48,112},{56,120},{... | collective-permute-start | bytes 1198088 | tf_op jit(solution)/shard_map/ppermute | solution.py:47
  92.0 1.5 collective-permute-start.28
  93.4 4.5 %back.3 = (bf16[24,8192]{1,0:T(8,128)(2,1)S(1)}, bf16[24,8192]{1,0:T(8,128)(2,1)S(1)}, bf16[24,8192]{1,0:T(8,128)(2,1)S(1)}, bf16[24,8192]{1,0:T(8,128)(2,1)S(1)...) custom-call(bf16[192,512]{1,0:T(8,128)(2,1)S(1)} %get-tuple-element., ...), custom_call_target="tpu_custom_call" | custom-call | flops 1024 | bytes 1024 | tf_op jit(solution)/shard_map/back/pallas_call | solution.py:287
  97.9 1.1 collective-permute-start.30
  99.0 2.2 %collective-permute-start.33 = (bf16[24,8192]{1,0:T(8,128)(2,1)S(1)}, bf16[24,8192]{1,0:T(8,128)(2,1)S(1)}, u32[]{:S(2)}, u32[]{:S(2)}) collective-permute-start(bf16[24,8192]{1,0:T(8,128)(2,1)S(1)} %get-tuple-element.78), channel_id=1, source_target_pairs={{0,48},{8,56},{16,0},{24,8},{32,16},{40,24},{48,32},{56,40},{64,11... | collective-permute-start | bytes 1179656 | tf_op jit(solution)/shard_map/ppermute | solution.py:43
  101.2 0.2 add.49
  101.5 1.5 collective-permute-start.23
  103.0 4.2 %collective-permute-done.30.refs_1_ = bf16[24,8192]{1,0:T(8,128)(2,1)S(1)} collective-permute-done((bf16[24,8192]{1,0:T(8,128)(2,1)S(1)}, bf16[24,8192]{1,0:T(8,128)(2,1)S(1)}, u32[]{:S(2)}, u32[]{:S(2)}) %collective-permute-start.30) | collective-permute-done | bytes 393248 | tf_op jit(solution)/shard_map/ppermute | solution.py:47
  107.3 0.3 collective-permute-start.31
  107.6 0.7 collective-permute-done.33.refs_1_
  108.3 2.0 %collective-permute-start.34 = (bf16[24,8192]{1,0:T(8,128)(2,1)S(1)}, bf16[24,8192]{1,0:T(8,128)(2,1)S(1)}, u32[]{:S(2)}, u32[]{:S(2)}) collective-permute-start(bf16[24,8192]{1,0:T(8,128)(2,1)S(1)} %get-tuple-element.79), channel_id=1, source_target_pairs={{0,48},{8,56},{16,0},{24,8},{32,16},{40,24},{48,32},{56,40},{64,11... | collective-permute-start | bytes 1179656 | tf_op jit(solution)/shard_map/ppermute | solution.py:43
  110.2 0.3 add.51
  110.5 3.0 %collective-permute-start.29 = (bf16[24,8320]{1,0:T(8,128)(2,1)S(1)}, bf16[24,8320]{1,0:T(8,128)(2,1)S(1)}, u32[]{:S(2)}, u32[]{:S(2)}) collective-permute-start(bf16[24,8320]{1,0:T(8,128)(2,1)S(1)} %add.51), channel_id=1, source_target_pairs={{0,64},{8,72},{16,80},{24,88},{32,96},{40,104},{48,112},{56,120},{... | collective-permute-start | bytes 1198088 | tf_op jit(solution)/shard_map/ppermute | solution.py:47
  113.5 3.3 %collective-permute-done.26.refs_1_ = bf16[24,8320]{1,0:T(8,128)(2,1)S(1)} collective-permute-done((bf16[24,8320]{1,0:T(8,128)(2,1)S(1)}, bf16[24,8320]{1,0:T(8,128)(2,1)S(1)}, u32[]{:S(2)}, u32[]{:S(2)}) %collective-permute-start.26) | collective-permute-done | bytes 399392 | tf_op jit(solution)/shard_map/ppermute | solution.py:43
  116.8 0.2 add.50
  117.1 0.5 collective-permute-start.27
  117.7 2.2 %collective-permute-done.31.refs_1_ = bf16[24,8192]{1,0:T(8,128)(2,1)S(1)} collective-permute-done((bf16[24,8192]{1,0:T(8,128)(2,1)S(1)}, bf16[24,8192]{1,0:T(8,128)(2,1)S(1)}, u32[]{:S(2)}, u32[]{:S(2)}) %collective-permute-start.31) | collective-permute-done | bytes 393248 | tf_op jit(solution)/shard_map/ppermute | solution.py:39
  119.9 2.0 %collective-permute-start.35 = (bf16[24,8192]{1,0:T(8,128)(2,1)S(1)}, bf16[24,8192]{1,0:T(8,128)(2,1)S(1)}, u32[]{:S(2)}, u32[]{:S(2)}) collective-permute-start(bf16[24,8192]{1,0:T(8,128)(2,1)S(1)} %add.55), channel_id=1, source_target_pairs={{0,64},{8,72},{16,80},{24,88},{32,96},{40,104},{48,112},{56,120},{... | collective-permute-start | bytes 1179656 | tf_op jit(solution)/shard_map/ppermute | solution.py:47
  121.9 3.3 %collective-permute-done.34.refs_2_ = bf16[24,8192]{1,0:T(8,128)(2,1)S(1)} collective-permute-done((bf16[24,8192]{1,0:T(8,128)(2,1)S(1)}, bf16[24,8192]{1,0:T(8,128)(2,1)S(1)}, u32[]{:S(2)}, u32[]{:S(2)}) %collective-permute-start.34) | collective-permute-done | bytes 393248 | tf_op jit(solution)/shard_map/ppermute | solution.py:43
  125.2 1.2 fusion.2
  126.5 6.0 %collective-permute-done.35.refs_3_ = bf16[24,8192]{1,0:T(8,128)(2,1)S(1)} collective-permute-done((bf16[24,8192]{1,0:T(8,128)(2,1)S(1)}, bf16[24,8192]{1,0:T(8,128)(2,1)S(1)}, u32[]{:S(2)}, u32[]{:S(2)}) %collective-permute-start.35) | collective-permute-done | bytes 393248 | tf_op jit(solution)/shard_map/ppermute | solution.py:47
  132.4 3.6 %collective-permute-done.32.refs_1_ = bf16[24,8192]{1,0:T(8,128)(2,1)S(1)} collective-permute-done((bf16[24,8192]{1,0:T(8,128)(2,1)S(1)}, bf16[24,8192]{1,0:T(8,128)(2,1)S(1)}, u32[]{:S(2)}, u32[]{:S(2)}) %collective-permute-start.32) | collective-permute-done | bytes 393248 | tf_op jit(solution)/shard_map/ppermute | solution.py:39
  136.0 0.2 add.56
  136.2 0.4 add.52
  136.7 0.2 select_bitcast_fusion
  136.9 5.5 %collective-permute-start.36 = (bf16[12,16384]{1,0:T(8,128)(2,1)S(1)}, bf16[12,16384]{1,0:T(8,128)(2,1)S(1)}, u32[]{:S(2)}, u32[]{:S(2)}) collective-permute-start(bf16[12,16384]{1,0:T(8,128)(2,1)S(1)} %get-tuple-element.93), channel_id=1, source_target_pairs={{0,8},{8,0},{16,24},{24,16},{32,40},{40,32},{48,56},{56,48},{64,72... | collective-permute-start | bytes 1179656 | tf_op jit(solution)/shard_map/ppermute | solution.py:51
  142.5 1.2 convolution_bitcast_fusion
  143.7 1.7 %copy.15 = f32[1,12,16384]{2,0,1:T(1,128)} copy(f32[1,12,16384]{2,1,0:T(8,128)S(1)} %convolution_bitcast_fusion) | data formatting | bytes 1572864
  145.4 1.3 maximum_select_fusion
  (55 shorter events, 1.7 us)
Async XLA Ops:
  0.6 2.8 %copy-start.1 = (s32[256]{0:T(256)S(1)}, s32[256]{0:T(256)}, u32[]{:S(2)}) copy-start(s32[256]{0:T(256)} %param.7) | copy-start | bytes 3076
  1.9 3.0 %collective-permute-start = (bf16[12,16384]{1,0:T(8,128)(2,1)S(1)}, bf16[12,16384]{1,0:T(8,128)(2,1)S(1)}, u32[]{:S(2)}, u32[]{:S(2)}) collective-permute-start(bf16[12,16384]{1,0:T(8,128)(2,1)S(1)} %get-tuple-element.91), channel_id=1, source_target_pairs={{0,8},{8,0},{16,24},{24,16},{32,40},{40,32},{48,56},{56,48},{64,72... | collective-permute-start | bytes 1179656 | tf_op jit(solution)/shard_map/ppermute | solution.py:51
  5.2 23.6 %collective-permute-start.7 = (bf16[24,8192]{1,0:T(8,128)(2,1)S(1)}, bf16[24,8192]{1,0:T(8,128)(2,1)S(1)}, u32[]{:S(2)}, u32[]{:S(2)}) collective-permute-start(bf16[24,8192]{1,0:T(8,128)(2,1)S(1)} %maximum_select_fusion.2.refs_0_), channel_id=1, source_target_pairs={{0,16},{8,24},{16,32},{24,40},{32,48},{40,56},{48,0},{56,8},{64,80... | collective-permute-start | bytes 1179656 | tf_op jit(solution)/shard_map/ppermute | solution.py:39
  6.6 22.2 %collective-permute-start.9 = (bf16[24,8192]{1,0:T(8,128)(2,1)S(1)}, bf16[24,8192]{1,0:T(8,128)(2,1)S(1)}, u32[]{:S(2)}, u32[]{:S(2)}) collective-permute-start(bf16[24,8192]{1,0:T(8,128)(2,1)S(1)} %maximum_select_fusion.2.refs_0_), channel_id=1, source_target_pairs={{0,48},{8,56},{16,0},{24,8},{32,16},{40,24},{48,32},{56,40},{64,11... | collective-permute-start | bytes 1179656 | tf_op jit(solution)/shard_map/ppermute | solution.py:43
  8.0 2.7 %collective-permute-start.3 = (s32[256]{0:T(256)S(1)}, s32[256]{0:T(256)S(1)}, u32[]{:S(2)}, u32[]{:S(2)}) collective-permute-start(s32[256]{0:T(256)S(1)} %copy-done.1), channel_id=1, source_target_pairs={{0,8},{8,0},{16,24},{24,16},{32,40},{40,32},{48,56},{56,48},{64,72... | collective-permute-start | bytes 3080 | tf_op jit(solution)/shard_map/ppermute | solution.py:51
  9.1 19.7 %collective-permute-start.1 = (bf16[24,8192]{1,0:T(8,128)(2,1)S(1)}, bf16[24,8192]{1,0:T(8,128)(2,1)S(1)}, u32[]{:S(2)}, u32[]{:S(2)}) collective-permute-start(bf16[24,8192]{1,0:T(8,128)(2,1)S(1)} %maximum_select_fusion.1.refs_0_), channel_id=1, source_target_pairs={{0,48},{8,56},{16,0},{24,8},{32,16},{40,24},{48,32},{56,40},{64,11... | collective-permute-start | bytes 1179656 | tf_op jit(solution)/shard_map/ppermute | solution.py:43
  10.5 18.3 %collective-permute-start.2 = (bf16[24,8192]{1,0:T(8,128)(2,1)S(1)}, bf16[24,8192]{1,0:T(8,128)(2,1)S(1)}, u32[]{:S(2)}, u32[]{:S(2)}) collective-permute-start(bf16[24,8192]{1,0:T(8,128)(2,1)S(1)} %maximum_select_fusion.1.refs_0_), channel_id=1, source_target_pairs={{0,16},{8,24},{16,32},{24,40},{32,48},{40,56},{48,0},{56,8},{64,80... | collective-permute-start | bytes 1179656 | tf_op jit(solution)/shard_map/ppermute | solution.py:39
  10.6 18.2 %collective-permute-start.4 = (bf16[24,8192]{1,0:T(8,128)(2,1)S(1)}, bf16[24,8192]{1,0:T(8,128)(2,1)S(1)}, u32[]{:S(2)}, u32[]{:S(2)}) collective-permute-start(bf16[24,8192]{1,0:T(8,128)(2,1)S(1)} %maximum_select_fusion.2.refs_0_), channel_id=1, source_target_pairs={{0,64},{8,72},{16,80},{24,88},{32,96},{40,104},{48,112},{56,120},{... | collective-permute-start | bytes 1179656 | tf_op jit(solution)/shard_map/ppermute | solution.py:47
  28.8 15.2 %collective-permute-start.10 = (bf16[16,256,1024]{2,1,0:T(8,128)(2,1)}, bf16[16,256,1024]{2,1,0:T(8,128)(2,1)}, u32[]{:S(2)}, u32[]{:S(2)}) collective-permute-start(bf16[16,256,1024]{2,1,0:T(8,128)(2,1)} %get-tuple-element.49), channel_id=1, source_target_pairs={{0,8},{8,0},{16,24},{24,16},{32,40},{40,32},{48,56},{56,48},{64,72... | collective-permute-start | bytes 25165832 | tf_op jit(solution)/shard_map/ppermute | solution.py:51
  29.7 12.0 %collective-permute-start.8 = (bf16[24,8192]{1,0:T(8,128)(2,1)S(1)}, bf16[24,8192]{1,0:T(8,128)(2,1)}, u32[]{:S(2)}, u32[]{:S(2)}) collective-permute-start(bf16[24,8192]{1,0:T(8,128)(2,1)S(1)} %collective-permute-done.7.refs_2_), channel_id=1, source_target_pairs={{0,16},{8,24},{16,32},{24,40},{32,48},{40,56},{48,0},{56,8},{64,80... | collective-permute-start | bytes 1179656 | tf_op jit(solution)/shard_map/ppermute | solution.py:39
  29.8 12.4 %collective-permute-start.6 = (bf16[24,8192]{1,0:T(8,128)(2,1)S(1)}, bf16[24,8192]{1,0:T(8,128)(2,1)S(1)}, u32[]{:S(2)}, u32[]{:S(2)}) collective-permute-start(bf16[24,8192]{1,0:T(8,128)(2,1)S(1)} %collective-permute-done.1.refs_1_), channel_id=1, source_target_pairs={{0,48},{8,56},{16,0},{24,8},{32,16},{40,24},{48,32},{56,40},{64,11... | collective-permute-start | bytes 1179656 | tf_op jit(solution)/shard_map/ppermute | solution.py:43
  32.4 11.6 %collective-permute-start.5 = (bf16[24,8192]{1,0:T(8,128)(2,1)S(1)}, bf16[24,8192]{1,0:T(8,128)(2,1)S(1)}, u32[]{:S(2)}, u32[]{:S(2)}) collective-permute-start(bf16[24,8192]{1,0:T(8,128)(2,1)S(1)} %maximum_select_fusion.1.refs_0_), channel_id=1, source_target_pairs={{0,64},{8,72},{16,80},{24,88},{32,96},{40,104},{48,112},{56,120},{... | collective-permute-start | bytes 1179656 | tf_op jit(solution)/shard_map/ppermute | solution.py:47
  41.7 11.6 %collective-permute-start.13 = (bf16[24,8192]{1,0:T(8,128)(2,1)}, bf16[24,8192]{1,0:T(8,128)(2,1)}, u32[]{:S(2)}, u32[]{:S(2)}) collective-permute-start(bf16[24,8192]{1,0:T(8,128)(2,1)} %collective-permute-done.8.refs_4_), channel_id=1, source_target_pairs={{0,64},{8,72},{16,80},{24,88},{32,96},{40,104},{48,112},{56,120},{... | collective-permute-start | bytes 1179656 | tf_op jit(solution)/shard_map/ppermute | solution.py:47
  42.2 11.8 %collective-permute-start.15 = (bf16[24,8192]{1,0:T(8,128)(2,1)S(1)}, bf16[24,8192]{1,0:T(8,128)(2,1)S(1)}, u32[]{:S(2)}, u32[]{:S(2)}) collective-permute-start(bf16[24,8192]{1,0:T(8,128)(2,1)S(1)} %collective-permute-done.4.refs_3_), channel_id=1, source_target_pairs={{0,48},{8,56},{16,0},{24,8},{32,16},{40,24},{48,32},{56,40},{64,11... | collective-permute-start | bytes 1179656 | tf_op jit(solution)/shard_map/ppermute | solution.py:43
  44.0 10.5 %collective-permute-start.16 = (bf16[24,8192]{1,0:T(8,128)(2,1)S(1)}, bf16[24,8192]{1,0:T(8,128)(2,1)S(1)}, u32[]{:S(2)}, u32[]{:S(2)}) collective-permute-start(bf16[24,8192]{1,0:T(8,128)(2,1)S(1)} %collective-permute-done.4.refs_3_), channel_id=1, source_target_pairs={{0,16},{8,24},{16,32},{24,40},{32,48},{40,56},{48,0},{56,8},{64,80... | collective-permute-start | bytes 1179656 | tf_op jit(solution)/shard_map/ppermute | solution.py:39
  44.0 19.7 %collective-permute-start.11 = (bf16[24,8192]{1,0:T(8,128)(2,1)S(1)}, bf16[24,8192]{1,0:T(8,128)(2,1)S(1)}, u32[]{:S(2)}, u32[]{:S(2)}) collective-permute-start(bf16[24,8192]{1,0:T(8,128)(2,1)S(1)} %collective-permute-done.5.refs_3_), channel_id=1, source_target_pairs={{0,48},{8,56},{16,0},{24,8},{32,16},{40,24},{48,32},{56,40},{64,11... | collective-permute-start | bytes 1179656 | tf_op jit(solution)/shard_map/ppermute | solution.py:43
  46.7 17.0 %collective-permute-start.12 = (bf16[24,8192]{1,0:T(8,128)(2,1)S(1)}, bf16[24,8192]{1,0:T(8,128)(2,1)S(1)}, u32[]{:S(2)}, u32[]{:S(2)}) collective-permute-start(bf16[24,8192]{1,0:T(8,128)(2,1)S(1)} %collective-permute-done.5.refs_3_), channel_id=1, source_target_pairs={{0,16},{8,24},{16,32},{24,40},{32,48},{40,56},{48,0},{56,8},{64,80... | collective-permute-start | bytes 1179656 | tf_op jit(solution)/shard_map/ppermute | solution.py:39
  53.3 10.4 %collective-permute-start.14 = (bf16[24,8192]{1,0:T(8,128)(2,1)S(1)}, bf16[24,8192]{1,0:T(8,128)(2,1)S(1)}, u32[]{:S(2)}, u32[]{:S(2)}) collective-permute-start(bf16[24,8192]{1,0:T(8,128)(2,1)S(1)} %collective-permute-done.6.refs_4_), channel_id=1, source_target_pairs={{0,64},{8,72},{16,80},{24,88},{32,96},{40,104},{48,112},{56,120},{... | collective-permute-start | bytes 1179656 | tf_op jit(solution)/shard_map/ppermute | solution.py:47
  62.4 12.2 %copy-start.2 = (s32[512]{0:T(512)S(1)}, s32[512]{0:T(512)}, u32[]{:S(2)}) copy-start(s32[512]{0:T(512)} %param.11) | copy-start | bytes 6148
  71.5 4.4 %collective-permute-start.17 = (f32[192,512]{1,0:T(8,128)S(1)}, f32[192,512]{1,0:T(8,128)S(1)}, u32[]{:S(2)}, u32[]{:S(2)}) collective-permute-start(f32[192,512]{1,0:T(8,128)S(1)} %score.3.mine), channel_id=1, source_target_pairs={{0,8},{8,0},{16,24},{24,16},{32,40},{40,32},{48,56},{56,48},{64,72... | collective-permute-start | bytes 1179656 | tf_op jit(solution)/shard_map/ppermute | solution.py:51
  76.1 2.5 %collective-permute-start.18 = (f32[2,512]{1,0:T(2,128)S(1)}, f32[2,512]{1,0:T(2,128)S(1)}, u32[]{:S(2)}, u32[]{:S(2)}) collective-permute-start(f32[2,512]{1,0:T(2,128)S(1)} %get-tuple-element.56.refs_0_), channel_id=1, source_target_pairs={{0,4},{1,5},{2,6},{3,7},{4,0},{5,1},{6,2},{7,3},{8,12},{9,13},{10,... | collective-permute-start | bytes 12296 | tf_op jit(solution)/shard_map/ppermute | solution.py:409
  78.6 5.2 %collective-permute-start.19 = (f32[2,512]{1,0:T(2,128)S(1)}, f32[2,512]{1,0:T(2,128)S(1)}, u32[]{:S(2)}, u32[]{:S(2)}) collective-permute-start(f32[2,512]{1,0:T(2,128)S(1)} %merge.1.refs_3_), channel_id=1, source_target_pairs={{0,1},{1,2},{2,3},{3,0},{4,5},{5,6},{6,7},{7,4},{8,9},{9,10},{10,1... | collective-permute-start | bytes 12296 | tf_op jit(solution)/shard_map/ppermute | solution.py:411
  80.0 4.0 %collective-permute-start.20 = (f32[2,512]{1,0:T(2,128)S(1)}, f32[2,512]{1,0:T(2,128)S(1)}, u32[]{:S(2)}, u32[]{:S(2)}) collective-permute-start(f32[2,512]{1,0:T(2,128)S(1)} %merge.1.refs_3_), channel_id=1, source_target_pairs={{0,2},{1,3},{2,0},{3,1},{4,6},{5,7},{6,4},{7,5},{8,10},{9,11},{10,... | collective-permute-start | bytes 12296 | tf_op jit(solution)/shard_map/ppermute | solution.py:411
  82.6 2.5 %collective-permute-start.21 = (f32[2,512]{1,0:T(2,128)S(1)}, f32[2,512]{1,0:T(2,128)S(1)}, u32[]{:S(2)}, u32[]{:S(2)}) collective-permute-start(f32[2,512]{1,0:T(2,128)S(1)} %merge.1.refs_3_), channel_id=1, source_target_pairs={{0,3},{1,0},{2,1},{3,2},{4,7},{5,4},{6,5},{7,6},{8,11},{9,8},{10,9... | collective-permute-start | bytes 12296 | tf_op jit(solution)/shard_map/ppermute | solution.py:411
  89.9 11.3 %collective-permute-start.22 = (bf16[24,8320]{1,0:T(8,128)(2,1)S(1)}, bf16[24,8320]{1,0:T(8,128)(2,1)S(1)}, u32[]{:S(2)}, u32[]{:S(2)}) collective-permute-start(bf16[24,8320]{1,0:T(8,128)(2,1)S(1)} %get-tuple-element.63), channel_id=1, source_target_pairs={{0,64},{8,72},{16,80},{24,88},{32,96},{40,104},{48,112},{56,120},{... | collective-permute-start | bytes 1198088 | tf_op jit(solution)/shard_map/ppermute | solution.py:47
  91.9 9.5 %collective-permute-start.25 = (bf16[24,8320]{1,0:T(8,128)(2,1)S(1)}, bf16[24,8320]{1,0:T(8,128)(2,1)S(1)}, u32[]{:S(2)}, u32[]{:S(2)}) collective-permute-start(bf16[24,8320]{1,0:T(8,128)(2,1)S(1)} %get-tuple-element.68), channel_id=1, source_target_pairs={{0,48},{8,56},{16,0},{24,8},{32,16},{40,24},{48,32},{56,40},{64,11... | collective-permute-start | bytes 1198088 | tf_op jit(solution)/shard_map/ppermute | solution.py:43
  92.0 15.3 %collective-permute-start.28 = (bf16[24,8320]{1,0:T(8,128)(2,1)S(1)}, bf16[24,8320]{1,0:T(8,128)(2,1)S(1)}, u32[]{:S(2)}, u32[]{:S(2)}) collective-permute-start(bf16[24,8320]{1,0:T(8,128)(2,1)S(1)} %get-tuple-element.71), channel_id=1, source_target_pairs={{0,16},{8,24},{16,32},{24,40},{32,48},{40,56},{48,0},{56,8},{64,80... | collective-permute-start | bytes 1198088 | tf_op jit(solution)/shard_map/ppermute | solution.py:39
  97.9 9.2 %collective-permute-start.30 = (bf16[24,8192]{1,0:T(8,128)(2,1)S(1)}, bf16[24,8192]{1,0:T(8,128)(2,1)S(1)}, u32[]{:S(2)}, u32[]{:S(2)}) collective-permute-start(bf16[24,8192]{1,0:T(8,128)(2,1)S(1)} %get-tuple-element.75), channel_id=1, source_target_pairs={{0,64},{8,72},{16,80},{24,88},{32,96},{40,104},{48,112},{56,120},{... | collective-permute-start | bytes 1179656 | tf_op jit(solution)/shard_map/ppermute | solution.py:47
  99.0 9.3 %collective-permute-start.33 = (bf16[24,8192]{1,0:T(8,128)(2,1)S(1)}, bf16[24,8192]{1,0:T(8,128)(2,1)S(1)}, u32[]{:S(2)}, u32[]{:S(2)}) collective-permute-start(bf16[24,8192]{1,0:T(8,128)(2,1)S(1)} %get-tuple-element.78), channel_id=1, source_target_pairs={{0,48},{8,56},{16,0},{24,8},{32,16},{40,24},{48,32},{56,40},{64,11... | collective-permute-start | bytes 1179656 | tf_op jit(solution)/shard_map/ppermute | solution.py:43
  101.4 15.4 %collective-permute-start.26 = (bf16[24,8320]{1,0:T(8,128)(2,1)S(1)}, bf16[24,8320]{1,0:T(8,128)(2,1)S(1)}, u32[]{:S(2)}, u32[]{:S(2)}) collective-permute-start(bf16[24,8320]{1,0:T(8,128)(2,1)S(1)} %add.49), channel_id=1, source_target_pairs={{0,48},{8,56},{16,0},{24,8},{32,16},{40,24},{48,32},{56,40},{64,11... | collective-permute-start | bytes 1198088 | tf_op jit(solution)/shard_map/ppermute | solution.py:43
  101.5 12.0 %collective-permute-start.23 = (bf16[24,8192]{1,0:T(8,128)(2,1)S(1)}, bf16[24,8192]{1,0:T(8,128)(2,1)S(1)}, u32[]{:S(2)}, u32[]{:S(2)}) collective-permute-start(bf16[24,8192]{1,0:T(8,128)(2,1)S(1)} %get-tuple-element.64), channel_id=1, source_target_pairs={{0,16},{8,24},{16,32},{24,40},{32,48},{40,56},{48,0},{56,8},{64,80... | collective-permute-start | bytes 1179656 | tf_op jit(solution)/shard_map/ppermute | solution.py:39
  107.3 12.6 %collective-permute-start.31 = (bf16[24,8192]{1,0:T(8,128)(2,1)S(1)}, bf16[24,8192]{1,0:T(8,128)(2,1)S(1)}, u32[]{:S(2)}, u32[]{:S(2)}) collective-permute-start(bf16[24,8192]{1,0:T(8,128)(2,1)S(1)} %add.53), channel_id=1, source_target_pairs={{0,16},{8,24},{16,32},{24,40},{32,48},{40,56},{48,0},{56,8},{64,80... | collective-permute-start | bytes 1179656 | tf_op jit(solution)/shard_map/ppermute | solution.py:39
  108.3 17.0 %collective-permute-start.34 = (bf16[24,8192]{1,0:T(8,128)(2,1)S(1)}, bf16[24,8192]{1,0:T(8,128)(2,1)S(1)}, u32[]{:S(2)}, u32[]{:S(2)}) collective-permute-start(bf16[24,8192]{1,0:T(8,128)(2,1)S(1)} %get-tuple-element.79), channel_id=1, source_target_pairs={{0,48},{8,56},{16,0},{24,8},{32,16},{40,24},{48,32},{56,40},{64,11... | collective-permute-start | bytes 1179656 | tf_op jit(solution)/shard_map/ppermute | solution.py:43
  110.5 25.6 %collective-permute-start.29 = (bf16[24,8320]{1,0:T(8,128)(2,1)S(1)}, bf16[24,8320]{1,0:T(8,128)(2,1)S(1)}, u32[]{:S(2)}, u32[]{:S(2)}) collective-permute-start(bf16[24,8320]{1,0:T(8,128)(2,1)S(1)} %add.51), channel_id=1, source_target_pairs={{0,64},{8,72},{16,80},{24,88},{32,96},{40,104},{48,112},{56,120},{... | collective-permute-start | bytes 1198088 | tf_op jit(solution)/shard_map/ppermute | solution.py:47
  113.5 22.7 %collective-permute-start.24 = (bf16[24,8320]{1,0:T(8,128)(2,1)S(1)}, bf16[24,8320]{1,0:T(8,128)(2,1)S(1)}, u32[]{:S(2)}, u32[]{:S(2)}) collective-permute-start(bf16[24,8320]{1,0:T(8,128)(2,1)S(1)} %get-tuple-element.65), channel_id=1, source_target_pairs={{0,16},{8,24},{16,32},{24,40},{32,48},{40,56},{48,0},{56,8},{64,80... | collective-permute-start | bytes 1198088 | tf_op jit(solution)/shard_map/ppermute | solution.py:39
  117.1 19.2 %collective-permute-start.27 = (bf16[24,8320]{1,0:T(8,128)(2,1)S(1)}, bf16[24,8320]{1,0:T(8,128)(2,1)S(1)}, u32[]{:S(2)}, u32[]{:S(2)}) collective-permute-start(bf16[24,8320]{1,0:T(8,128)(2,1)S(1)} %add.50), channel_id=1, source_target_pairs={{0,48},{8,56},{16,0},{24,8},{32,16},{40,24},{48,32},{56,40},{64,11... | collective-permute-start | bytes 1198088 | tf_op jit(solution)/shard_map/ppermute | solution.py:43
  119.9 12.6 %collective-permute-start.35 = (bf16[24,8192]{1,0:T(8,128)(2,1)S(1)}, bf16[24,8192]{1,0:T(8,128)(2,1)S(1)}, u32[]{:S(2)}, u32[]{:S(2)}) collective-permute-start(bf16[24,8192]{1,0:T(8,128)(2,1)S(1)} %add.55), channel_id=1, source_target_pairs={{0,64},{8,72},{16,80},{24,88},{32,96},{40,104},{48,112},{56,120},{... | collective-permute-start | bytes 1179656 | tf_op jit(solution)/shard_map/ppermute | solution.py:47
  125.2 10.8 %collective-permute-start.32 = (bf16[24,8192]{1,0:T(8,128)(2,1)S(1)}, bf16[24,8192]{1,0:T(8,128)(2,1)S(1)}, u32[]{:S(2)}, u32[]{:S(2)}) collective-permute-start(bf16[24,8192]{1,0:T(8,128)(2,1)S(1)} %add.54), channel_id=1, source_target_pairs={{0,16},{8,24},{16,32},{24,40},{32,48},{40,56},{48,0},{56,8},{64,80... | collective-permute-start | bytes 1179656 | tf_op jit(solution)/shard_map/ppermute | solution.py:39
  136.2 6.3 %copy-start = (f32[32,16384]{1,0:T(8,128)S(1)}, f32[32,16384]{1,0:T(8,128)}, u32[]{:S(2)}) copy-start(f32[32,16384]{1,0:T(8,128)} %contrast.1) | copy-start | bytes 6291460
  136.9 8.4 %collective-permute-start.36 = (bf16[12,16384]{1,0:T(8,128)(2,1)S(1)}, bf16[12,16384]{1,0:T(8,128)(2,1)S(1)}, u32[]{:S(2)}, u32[]{:S(2)}) collective-permute-start(bf16[12,16384]{1,0:T(8,128)(2,1)S(1)} %get-tuple-element.93), channel_id=1, source_target_pairs={{0,8},{8,0},{16,24},{24,16},{32,40},{40,32},{48,56},{56,48},{64,72... | collective-permute-start | bytes 1179656 | tf_op jit(solution)/shard_map/ppermute | solution.py:51
